TPU v7x, 128 devices: a whole 4x4x4 slice. The times are simulated.
128 devices in a mesh: rep: 16 (over z, x_hi, core), tp: 8 (over x_lo, y).
Axes of the slice: x: 4 (x_hi: 2, x_lo: 2; x = x_hi * 2 + x_lo), y: 4, z: 4, core: 2. Of those that a mesh axis runs over, the one named last changes fastest.
Arguments:
- kv_master: float32 [16384, 2048], P(('rep', 'tp')), may hold values from -0.046875 to 0.046875
- hidden: bfloat16 [2, 64, 16384], P(None, 'rep', 'tp'), may hold values from -6 to 6
- queries: bfloat16 [2, 64, 16384], P(None, 'rep', 'tp'), may hold values from -34 to 34
- key_cache: bfloat16 [64, 8192, 1024], P('rep', None, 'tp'), may hold values from -6 to 6
- value_cache: bfloat16 [64, 8192, 1024], P('rep', None, 'tp'), may hold values from -6 to 6
- lengths: int32 [64], P('rep'), may hold values from 1 to 8192, as said below
Outputs:
- rollout_weight: bfloat16 [16384, 2048], P(None, 'tp')
- new_kv: bfloat16 [2, 64, 2048], P(None, 'rep', 'tp')
- attended: bfloat16 [2, 64, 16384], P(None, 'rep', 'tp')
Inputs may be any that keep to these rules, and one draw needn't show every extreme that they name: `lengths`: some row holds exactly 8192 cached positions and some exactly 1.
All inputs are finite; a program needn't handle non-finite values.
Results may differ from a plain program's by a relative error of at most 0.0056.
Values may be sent and summed in bfloat16 or wider, within the bound.
No kernel may reach another device: no remote copies, remote signals or barrier semaphores. Data moves between devices by JAX's collectives and lax.ppermute only.
A program may use at most 128 MiB of HBM per device.

v0:
```python
import math

import jax
import jax.numpy as jnp
from jax import lax
from jax.sharding import PartitionSpec as P

KVH = 8
HD = 128
QH = 128


rope_base = 500000.0


def scaled_frequencies(width):
    pair_index = jnp.arange(width // 2, dtype=jnp.float32)
    base_freq = rope_base ** (-2.0 * pair_index / width)
    wavelength = 2.0 * math.pi / base_freq
    smooth = (8192.0 / wavelength - 1.0) / 3.0
    blended = (1.0 - smooth) * base_freq / 8.0 + smooth * base_freq
    return jnp.where(
        wavelength < 2048.0, base_freq, jnp.where(wavelength > 8192.0, base_freq / 8.0, blended)
    )


def rotate_keys(key_part, positions):
    half_width = key_part.shape[-1] // 2
    inverse = scaled_frequencies(key_part.shape[-1])
    angles = positions.astype(jnp.float32)[..., None] * inverse
    cosine = jnp.cos(angles)
    sine_part = jnp.sin(angles)
    front_half = key_part[..., :half_width]
    back_half = key_part[..., half_width:]
    return jnp.concatenate(
        [front_half * cosine - back_half * sine_part, back_half * cosine + front_half * sine_part],
        axis=-1,
    )


def attend(queries, key_cache, value_cache, lengths, new_kv, local_heads):
    step_count, row_count, _ = queries.shape
    groups = QH // KVH
    cache_span = key_cache.shape[1]
    score_scale = HD ** (-0.5)
    query_heads = queries.reshape(step_count, row_count, local_heads, groups, HD)
    cache_keys = key_cache.reshape(row_count, cache_span, local_heads, HD)
    cache_values = value_cache.reshape(row_count, cache_span, local_heads, HD)
    fresh_pairs = new_kv.reshape(step_count, row_count, local_heads, 2, HD)
    cache_scores = (
        jnp.einsum("srgqd,rpgd->srgqp", query_heads, cache_keys, preferred_element_type=jnp.float32)
        * score_scale
    )
    visible = jnp.arange(cache_span, dtype=jnp.int32)[None, :] < lengths[:, None]
    cache_scores = jnp.where(visible[None, :, None, None, :], cache_scores, -jnp.inf)
    new_scores = (
        jnp.einsum(
            "srgqd,jrgd->srgqj",
            query_heads,
            fresh_pairs[:, :, :, 0, :],
            preferred_element_type=jnp.float32,
        )
        * score_scale
    )
    causal = jnp.arange(step_count)[:, None] >= jnp.arange(step_count)[None, :]
    new_scores = jnp.where(causal[:, None, None, None, :], new_scores, -jnp.inf)
    row_max = jnp.maximum(jnp.max(cache_scores, axis=-1), jnp.max(new_scores, axis=-1))[..., None]
    cache_exp = jnp.exp(cache_scores - row_max)
    new_exp = jnp.exp(new_scores - row_max)
    denominator = jnp.sum(cache_exp, axis=-1, keepdims=True) + jnp.sum(
        new_exp, axis=-1, keepdims=True
    )
    cache_probs = (cache_exp / denominator).astype(jnp.bfloat16)
    new_probs = (new_exp / denominator).astype(jnp.bfloat16)
    mixed = jnp.einsum(
        "srgqp,rpgd->srgqd", cache_probs, cache_values, preferred_element_type=jnp.float32
    )
    mixed = mixed + jnp.einsum(
        "srgqj,jrgd->srgqd",
        new_probs,
        fresh_pairs[:, :, :, 1, :],
        preferred_element_type=jnp.float32,
    )
    return mixed.astype(jnp.bfloat16).reshape(step_count, row_count, local_heads * groups * HD)


def local(kv_master, hidden, queries, key_cache, value_cache, lengths):
    weight = kv_master.astype(jnp.bfloat16)
    block_rows, columns = weight.shape
    replicas = lax.axis_size("rep")
    rank_count = lax.axis_size("tp")
    step_count, row_count, features = hidden.shape
    local_heads = KVH // rank_count
    local_columns = columns // rank_count
    gathered = lax.all_gather(weight, "rep", axis=0, tiled=True)
    grouped = gathered.reshape(rank_count, replicas // rank_count, block_rows, columns).transpose(
        1, 0, 2, 3
    )
    arrived = lax.all_to_all(grouped, "tp", split_axis=1, concat_axis=1, tiled=True)
    owned_rows = arrived.reshape(replicas * block_rows, columns)
    split_owned = owned_rows.reshape(replicas * block_rows, rank_count, local_columns)
    served = lax.all_to_all(split_owned, "tp", split_axis=1, concat_axis=0, tiled=True)
    rollout_weight = served.reshape(replicas * rank_count * block_rows, local_columns)
    partial_value = jnp.dot(
        hidden.reshape(step_count * row_count, features),
        owned_rows,
        preferred_element_type=jnp.float32,
    )
    summed = lax.psum(partial_value, "tp")
    projected = lax.dynamic_slice_in_dim(
        summed, lax.axis_index("tp") * local_columns, local_columns, 1
    )
    paired = projected.reshape(step_count, row_count, local_heads, 2, HD)
    positions = lengths[None, :] + jnp.arange(step_count, dtype=jnp.int32)[:, None]
    rotated = rotate_keys(paired[:, :, :, 0, :], positions[:, :, None])
    new_kv = (
        jnp.stack([rotated, paired[:, :, :, 1, :]], axis=3)
        .astype(jnp.bfloat16)
        .reshape(step_count, row_count, local_heads * 2 * HD)
    )
    attended = attend(queries, key_cache, value_cache, lengths, new_kv, local_heads)
    return (rollout_weight, new_kv, attended)


def solution(mesh):
    return jax.shard_map(
        local,
        mesh=mesh,
        in_specs=(
            P(("rep", "tp"), None),
            P(None, "rep", "tp"),
            P(None, "rep", "tp"),
            P("rep", None, "tp"),
            P("rep", None, "tp"),
            P("rep"),
        ),
        out_specs=(P(None, "tp"), P(None, "rep", "tp"), P(None, "rep", "tp")),
        check_vma=False,
    )
```

profile of v0, /device:TPU:1, one launch (start us, length us, event | category | flops | bytes accessed | tf_op | source)
XLA Modules:
  0.0 367.1 jit_solution(1514606267000072169)
XLA Ops:
  7.2 0.0 all-gather.2.cloned.1.call-start
  7.2 2.1 convert_element_type.42
  9.3 0.0 all-gather.2.cloned.1.call-update
  9.3 78.5 %all-gather.2.cloned.1.call-done = bf16[2048,2048]{1,0:T(8,128)(2,1)} async-done(((bf16[128,2048]{1,0:T(8,128)(2,1)}), bf16[2048,2048]{1,0:T(8,128)(2,1)}) %all-gather.2.cloned.1.call-update) | async-done | bytes 8388624 | tf_op jit(solution)/shard_map/all_gather | solution.py:95
  87.8 99.0 %all_to_all.20 = bf16[2,8,128,2048]{3,2,0,1:T(8,128)(2,1)} all-to-all(bf16[2,8,128,2048]{3,2,0,1:T(8,128)(2,1)} %bitcast.88), channel_id=1, replica_groups=mesh['rep'=16,'tp'=8] {'tp'}, dimensions={1} | all-to-all | bytes 16777216 | tf_op jit(solution)/shard_map/all_to_all | solution.py:99
  186.9 8.4 %copy.27 = bf16[2,8,128,2048]{3,2,1,0:T(8,128)(2,1)} copy(bf16[2,8,128,2048]{3,2,0,1:T(8,128)(2,1)} %all_to_all.20) | data formatting | bytes 16777216 | tf_op jit(solution)/shard_map/all_to_all | solution.py:99
  195.3 10.3 %copy.42 = bf16[256,8,8,256]{3,2,1,0:T(8,128)(2,1)} copy(bf16[256,8,8,256]{3,1,2,0:T(8,128)(2,1)} %bitcast.85) | data formatting | bytes 16777216
  205.6 8.3 %copy.28 = bf16[2048,8,256]{2,0,1:T(8,128)(2,1)} copy(bf16[2048,8,256]{2,1,0:T(8,128)(2,1)} %bitcast.87) | data formatting | bytes 16777216 | tf_op jit(solution)/shard_map/reshape;reshape | solution.py:101
  213.9 0.0 copy-start.1
  213.9 0.0 copy-start.2
  213.9 0.0 copy-start.3
  213.9 5.2 %all-to-all-start.1 = ((bf16[2048,8,256]{2,0,1:T(8,128)(2,1)}), bf16[2048,8,256]{2,0,1:T(8,128)(2,1)}, u32[]{:S(2)}, u32[]{:S(2)}) async-start(bf16[2048,8,256]{2,0,1:T(8,128)(2,1)} %copy.28), calls=%async_computation.1 | async-start | bytes 16777216 | tf_op jit(solution)/shard_map/all_to_all | solution.py:102
  219.1 0.2 all-reduce.2.cloned.1.call-start
  219.3 0.0 copy-done.1
  219.3 0.0 copy-done.2
  219.4 0.0 copy-done.3
  219.4 0.1 add_convert_fusion
  219.5 0.1 iota_compare_fusion
  219.6 8.3 %fusion.29 = (f32[2,4,16]{2,0,1:T(2,128)S(1)}, f32[2,4,1,16,8192]{4,3,0,1,2:T(8,128)}) fusion(bf16[2,4,16,128]{3,2,1,0:T(8,128)(2,1)S(1)} %reshape.230, bf16[4,8192,128]{2,1,0:T(8,128)(2,1)} %param.9, pred[4,8192]{1,0:T(4,128)(4,1)S(1)} %iota_compare_fusion), kind=kOutput, calls=%fused_computation.46 | convolution fusion | flops 271581056 | bytes 12648960 | tf_op jit(solution)/shard_map/srgqd,rpgd->srgqp/dot_general | solution.py:51
  227.9 5.2 %fusion.31 = f32[8,2048]{1,0:T(8,128)} fusion(bf16[8,2048]{1,0:T(8,128)(2,1)S(1)} %reshape.227, bf16[2048,2048]{1,0:T(8,128)(2,1)} %bitcast.86), kind=kOutput, calls=%fused_computation.48 | convolution fusion | flops 67108864 | bytes 8486912 | tf_op jit(solution)/shard_map/dot_general | solution.py:104
  233.1 0.0 all-reduce.2.cloned.1.call-update
  233.1 109.2 %all-reduce.2.cloned.1.call-done = f32[8,2048]{1,0:T(8,128)} async-done(((f32[8,2048]{1,0:T(8,128)}), f32[8,2048]{1,0:T(8,128)}) %all-reduce.2.cloned.1.call-update) | async-done | bytes 65552 | tf_op jit(solution)/shard_map/psum | solution.py:109
  342.3 0.7 constant_dynamic-slice_fusion
  343.0 0.0 copy-start
  343.1 0.1 fusion.25
  343.2 0.1 maximum_bitcast_fusion
  343.3 0.6 copy.54
  343.9 0.2 fusion.30
  344.2 3.0 fusion.6
  347.2 0.0 copy-done
  347.2 5.0 %fusion.9 = f32[4,128,2,16]{1,3,2,0:T(8,128)S(1)} fusion(bf16[4,8192,128]{2,1,0:T(8,128)(2,1)} %param.10, f32[2,4,16]{2,0,1:T(2,128)S(1)} %add.57, f32[2,4,1,16,8192]{4,3,0,1,2:T(8,128)S(1)} %copy-done, f32[2,4,16]{2,0,1:T(2,128)S(1)} %max.9), kind=kOutput, calls=%fused_computation.12 | convolution fusion | flops 271581184 | bytes 12649472 | tf_op jit(solution)/shard_map/srgqp,rpgd->srgqd/dot_general | solution.py:75
  352.3 0.2 fusion.15
  352.5 0.6 copy.35
  353.1 0.0 all-to-all-done.1
  353.1 7.1 %copy.57 = bf16[16384,256]{1,0:T(8,128)(2,1)} copy(bf16[16384,256]{1,0:T(8,128)(2,1)} %bitcast.4) | data formatting | bytes 16777216
  (14 shorter events, 0.2 us)
Async XLA Ops:
  7.2 80.7 %all-gather.2.cloned.1.call-start = ((), (), s32[]{:S(2)}) async-start(), calls=%async_computation.2 | async-start | bytes 8912896 | tf_op jit(solution)/shard_map/all_gather | solution.py:95
  213.9 5.4 %copy-start.1 = (bf16[2,4,2048]{2,1,0:T(4,128)(2,1)S(1)}, bf16[2,4,2048]{2,1,0:T(4,128)(2,1)}, u32[]{:S(2)}) copy-start(bf16[2,4,2048]{2,1,0:T(4,128)(2,1)} %param.7) | copy-start | bytes 98308
  213.9 5.4 %copy-start.2 = (bf16[2,4,2048]{2,1,0:T(4,128)(2,1)S(1)}, bf16[2,4,2048]{2,1,0:T(4,128)(2,1)}, u32[]{:S(2)}) copy-start(bf16[2,4,2048]{2,1,0:T(4,128)(2,1)} %param.8) | copy-start | bytes 98308
  213.9 5.5 %copy-start.3 = (s32[4]{0:T(128)S(1)}, s32[4]{0:T(128)}, u32[]{:S(2)}) copy-start(s32[4]{0:T(128)} %param.11) | copy-start | bytes 52
  213.9 139.2 %all-to-all-start.1 = ((bf16[2048,8,256]{2,0,1:T(8,128)(2,1)}), bf16[2048,8,256]{2,0,1:T(8,128)(2,1)}, u32[]{:S(2)}, u32[]{:S(2)}) async-start(bf16[2048,8,256]{2,0,1:T(8,128)(2,1)} %copy.28), calls=%async_computation.1 | async-start | bytes 16777216 | tf_op jit(solution)/shard_map/all_to_all | solution.py:102
  219.1 123.2 %all-reduce.2.cloned.1.call-start = ((), (), s32[]{:S(2)}) async-start(), calls=%async_computation.3 | async-start | bytes 131072 | tf_op jit(solution)/shard_map/psum | solution.py:109
  343.0 4.2 %copy-start = (f32[2,4,1,16,8192]{4,3,0,1,2:T(8,128)S(1)}, f32[2,4,1,16,8192]{4,3,0,1,2:T(8,128)}, u32[]{:S(2)}) copy-start(f32[2,4,1,16,8192]{4,3,0,1,2:T(8,128)} %get-tuple-element.18) | copy-start | bytes 12582916
Sparse Core Ops, SparseCore 0:
  11.0 76.7 all-gather.1
  233.3 109.0 all-reduce.1
where the time goes:
time: 372 us; the launch traced here: 367 us
  waiting for transfers between devices  188 us (51%)
  blocking collectives  99 us (27%)
  local copies, waits for them, and re-layouts  36.2 us (10%)
  matrix products  18.9 us (5%)
  between operations  14.2 us (4%)
  other arithmetic  5.6 us (2%)
  starting transfers between devices  5.43 us (1%)
    psum x1, waiting for transfers between devices, local(): summed = lax.psum(partial_value, 'tp')  109 us
    all_to_all x1, blocking collectives, local(): lax.all_to_all(grouped, 'tp', split_axis=1, concat_axis=1, tiled=True)  99 us
    all_gather x1, waiting for transfers between devices, local(): gathered = lax.all_gather(weight, 'rep', axis=0, tiled=True)  78.5 us
    unnamed x13, local copies, waits for them, and re-layouts  18 us
    all_to_all x1, local copies, waits for them, and re-layouts, local(): lax.all_to_all(grouped, 'tp', split_axis=1, concat_axis=1, tiled=True)  8.44 us
    another operation x1, local copies, waits for them, and re-layouts, local(): owned_rows.reshape(replicas * block_rows, rank_count, local_columns)  8.34 us
    dot_general x1, matrix products, attend(): jnp.einsum('srgqd,rpgd->srgqp', query_heads, cache_keys, preferred_elemen...  8.31 us
  transfers between devices with their start and end apart: 3, of which 2 were waited for; matrix products, arithmetic and copies ran while one was open for 7% of the time, Pallas kernels for 0%

commit v1 on v0

v1 whole, which is shorter than its diff:
```python
import math

import jax
import jax.numpy as jnp
from jax import lax
from jax.experimental import pallas as pl
from jax.experimental.pallas import tpu as pltpu
from jax.sharding import PartitionSpec as P

KVH = 8
HD = 128
QH = 128
GROUPS = QH // KVH
SCALE = HD ** (-0.5)

REP = 16
TP = 8
ROWS = 128
OWNED = TP * ROWS
HALF = OWNED // 2
COLS = 2 * HD
VMEM_BYTES = 60 * 2**20
CACHE_VMEM = 60 * 2**20
PLACE_VMEM = 60 * 2**20
PLACE_COST = pl.CostEstimate(flops=1000, bytes_accessed=1000, transcendentals=0)

rope_base = 500000.0

ANY = pl.BlockSpec(memory_space=pl.ANY)
SMEM = pl.BlockSpec(memory_space=pltpu.SMEM)
VMEM = pl.BlockSpec(memory_space=pltpu.VMEM)


def z_shift(step):
    return [(r, ((((r >> 2) + step) % 4) << 2) | (r & 3)) for r in range(REP)]


X_SWAP = [(r, r ^ 2) for r in range(REP)]
CORE_SWAP = [(r, r ^ 1) for r in range(REP)]


def send(value, pairs):
    return lax.ppermute(value, "rep", pairs)


def scaled_frequencies(width):
    pair_index = jnp.arange(width // 2, dtype=jnp.float32)
    base_freq = rope_base ** (-2.0 * pair_index / width)
    wavelength = 2.0 * math.pi / base_freq
    smooth = (8192.0 / wavelength - 1.0) / 3.0
    blended = (1.0 - smooth) * base_freq / 8.0 + smooth * base_freq
    return jnp.where(
        wavelength < 2048.0, base_freq, jnp.where(wavelength > 8192.0, base_freq / 8.0, blended)
    )


def rotation_tables(lengths, steps):
    positions = lengths[None, :] + jnp.arange(steps, dtype=jnp.int32)[:, None]
    angles = positions.reshape(-1, 1).astype(jnp.float32) * scaled_frequencies(HD)
    cosine, sine = jnp.cos(angles), jnp.sin(angles)
    return (
        jnp.concatenate([cosine, cosine], axis=-1),
        jnp.concatenate([-sine, sine], axis=-1),
    )


def pack_kernel(kv_ref, hid_ref, out_ref):
    steps, _, width = hid_ref.shape
    flat = jnp.concatenate([hid_ref[s].astype(jnp.float32) for s in range(steps)], axis=0)
    cut = [flat[:, c : c + COLS] for c in range(0, width, COLS)]
    cut = jnp.concatenate(cut, axis=0).astype(jnp.bfloat16)
    for t in range(TP):
        out_ref[t, :ROWS] = kv_ref[:, t * COLS : (t + 1) * COLS].astype(jnp.bfloat16)
        out_ref[t, ROWS:] = cut


def pack(kv_master, hidden):
    return pl.pallas_call(
        pack_kernel,
        in_specs=[VMEM, VMEM],
        out_specs=VMEM,
        out_shape=jax.ShapeDtypeStruct((TP, ROWS + hidden.size // COLS, COLS), jnp.bfloat16),
        compiler_params=pltpu.CompilerParams(vmem_limit_bytes=VMEM_BYTES),
    )(kv_master, hidden)


def cache_kernel(first, count, len_ref, q_ref, k_ref, v_ref, q_out, acc_out, m_out, l_out, q_scr, s_scr):
    i = pl.program_id(0)
    steps, rows = q_ref.shape[0], q_ref.shape[1]
    span = k_ref.shape[1]
    chunk = 2048

    @pl.when(i == 0)
    def _():
        flat = jnp.concatenate([q_ref[s].astype(jnp.float32) for s in range(steps)], axis=0)
        for g in range(GROUPS):
            q_scr[pl.ds(g, steps * rows, stride=GROUPS), :] = flat[:, g * HD : (g + 1) * HD]
        q_out[...] = q_scr[...].reshape(q_out.shape).astype(q_out.dtype)

    b = first + i
    base = [pl.multiple_of((s * rows + b) * GROUPS, GROUPS) for s in range(steps)]
    q = jnp.concatenate([q_scr[pl.ds(o, GROUPS), :] for o in base], axis=0).astype(jnp.bfloat16)
    length = len_ref[b]
    top = jnp.full((steps * GROUPS, 1), -jnp.inf, jnp.float32)
    for c in range(span // chunk):
        keys = k_ref[0, c * chunk : (c + 1) * chunk, :]
        scores = (
            lax.dot_general(q, keys, (((1,), (1,)), ((), ())), preferred_element_type=jnp.float32)
            * SCALE
        )
        place = c * chunk + lax.broadcasted_iota(jnp.int32, scores.shape, 1)
        scores = jnp.where(place < length, scores, -jnp.inf)
        s_scr[:, c * chunk : (c + 1) * chunk] = scores
        top = jnp.maximum(top, jnp.max(scores, axis=-1, keepdims=True))
    total = jnp.zeros((steps * GROUPS, 1), jnp.float32)
    acc = jnp.zeros((steps * GROUPS, HD), jnp.float32)
    for c in range(span // chunk):
        weights = jnp.exp(s_scr[:, c * chunk : (c + 1) * chunk] - top)
        total = total + jnp.sum(weights, axis=-1, keepdims=True)
        acc = acc + jnp.dot(
            weights.astype(jnp.bfloat16),
            v_ref[0, c * chunk : (c + 1) * chunk, :],
            preferred_element_type=jnp.float32,
        )
    for s in range(steps):
        part = slice(s * GROUPS, (s + 1) * GROUPS)
        place = s * count + i
        acc_out[place] = acc[part]
        m_out[place] = jnp.broadcast_to(top[part], (GROUPS, HD))
        l_out[place] = jnp.broadcast_to(total[part], (GROUPS, HD))


def attend_cache(queries, key_cache, value_cache, lengths, first, count):
    steps, rows, width = queries.shape
    span = key_cache.shape[1]
    part = jax.ShapeDtypeStruct((steps * count, GROUPS, HD), jnp.float32)
    return pl.pallas_call(
        lambda *refs: cache_kernel(first, count, *refs),
        grid=(count,),
        in_specs=[
            SMEM,
            pl.BlockSpec((steps, rows, width), lambda i: (0, 0, 0)),
            pl.BlockSpec((1, span, HD), lambda i: (first + i, 0, 0)),
            pl.BlockSpec((1, span, HD), lambda i: (first + i, 0, 0)),
        ],
        out_specs=[pl.BlockSpec((steps * rows, GROUPS, HD), lambda i: (0, 0, 0))]
        + [pl.BlockSpec(part.shape, lambda i: (0, 0, 0))] * 3,
        out_shape=[jax.ShapeDtypeStruct((steps * rows, GROUPS, HD), jnp.bfloat16)] + [part] * 3,
        scratch_shapes=[
            pltpu.VMEM((steps * rows * GROUPS, HD), jnp.float32),
            pltpu.VMEM((steps * GROUPS, span), jnp.float32),
        ],
        compiler_params=pltpu.CompilerParams(vmem_limit_bytes=CACHE_VMEM),
        cost_estimate=pl.CostEstimate(
            flops=4 * count * steps * GROUPS * span * HD,
            bytes_accessed=4 * count * span * HD,
            transcendentals=count * steps * GROUPS * span,
        ),
    )(lengths, queries, key_cache, value_cache)


def place_pieces(spots, where_ref, hid_ref, piece_refs, out_ref, buf, in_sem, out_sem):
    rep = where_ref[0]
    copies, offset = [], 0
    for i, (_, _, _, _, count) in enumerate(spots):
        copy = pltpu.make_async_copy(piece_refs[i], buf.at[pl.ds(offset, count)], in_sem.at[i])
        copy.start()
        copies.append((copy, offset))
        offset += count
    line = hid_ref.shape[1] // (2 * OWNED // COLS)
    total = jnp.zeros((line, COLS), jnp.float32)
    writes = []
    for i, (dz, dx, dc, first, count) in enumerate(spots):
        copy, offset = copies[i]
        copy.wait()
        owner = ((((rep >> 2) + dz) & 3) << 2) | ((rep & 3) ^ (2 * dx + dc))
        start = pl.multiple_of(owner * OWNED + first, ROWS)
        write = pltpu.make_async_copy(
            buf.at[pl.ds(offset, count)], out_ref.at[pl.ds(start, count)], out_sem.at[i]
        )
        write.start()
        writes.append(write)
        rows = pl.ds(pl.multiple_of((owner & 1) * (OWNED // COLS * line), 16), OWNED // COLS * line)
        blocks = hid_ref[owner >> 1, rows, :].astype(jnp.float32)
        for c in range(0, count, COLS):
            part = (first + c) // COLS * line
            total = total + jnp.dot(
                blocks[part : part + line].astype(jnp.bfloat16),
                buf[offset + c : offset + c + COLS, :],
                preferred_element_type=jnp.float32,
            )
    return total, writes


def early_kernel(spots, follows, where_ref, hid_ref, *refs):
    if follows:
        before_ref, _, *refs = refs
    count = len(spots)
    out_ref, sum_ref, buf, in_sem, out_sem = refs[count:]
    total, writes = place_pieces(
        spots, where_ref, hid_ref, refs[:count], out_ref, buf, in_sem, out_sem
    )
    sum_ref[...] = total + before_ref[...] if follows else total
    for write in writes:
        write.wait()


def late_kernel(spots, steps, rows, groups, where_ref, hid_ref, sum_ref, cos_ref, sin_ref, *refs):
    cached = [refs[4 * i : 4 * i + 4] for i in range(len(groups))]
    refs = refs[4 * len(groups) + 1 :]
    count = len(spots)
    out_ref, kv_ref, att_ref, buf, turn, in_sem, out_sem = refs[count:]
    total, writes = place_pieces(
        spots, where_ref, hid_ref, refs[:count], out_ref, buf, in_sem, out_sem
    )
    heads = steps * rows * GROUPS

    def join(which):
        return jnp.concatenate(
            [
                group[which][s * n : (s + 1) * n].reshape(n * GROUPS, HD)
                for s in range(steps)
                for group, n in zip(cached, groups)
            ],
            axis=0,
        )

    acc, old_top, old_total = join(1), join(2)[:, :1], join(3)[:, :1]
    total = total + sum_ref[...]
    keys = total[:, :HD]
    keys = keys * cos_ref[...] + pltpu.roll(keys, HD // 2, 1) * sin_ref[...]
    keys = keys.astype(jnp.bfloat16)
    values = total[:, HD:].astype(jnp.bfloat16)
    for s in range(steps):
        kv_ref[s, :, :HD] = keys[s * rows : (s + 1) * rows]
        kv_ref[s, :, HD:] = values[s * rows : (s + 1) * rows]
    scores = (
        lax.dot_general(
            cached[0][0][...].reshape(heads, HD),
            keys,
            (((1,), (1,)), ((), ())),
            preferred_element_type=jnp.float32,
        )
        * SCALE
    )
    line = lax.broadcasted_iota(jnp.int32, scores.shape, 0) // GROUPS
    column = lax.broadcasted_iota(jnp.int32, scores.shape, 1)
    seen = (line % rows == column % rows) & (column // rows <= line // rows)
    scores = jnp.where(seen, scores, -jnp.inf)
    top = jnp.maximum(old_top, jnp.max(scores, axis=-1, keepdims=True))
    fresh = jnp.exp(scores - top)
    fade = jnp.exp(old_top - top)
    denominator = old_total * fade + jnp.sum(fresh, axis=-1, keepdims=True)
    mixed = acc * (fade / denominator) + jnp.dot(
        (fresh / denominator).astype(jnp.bfloat16), values, preferred_element_type=jnp.float32
    )
    turn[...] = mixed
    for g in range(GROUPS):
        head = turn[pl.ds(g, steps * rows, stride=GROUPS), :].astype(jnp.bfloat16)
        for s in range(steps):
            att_ref[s, :, g * HD : (g + 1) * HD] = head[s * rows : (s + 1) * rows]
    for write in writes:
        write.wait()


def scratch(spots):
    return (
        pltpu.VMEM((sum(s[4] for s in spots), COLS), jnp.bfloat16),
        [pltpu.SemaphoreType.DMA((len(spots),)), pltpu.SemaphoreType.DMA((len(spots),))],
    )


def place_early(where, hid, before, pieces):
    spots = [p[1:] for p in pieces]
    buf, sems = scratch(spots)
    return pl.pallas_call(
        lambda *refs: early_kernel(spots, bool(before), *refs),
        in_specs=[SMEM, VMEM] + [VMEM, ANY][: len(before)] + [ANY] * len(pieces),
        out_specs=[VMEM, ANY][::-1],
        out_shape=[
            jax.ShapeDtypeStruct((REP * OWNED, COLS), jnp.bfloat16),
            jax.ShapeDtypeStruct((hid.shape[1] * COLS // (2 * OWNED), COLS), jnp.float32),
        ],
        scratch_shapes=[buf, *sems],
        input_output_aliases={3: 0} if before else {},
        compiler_params=pltpu.CompilerParams(vmem_limit_bytes=PLACE_VMEM),
        cost_estimate=PLACE_COST,
    )(where, hid, *before, *[p[0] for p in pieces])


def place_late(where, hid, partial, cosine, sine, cached, placed, pieces, steps, rows, groups):
    spots = [p[1:] for p in pieces]
    buf, sems = scratch(spots)
    small = 4 + 4 * len(groups)
    return pl.pallas_call(
        lambda *refs: late_kernel(spots, steps, rows, groups, *refs),
        in_specs=[SMEM] + [VMEM] * small + [ANY] * (1 + len(pieces)),
        out_specs=[ANY, VMEM, VMEM],
        out_shape=[
            jax.ShapeDtypeStruct((REP * OWNED, COLS), jnp.bfloat16),
            jax.ShapeDtypeStruct((steps, rows, COLS), jnp.bfloat16),
            jax.ShapeDtypeStruct((steps, rows, GROUPS * HD), jnp.bfloat16),
        ],
        scratch_shapes=[buf, pltpu.VMEM((steps * rows * GROUPS, HD), jnp.float32), *sems],
        input_output_aliases={1 + small: 0},
        compiler_params=pltpu.CompilerParams(vmem_limit_bytes=PLACE_VMEM),
        cost_estimate=PLACE_COST,
    )(where, hid, partial, cosine, sine, *cached, placed, *[p[0] for p in pieces])


def after(value, *others):
    return lax.optimization_barrier((value, *others))[0]


def local(kv_master, hidden, queries, key_cache, value_cache, lengths):
    steps, rows, _ = hidden.shape
    where = lax.axis_index("rep").astype(jnp.int32).reshape(1)

    moved = lax.all_to_all(pack(kv_master, hidden), "tp", split_axis=0, concat_axis=0, tiled=True)
    owned, hid = moved[:, :ROWS], moved[:, ROWS:]
    low, high = owned[: TP // 2].reshape(HALF, COLS), owned[TP // 2 :].reshape(HALF, COLS)
    cosine, sine = rotation_tables(lengths, steps)
    cached = attend_cache(queries, key_cache, value_cache, lengths, 0, rows)
    owned, low, high, *cached = lax.optimization_barrier((owned, low, high, *cached))
    owned = owned.reshape(OWNED, COLS)

    up, down = z_shift(1), z_shift(-1)
    near_x = send(owned, X_SWAP)
    low_b, high_a = send(low, up), send(high, down)
    low_a, high_b = send(low, down), send(high, up)
    low_b, high_a, cosine, sine = lax.optimization_barrier((low_b, high_a, cosine, sine))
    far_low, far_high = send(low_b, up), send(high_a, down)
    below_x, above_x = send(near_x, up), send(near_x, down)
    far_low_x, far_high_x = send(far_low, X_SWAP), send(far_high, X_SWAP)

    def both(pieces, *first):
        values = lax.optimization_barrier(tuple(p[0] for p in pieces) + first)
        pieces = [(v, *p[1:]) for v, p in zip(values, pieces)]
        return pieces + [(send(p[0], CORE_SWAP), p[1], p[2], 1, p[4], p[5]) for p in pieces]

    pieces = [
        (owned, 0, 0, 0, 0, OWNED),
        (near_x, 0, 1, 0, 0, OWNED),
        (low_b, 3, 0, 0, 0, HALF),
        (low_a, 1, 0, 0, 0, HALF),
        (high_b, 3, 0, 0, HALF, HALF),
        (high_a, 1, 0, 0, HALF, HALF),
    ]
    pieces += [(far_low, 2, 0, 0, 0, HALF), (far_high, 2, 0, 0, HALF, HALF)]
    placed, partial = place_early(where, hid, [], both(pieces, far_low, far_high))
    pieces = [
        (below_x, 3, 1, 0, 0, OWNED),
        (above_x, 1, 1, 0, 0, OWNED),
        (far_low_x, 2, 1, 0, 0, HALF),
        (far_high_x, 2, 1, 0, HALF, HALF),
    ]
    pieces = both(pieces, partial)
    return tuple(
        place_late(where, hid, partial, cosine, sine, cached, placed, pieces, steps, rows, [rows])
    )


def solution(mesh):
    return jax.shard_map(
        local,
        mesh=mesh,
        in_specs=(
            P(("rep", "tp"), None),
            P(None, "rep", "tp"),
            P(None, "rep", "tp"),
            P("rep", None, "tp"),
            P("rep", None, "tp"),
            P("rep"),
        ),
        out_specs=(P(None, "tp"), P(None, "rep", "tp"), P(None, "rep", "tp")),
        check_vma=False,
    )
```

time: 372 us -> 74.9 us (0.20); the launches traced: 367 us -> 74.6 us
  waiting for transfers between devices: 188 us -> 19.1 us
  blocking collectives: 99 us -> 0 us
  local copies, waits for them, and re-layouts: 36.2 us -> 1.98 us
  Pallas kernels: 0 us -> 22.9 us
  starting transfers between devices: 5.43 us -> 28.3 us
  matrix products: 18.9 us -> 0 us
  between operations: 14.2 us -> 0.79 us
  other arithmetic: 5.6 us -> 1.46 us
    psum x1 -> x0, waiting for transfers between devices: 109 us -> none  [local(): summed = lax.psum(partial_value, 'tp')]
    all_to_all x1 -> x0, blocking collectives: 99 us -> none  [local(): lax.all_to_all(grouped, 'tp', split_axis=1, concat_axis=1, tiled=True)]
    all_gather x1 -> x0, waiting for transfers between devices: 78.5 us -> none  [local(): gathered = lax.all_gather(weight, 'rep', axis=0, tiled=True)]
    pallas_call x0 -> x4, Pallas kernels: none -> 22.9 us  [the longest x1 9.65 us: attend_cache(): pl.pallas_call(lambda *refs: cache_kernel(first, count, *refs), grid=(cou...]
    ppermute x0 -> x23, starting transfers between devices: none -> 22.4 us  [send(): return lax.ppermute(value, 'rep', pairs)]
    dot_general x5 -> x0, matrix products: 18.9 us -> none  [the longest x1 8.31 us: attend(): jnp.einsum('srgqd,rpgd->srgqp', query_heads, cache_keys, preferred_elemen...]
    ppermute x0 -> x23, waiting for transfers between devices: none -> 18.1 us  [send(): return lax.ppermute(value, 'rep', pairs)]
    unnamed x13 -> x38, local copies, waits for them, and re-layouts: 18 us -> 1.09 us
  transfers between devices with their start and end apart: 3 -> 24, of which waited for: 2 -> 12; matrix products, arithmetic and copies ran while one was open for 7% -> 3% of each run, Pallas kernels for 0% -> 21%
where the time goes in v1:
time: 74.9 us; the launch traced here: 74.6 us
  starting transfers between devices  28.3 us (38%)
  Pallas kernels  22.9 us (31%)
  waiting for transfers between devices  19.1 us (26%)
  local copies, waits for them, and re-layouts  1.98 us (3%)
  other arithmetic  1.46 us (2%)
  between operations  0.79 us (1%)
    ppermute x23, starting transfers between devices, send(): return lax.ppermute(value, 'rep', pairs)  22.4 us
    ppermute x23, waiting for transfers between devices, send(): return lax.ppermute(value, 'rep', pairs)  18.1 us
    pallas_call x1, Pallas kernels, attend_cache(): pl.pallas_call(lambda *refs: cache_kernel(first, count, *refs), grid=(cou...  9.65 us
    pallas_call x1, Pallas kernels, place_early(): pl.pallas_call(lambda *refs: early_kernel(spots, bool(before), *refs), in...  6.26 us
    all_to_all x1, starting transfers between devices, local(): lax.all_to_all(pack(kv_master, hidden), 'tp', split_axis=0, concat_axis=0...  5.95 us
    pallas_call x1, Pallas kernels, place_late(): pl.pallas_call(lambda *refs: late_kernel(spots, steps, rows, groups, *ref...  4.83 us
    pallas_call x1, Pallas kernels, pack(): pl.pallas_call(pack_kernel, in_specs=[VMEM, VMEM], out_specs=VMEM, out_sh...  2.17 us
  transfers between devices with their start and end apart: 24, of which 12 were waited for; matrix products, arithmetic and copies ran while one was open for 3% of the time, Pallas kernels for 21%

profile of v1, /device:TPU:1, one launch (start us, length us, event | category | flops | bytes accessed | tf_op | source)
XLA Modules:
  0.0 74.6 jit_solution(9254685731849225696)
XLA Ops:
  0.6 2.2 %shard_map.85 = bf16[8,192,256]{2,1,0:T(8,128)(2,1)} custom-call(f32[128,2048]{1,0:T(8,128)} %kv_ref.1, bf16[2,4,2048]{2,1,0:T(4,128)(2,1)} %hid_ref.1), custom_call_target="tpu_custom_call" | custom-call | tf_op jit(solution)/shard_map/pallas_call | solution.py:78
  2.8 5.9 %all-to-all-start = ((bf16[8,192,256]{2,1,0:T(8,128)(2,1)}), bf16[8,192,256]{2,1,0:T(8,128)(2,1)S(1)}, u32[]{:S(2)}, u32[]{:S(2)}) async-start(bf16[8,192,256]{2,1,0:T(8,128)(2,1)} %shard_map.85), calls=%async_computation | async-start | bytes 1572864 | tf_op jit(solution)/shard_map/all_to_all | solution.py:319
  8.8 0.7 add_convert_fusion
  9.4 0.1 convert_element_type.12
  9.5 9.7 %shard_map.86 = (bf16[8,16,128]{2,1,0:T(8,128)(2,1)}, f32[8,16,128]{2,1,0:T(8,128)}, f32[8,16,128]{2,1,0:T(8,128)}, f32[8,16,128]{2,1,0:T(8,128)}) custom-call(s32[4]{0:T(128)} %refs_0_.1, bf16[2,4,2048]{2,1,0:T(4,128)(2,1)} %refs_1_.1, bf16[4,8192,128]{2,1,0:T(8,128)(2,1)} %refs_2_.1, bf16[4,8192,128]{2,1,0:T(8,128)(2,1)} %refs_3_.1), custom_call_target="tpu_custom_call" | custom-call | flops 536870912 | bytes 16777216 | tf_op jit(solution)/shard_map/pallas_call | solution.py:137
  19.2 1.0 %all-to-all-done = bf16[8,192,256]{2,1,0:T(8,128)(2,1)S(1)} async-done(((bf16[8,192,256]{2,1,0:T(8,128)(2,1)}), bf16[8,192,256]{2,1,0:T(8,128)(2,1)S(1)}, u32[]{:S(2)}, u32[]{:S(2)}) %all-to-all-start) | async-done | bytes 786464 | tf_op jit(solution)/shard_map/all_to_all | solution.py:319
  20.2 1.7 %collective-permute-start.1 = (bf16[512,256]{1,0:T(8,128)(2,1)S(1)}, bf16[512,256]{1,0:T(8,128)(2,1)S(1)}, u32[]{:S(2)}, u32[]{:S(2)}) collective-permute-start(bf16[512,256]{1,0:T(8,128)(2,1)S(1)} %bitcast.9), channel_id=1, source_target_pairs={{0,32},{8,40},{16,48},{24,56},{32,64},{40,72},{48,80},{56,88},{64,... | collective-permute-start | bytes 786440 | tf_op jit(solution)/shard_map/ppermute | solution.py:43
  21.9 2.2 %collective-permute-start.2 = (bf16[512,256]{1,0:T(8,128)(2,1)S(1)}, bf16[512,256]{1,0:T(8,128)(2,1)S(1)}, u32[]{:S(2)}, u32[]{:S(2)}) collective-permute-start(bf16[512,256]{1,0:T(8,128)(2,1)S(1)} %bitcast.7), channel_id=1, source_target_pairs={{0,96},{8,104},{16,112},{24,120},{32,0},{40,8},{48,16},{56,24},{64... | collective-permute-start | bytes 786440 | tf_op jit(solution)/shard_map/ppermute | solution.py:43
  24.1 2.5 %collective-permute-start = (bf16[1024,256]{1,0:T(8,128)(2,1)S(1)}, bf16[1024,256]{1,0:T(8,128)(2,1)S(1)}, u32[]{:S(2)}, u32[]{:S(2)}) collective-permute-start(bf16[1024,256]{1,0:T(8,128)(2,1)S(1)} %bitcast.4), channel_id=1, source_target_pairs={{0,16},{8,24},{16,0},{24,8},{32,48},{40,56},{48,32},{56,40},{64,80... | collective-permute-start | bytes 1572872 | tf_op jit(solution)/shard_map/ppermute | solution.py:43
  26.6 0.1 fusion
  26.7 0.7 pad_maximum_fusion
  27.4 1.4 %collective-permute-start.3 = (bf16[512,256]{1,0:T(8,128)(2,1)S(1)}, bf16[512,256]{1,0:T(8,128)(2,1)S(1)}, u32[]{:S(2)}, u32[]{:S(2)}) collective-permute-start(bf16[512,256]{1,0:T(8,128)(2,1)S(1)} %bitcast.10), channel_id=1, source_target_pairs={{0,96},{8,104},{16,112},{24,120},{32,0},{40,8},{48,16},{56,24},{64... | collective-permute-start | bytes 786440 | tf_op jit(solution)/shard_map/ppermute | solution.py:43
  28.8 0.1 collective-permute-start.4
  28.8 0.3 collective-permute-done.1.refs_4_
  29.1 0.0 collective-permute-done.2.refs_7_
  29.1 0.4 collective-permute-start.5
  29.5 2.3 %collective-permute-start.6 = (bf16[512,256]{1,0:T(8,128)(2,1)S(1)}, bf16[512,256]{1,0:T(8,128)(2,1)}, u32[]{:S(2)}, u32[]{:S(2)}) collective-permute-start(bf16[512,256]{1,0:T(8,128)(2,1)S(1)} %collective-permute-done.2.refs_7_), channel_id=1, source_target_pairs={{0,96},{8,104},{16,112},{24,120},{32,0},{40,8},{48,16},{56,24},{64... | collective-permute-start | bytes 786440 | tf_op jit(solution)/shard_map/ppermute | solution.py:43
  31.9 2.1 %collective-permute-done.3.refs_5_ = bf16[512,256]{1,0:T(8,128)(2,1)S(1)} collective-permute-done((bf16[512,256]{1,0:T(8,128)(2,1)S(1)}, bf16[512,256]{1,0:T(8,128)(2,1)S(1)}, u32[]{:S(2)}, u32[]{:S(2)}) %collective-permute-start.3) | collective-permute-done | bytes 262176 | tf_op jit(solution)/shard_map/ppermute | solution.py:43
  33.9 1.5 %collective-permute-done.4.refs_6_ = bf16[512,256]{1,0:T(8,128)(2,1)S(1)} collective-permute-done((bf16[512,256]{1,0:T(8,128)(2,1)S(1)}, bf16[512,256]{1,0:T(8,128)(2,1)S(1)}, u32[]{:S(2)}, u32[]{:S(2)}) %collective-permute-start.4) | collective-permute-done | bytes 262176 | tf_op jit(solution)/shard_map/ppermute | solution.py:43
  35.5 1.7 %collective-permute-done.refs_3_ = bf16[1024,256]{1,0:T(8,128)(2,1)S(1)} collective-permute-done((bf16[1024,256]{1,0:T(8,128)(2,1)S(1)}, bf16[1024,256]{1,0:T(8,128)(2,1)S(1)}, u32[]{:S(2)}, u32[]{:S(2)}) %collective-permute-start) | collective-permute-done | bytes 524320 | tf_op jit(solution)/shard_map/ppermute | solution.py:43
  37.2 3.5 %collective-permute-done.5.refs_8_ = bf16[512,256]{1,0:T(8,128)(2,1)} collective-permute-done((bf16[512,256]{1,0:T(8,128)(2,1)S(1)}, bf16[512,256]{1,0:T(8,128)(2,1)}, u32[]{:S(2)}, u32[]{:S(2)}) %collective-permute-start.5) | collective-permute-done | bytes 262176 | tf_op jit(solution)/shard_map/ppermute | solution.py:43
  40.7 3.7 %collective-permute-start.9 = (bf16[512,256]{1,0:T(8,128)(2,1)S(1)}, bf16[512,256]{1,0:T(8,128)(2,1)S(1)}, u32[]{:S(2)}, u32[]{:S(2)}) collective-permute-start(bf16[512,256]{1,0:T(8,128)(2,1)S(1)} %collective-permute-done.1.refs_4_), channel_id=1, source_target_pairs={{0,8},{8,0},{16,24},{24,16},{32,40},{40,32},{48,56},{56,48},{64,72... | collective-permute-start | bytes 786440 | tf_op jit(solution)/shard_map/ppermute | solution.py:43
  44.4 0.0 collective-permute-start.10
  44.4 0.5 collective-permute-start.11
  44.9 0.0 collective-permute-start.12
  44.9 0.5 collective-permute-start.7
  45.4 0.1 collective-permute-done.9.refs_12_
  45.6 0.4 collective-permute-start.13
  46.0 0.4 collective-permute-start.8
  46.3 0.4 collective-permute-start.14
  46.7 1.1 %collective-permute-start.16 = (bf16[1024,256]{1,0:T(8,128)(2,1)S(1)}, bf16[1024,256]{1,0:T(8,128)(2,1)S(1)}, u32[]{:S(2)}, u32[]{:S(2)}) collective-permute-start(bf16[1024,256]{1,0:T(8,128)(2,1)S(1)} %collective-permute-done.refs_3_), channel_id=1, source_target_pairs={{0,96},{8,104},{16,112},{24,120},{32,0},{40,8},{48,16},{56,24},{64... | collective-permute-start | bytes 1572872 | tf_op jit(solution)/shard_map/ppermute | solution.py:43
  47.8 0.6 collective-permute-done.13.refs_16_
  48.4 0.7 collective-permute-done.14.refs_17_
  49.2 1.3 %collective-permute-start.17 = (bf16[512,256]{1,0:T(8,128)(2,1)}, bf16[512,256]{1,0:T(8,128)(2,1)}, u32[]{:S(2)}, u32[]{:S(2)}) collective-permute-start(bf16[512,256]{1,0:T(8,128)(2,1)} %collective-permute-done.5.refs_8_), channel_id=1, source_target_pairs={{0,16},{8,24},{16,0},{24,8},{32,48},{40,56},{48,32},{56,40},{64,80... | collective-permute-start | bytes 786440 | tf_op jit(solution)/shard_map/ppermute | solution.py:43
  50.5 1.8 %collective-permute-start.18 = (bf16[512,256]{1,0:T(8,128)(2,1)}, bf16[512,256]{1,0:T(8,128)(2,1)}, u32[]{:S(2)}, u32[]{:S(2)}) collective-permute-start(bf16[512,256]{1,0:T(8,128)(2,1)} %collective-permute-done.6.refs_9_), channel_id=1, source_target_pairs={{0,16},{8,24},{16,0},{24,8},{32,48},{40,56},{48,32},{56,40},{64,80... | collective-permute-start | bytes 786440 | tf_op jit(solution)/shard_map/ppermute | solution.py:43
  52.2 0.7 slice.18.refs_1_
  53.0 6.3 %shard_map.87 = (bf16[16384,256]{1,0:T(8,128)(2,1)}, f32[8,256]{1,0:T(8,128)}) custom-call(s32[1]{0:T(128)} %bitcast.refs_0_, bf16[8,64,256]{2,1,0:T(8,128)(2,1)} %slice.18.refs_1_, bf16[1024,256]{1,0:T(8,128)(2,1)} %bitcast.6, bf16[1024,256]{1,0:T(8,128)(2,1)} %copy-done.5, bf16[512,256]{1,0:T(8,128)(2,1)} %copy-done.7, bf16[512,256]{1,0:T(8,128)(2,1)} %copy-done.9, ...), custom_call_target="tpu_custom_call" | custom-call | flops 1000 | bytes 1000 | tf_op jit(solution)/shard_map/pallas_call | solution.py:276
  59.3 4.8 %collective-permute-done.18.refs_13_ = bf16[512,256]{1,0:T(8,128)(2,1)} collective-permute-done((bf16[512,256]{1,0:T(8,128)(2,1)}, bf16[512,256]{1,0:T(8,128)(2,1)}, u32[]{:S(2)}, u32[]{:S(2)}) %collective-permute-start.18) | collective-permute-done | bytes 262176 | tf_op jit(solution)/shard_map/ppermute | solution.py:43
  64.1 1.3 %collective-permute-start.19 = (bf16[1024,256]{1,0:T(8,128)(2,1)S(1)}, bf16[1024,256]{1,0:T(8,128)(2,1)S(1)}, u32[]{:S(2)}, u32[]{:S(2)}) collective-permute-start(bf16[1024,256]{1,0:T(8,128)(2,1)S(1)} %collective-permute-done.15.refs_10_), channel_id=1, source_target_pairs={{0,8},{8,0},{16,24},{24,16},{32,40},{40,32},{48,56},{56,48},{64,72... | collective-permute-start | bytes 1572872 | tf_op jit(solution)/shard_map/ppermute | solution.py:43
  65.4 0.1 collective-permute-start.20
  65.5 0.4 collective-permute-start.21
  65.9 0.1 collective-permute-start.22
  66.0 1.9 %collective-permute-done.21.refs_16_ = bf16[512,256]{1,0:T(8,128)(2,1)S(1)} collective-permute-done((bf16[512,256]{1,0:T(8,128)(2,1)}, bf16[512,256]{1,0:T(8,128)(2,1)S(1)}, u32[]{:S(2)}, u32[]{:S(2)}) %collective-permute-start.21) | collective-permute-done | bytes 262176 | tf_op jit(solution)/shard_map/ppermute | solution.py:43
  67.9 0.7 %collective-permute-done.22.refs_17_ = bf16[512,256]{1,0:T(8,128)(2,1)S(1)} collective-permute-done((bf16[512,256]{1,0:T(8,128)(2,1)}, bf16[512,256]{1,0:T(8,128)(2,1)S(1)}, u32[]{:S(2)}, u32[]{:S(2)}) %collective-permute-start.22) | collective-permute-done | bytes 262176 | tf_op jit(solution)/shard_map/ppermute | solution.py:43
  68.7 0.7 copy-done.18
  69.4 0.2 copy-done.3
  69.6 0.2 copy-done.4
  69.8 4.8 %shard_map.88 = (bf16[16384,256]{1,0:T(8,128)(2,1)}, bf16[2,4,256]{2,1,0:T(4,128)(2,1)}, bf16[2,4,2048]{2,1,0:T(4,128)(2,1)}) custom-call(s32[1]{0:T(128)} %bitcast.refs_0_, bf16[8,64,256]{2,1,0:T(8,128)(2,1)} %slice.18.refs_1_, f32[8,256]{1,0:T(8,128)} %get-tuple-element.49.refs_2_, ...), custom_call_target="tpu_custom_call", output_to_operand_aliasing={{0}: (9, {})} | custom-call | flops 1000 | bytes 1000 | tf_op jit(solution)/shard_map/pallas_call | solution.py:295
  (50 shorter events, 0.2 us)
Async XLA Ops:
  2.8 17.3 %all-to-all-start = ((bf16[8,192,256]{2,1,0:T(8,128)(2,1)}), bf16[8,192,256]{2,1,0:T(8,128)(2,1)S(1)}, u32[]{:S(2)}, u32[]{:S(2)}) async-start(bf16[8,192,256]{2,1,0:T(8,128)(2,1)} %shard_map.85), calls=%async_computation | async-start | bytes 1572864 | tf_op jit(solution)/shard_map/all_to_all | solution.py:319
  20.2 32.8 %copy-start = (bf16[8,128,256]{2,1,0:T(8,128)(2,1)}, bf16[8,128,256]{2,1,0:T(8,128)(2,1)S(1)}, u32[]{:S(2)}) copy-start(bf16[8,128,256]{2,1,0:T(8,128)(2,1)S(1)} %slice.19) | copy-start | bytes 1572868
  20.2 8.9 %collective-permute-start.1 = (bf16[512,256]{1,0:T(8,128)(2,1)S(1)}, bf16[512,256]{1,0:T(8,128)(2,1)S(1)}, u32[]{:S(2)}, u32[]{:S(2)}) collective-permute-start(bf16[512,256]{1,0:T(8,128)(2,1)S(1)} %bitcast.9), channel_id=1, source_target_pairs={{0,32},{8,40},{16,48},{24,56},{32,64},{40,72},{48,80},{56,88},{64,... | collective-permute-start | bytes 786440 | tf_op jit(solution)/shard_map/ppermute | solution.py:43
  21.9 7.2 %collective-permute-start.2 = (bf16[512,256]{1,0:T(8,128)(2,1)S(1)}, bf16[512,256]{1,0:T(8,128)(2,1)S(1)}, u32[]{:S(2)}, u32[]{:S(2)}) collective-permute-start(bf16[512,256]{1,0:T(8,128)(2,1)S(1)} %bitcast.7), channel_id=1, source_target_pairs={{0,96},{8,104},{16,112},{24,120},{32,0},{40,8},{48,16},{56,24},{64... | collective-permute-start | bytes 786440 | tf_op jit(solution)/shard_map/ppermute | solution.py:43
  24.1 13.1 %collective-permute-start = (bf16[1024,256]{1,0:T(8,128)(2,1)S(1)}, bf16[1024,256]{1,0:T(8,128)(2,1)S(1)}, u32[]{:S(2)}, u32[]{:S(2)}) collective-permute-start(bf16[1024,256]{1,0:T(8,128)(2,1)S(1)} %bitcast.4), channel_id=1, source_target_pairs={{0,16},{8,24},{16,0},{24,8},{32,48},{40,56},{48,32},{56,40},{64,80... | collective-permute-start | bytes 1572872 | tf_op jit(solution)/shard_map/ppermute | solution.py:43
  27.4 6.6 %collective-permute-start.3 = (bf16[512,256]{1,0:T(8,128)(2,1)S(1)}, bf16[512,256]{1,0:T(8,128)(2,1)S(1)}, u32[]{:S(2)}, u32[]{:S(2)}) collective-permute-start(bf16[512,256]{1,0:T(8,128)(2,1)S(1)} %bitcast.10), channel_id=1, source_target_pairs={{0,96},{8,104},{16,112},{24,120},{32,0},{40,8},{48,16},{56,24},{64... | collective-permute-start | bytes 786440 | tf_op jit(solution)/shard_map/ppermute | solution.py:43
  28.8 6.7 %collective-permute-start.4 = (bf16[512,256]{1,0:T(8,128)(2,1)S(1)}, bf16[512,256]{1,0:T(8,128)(2,1)S(1)}, u32[]{:S(2)}, u32[]{:S(2)}) collective-permute-start(bf16[512,256]{1,0:T(8,128)(2,1)S(1)} %bitcast.8), channel_id=1, source_target_pairs={{0,32},{8,40},{16,48},{24,56},{32,64},{40,72},{48,80},{56,88},{64,... | collective-permute-start | bytes 786440 | tf_op jit(solution)/shard_map/ppermute | solution.py:43
  29.1 17.6 %copy-start.7 = (bf16[512,256]{1,0:T(8,128)(2,1)}, bf16[512,256]{1,0:T(8,128)(2,1)S(1)}, u32[]{:S(2)}) copy-start(bf16[512,256]{1,0:T(8,128)(2,1)S(1)} %collective-permute-done.1.refs_4_) | copy-start | bytes 786436
  29.1 17.6 %copy-start.8 = (bf16[512,256]{1,0:T(8,128)(2,1)}, bf16[512,256]{1,0:T(8,128)(2,1)S(1)}, u32[]{:S(2)}) copy-start(bf16[512,256]{1,0:T(8,128)(2,1)S(1)} %collective-permute-done.2.refs_7_) | copy-start | bytes 786436
  29.1 11.6 %collective-permute-start.5 = (bf16[512,256]{1,0:T(8,128)(2,1)S(1)}, bf16[512,256]{1,0:T(8,128)(2,1)}, u32[]{:S(2)}, u32[]{:S(2)}) collective-permute-start(bf16[512,256]{1,0:T(8,128)(2,1)S(1)} %collective-permute-done.1.refs_4_), channel_id=1, source_target_pairs={{0,32},{8,40},{16,48},{24,56},{32,64},{40,72},{48,80},{56,88},{64,... | collective-permute-start | bytes 786440 | tf_op jit(solution)/shard_map/ppermute | solution.py:43
  29.5 11.2 %collective-permute-start.6 = (bf16[512,256]{1,0:T(8,128)(2,1)S(1)}, bf16[512,256]{1,0:T(8,128)(2,1)}, u32[]{:S(2)}, u32[]{:S(2)}) collective-permute-start(bf16[512,256]{1,0:T(8,128)(2,1)S(1)} %collective-permute-done.2.refs_7_), channel_id=1, source_target_pairs={{0,96},{8,104},{16,112},{24,120},{32,0},{40,8},{48,16},{56,24},{64... | collective-permute-start | bytes 786440 | tf_op jit(solution)/shard_map/ppermute | solution.py:43
  33.9 13.8 %copy-start.9 = (bf16[512,256]{1,0:T(8,128)(2,1)}, bf16[512,256]{1,0:T(8,128)(2,1)S(1)}, u32[]{:S(2)}) copy-start(bf16[512,256]{1,0:T(8,128)(2,1)S(1)} %collective-permute-done.3.refs_5_) | copy-start | bytes 786436
  35.5 12.3 %copy-start.10 = (bf16[512,256]{1,0:T(8,128)(2,1)}, bf16[512,256]{1,0:T(8,128)(2,1)S(1)}, u32[]{:S(2)}) copy-start(bf16[512,256]{1,0:T(8,128)(2,1)S(1)} %collective-permute-done.4.refs_6_) | copy-start | bytes 786436
  37.2 15.8 %copy-start.5 = (bf16[1024,256]{1,0:T(8,128)(2,1)}, bf16[1024,256]{1,0:T(8,128)(2,1)S(1)}, u32[]{:S(2)}) copy-start(bf16[1024,256]{1,0:T(8,128)(2,1)S(1)} %collective-permute-done.refs_3_) | copy-start | bytes 1572868
  40.7 4.9 %collective-permute-start.9 = (bf16[512,256]{1,0:T(8,128)(2,1)S(1)}, bf16[512,256]{1,0:T(8,128)(2,1)S(1)}, u32[]{:S(2)}, u32[]{:S(2)}) collective-permute-start(bf16[512,256]{1,0:T(8,128)(2,1)S(1)} %collective-permute-done.1.refs_4_), channel_id=1, source_target_pairs={{0,8},{8,0},{16,24},{24,16},{32,40},{40,32},{48,56},{56,48},{64,72... | collective-permute-start | bytes 786440 | tf_op jit(solution)/shard_map/ppermute | solution.py:43
  44.4 1.5 %collective-permute-start.10 = (bf16[512,256]{1,0:T(8,128)(2,1)S(1)}, bf16[512,256]{1,0:T(8,128)(2,1)S(1)}, u32[]{:S(2)}, u32[]{:S(2)}) collective-permute-start(bf16[512,256]{1,0:T(8,128)(2,1)S(1)} %collective-permute-done.3.refs_5_), channel_id=1, source_target_pairs={{0,8},{8,0},{16,24},{24,16},{32,40},{40,32},{48,56},{56,48},{64,72... | collective-permute-start | bytes 786440 | tf_op jit(solution)/shard_map/ppermute | solution.py:43
  44.4 1.9 %collective-permute-start.11 = (bf16[512,256]{1,0:T(8,128)(2,1)S(1)}, bf16[512,256]{1,0:T(8,128)(2,1)S(1)}, u32[]{:S(2)}, u32[]{:S(2)}) collective-permute-start(bf16[512,256]{1,0:T(8,128)(2,1)S(1)} %collective-permute-done.4.refs_6_), channel_id=1, source_target_pairs={{0,8},{8,0},{16,24},{24,16},{32,40},{40,32},{48,56},{56,48},{64,72... | collective-permute-start | bytes 786440 | tf_op jit(solution)/shard_map/ppermute | solution.py:43
  44.9 1.8 %collective-permute-start.12 = (bf16[512,256]{1,0:T(8,128)(2,1)S(1)}, bf16[512,256]{1,0:T(8,128)(2,1)S(1)}, u32[]{:S(2)}, u32[]{:S(2)}) collective-permute-start(bf16[512,256]{1,0:T(8,128)(2,1)S(1)} %collective-permute-done.2.refs_7_), channel_id=1, source_target_pairs={{0,8},{8,0},{16,24},{24,16},{32,40},{40,32},{48,56},{56,48},{64,72... | collective-permute-start | bytes 786440 | tf_op jit(solution)/shard_map/ppermute | solution.py:43
  44.9 5.5 %collective-permute-start.7 = (bf16[1024,256]{1,0:T(8,128)(2,1)S(1)}, bf16[1024,256]{1,0:T(8,128)(2,1)S(1)}, u32[]{:S(2)}, u32[]{:S(2)}) collective-permute-start(bf16[1024,256]{1,0:T(8,128)(2,1)S(1)} %bitcast.5), channel_id=1, source_target_pairs={{0,8},{8,0},{16,24},{24,16},{32,40},{40,32},{48,56},{56,48},{64,72... | collective-permute-start | bytes 1572872 | tf_op jit(solution)/shard_map/ppermute | solution.py:43
  45.6 4.9 %copy-start.11 = (bf16[512,256]{1,0:T(8,128)(2,1)}, bf16[512,256]{1,0:T(8,128)(2,1)S(1)}, u32[]{:S(2)}) copy-start(bf16[512,256]{1,0:T(8,128)(2,1)S(1)} %collective-permute-done.9.refs_12_) | copy-start | bytes 786436
  45.6 2.8 %collective-permute-start.13 = (bf16[512,256]{1,0:T(8,128)(2,1)}, bf16[512,256]{1,0:T(8,128)(2,1)S(1)}, u32[]{:S(2)}, u32[]{:S(2)}) collective-permute-start(bf16[512,256]{1,0:T(8,128)(2,1)} %collective-permute-done.5.refs_8_), channel_id=1, source_target_pairs={{0,8},{8,0},{16,24},{24,16},{32,40},{40,32},{48,56},{56,48},{64,72... | collective-permute-start | bytes 786440 | tf_op jit(solution)/shard_map/ppermute | solution.py:43
  46.0 6.3 %copy-start.12 = (bf16[512,256]{1,0:T(8,128)(2,1)}, bf16[512,256]{1,0:T(8,128)(2,1)S(1)}, u32[]{:S(2)}) copy-start(bf16[512,256]{1,0:T(8,128)(2,1)S(1)} %collective-permute-done.10.refs_13_) | copy-start | bytes 786436
  46.0 7.0 %collective-permute-start.8 = (bf16[1024,256]{1,0:T(8,128)(2,1)S(1)}, bf16[1024,256]{1,0:T(8,128)(2,1)}, u32[]{:S(2)}, u32[]{:S(2)}) collective-permute-start(bf16[1024,256]{1,0:T(8,128)(2,1)S(1)} %collective-permute-done.refs_3_), channel_id=1, source_target_pairs={{0,8},{8,0},{16,24},{24,16},{32,40},{40,32},{48,56},{56,48},{64,72... | collective-permute-start | bytes 1572872 | tf_op jit(solution)/shard_map/ppermute | solution.py:43
  46.3 5.9 %copy-start.13 = (bf16[512,256]{1,0:T(8,128)(2,1)}, bf16[512,256]{1,0:T(8,128)(2,1)S(1)}, u32[]{:S(2)}) copy-start(bf16[512,256]{1,0:T(8,128)(2,1)S(1)} %collective-permute-done.11.refs_14_) | copy-start | bytes 786436
  46.3 2.8 %collective-permute-start.14 = (bf16[512,256]{1,0:T(8,128)(2,1)}, bf16[512,256]{1,0:T(8,128)(2,1)S(1)}, u32[]{:S(2)}, u32[]{:S(2)}) collective-permute-start(bf16[512,256]{1,0:T(8,128)(2,1)} %collective-permute-done.6.refs_9_), channel_id=1, source_target_pairs={{0,8},{8,0},{16,24},{24,16},{32,40},{40,32},{48,56},{56,48},{64,72... | collective-permute-start | bytes 786440 | tf_op jit(solution)/shard_map/ppermute | solution.py:43
  46.7 5.5 %copy-start.14 = (bf16[512,256]{1,0:T(8,128)(2,1)}, bf16[512,256]{1,0:T(8,128)(2,1)S(1)}, u32[]{:S(2)}) copy-start(bf16[512,256]{1,0:T(8,128)(2,1)S(1)} %collective-permute-done.12.refs_15_) | copy-start | bytes 786436
  46.7 17.4 %collective-permute-start.16 = (bf16[1024,256]{1,0:T(8,128)(2,1)S(1)}, bf16[1024,256]{1,0:T(8,128)(2,1)S(1)}, u32[]{:S(2)}, u32[]{:S(2)}) collective-permute-start(bf16[1024,256]{1,0:T(8,128)(2,1)S(1)} %collective-permute-done.refs_3_), channel_id=1, source_target_pairs={{0,96},{8,104},{16,112},{24,120},{32,0},{40,8},{48,16},{56,24},{64... | collective-permute-start | bytes 1572872 | tf_op jit(solution)/shard_map/ppermute | solution.py:43
  48.4 3.8 %copy-start.15 = (bf16[512,256]{1,0:T(8,128)(2,1)}, bf16[512,256]{1,0:T(8,128)(2,1)S(1)}, u32[]{:S(2)}) copy-start(bf16[512,256]{1,0:T(8,128)(2,1)S(1)} %collective-permute-done.13.refs_16_) | copy-start | bytes 786436
  48.4 15.7 %collective-permute-start.15 = (bf16[1024,256]{1,0:T(8,128)(2,1)S(1)}, bf16[1024,256]{1,0:T(8,128)(2,1)S(1)}, u32[]{:S(2)}, u32[]{:S(2)}) collective-permute-start(bf16[1024,256]{1,0:T(8,128)(2,1)S(1)} %collective-permute-done.refs_3_), channel_id=1, source_target_pairs={{0,32},{8,40},{16,48},{24,56},{32,64},{40,72},{48,80},{56,88},{64,... | collective-permute-start | bytes 1572872 | tf_op jit(solution)/shard_map/ppermute | solution.py:43
  49.2 3.1 %copy-start.16 = (bf16[512,256]{1,0:T(8,128)(2,1)}, bf16[512,256]{1,0:T(8,128)(2,1)S(1)}, u32[]{:S(2)}) copy-start(bf16[512,256]{1,0:T(8,128)(2,1)S(1)} %collective-permute-done.14.refs_17_) | copy-start | bytes 786436
  49.2 10.1 %collective-permute-start.17 = (bf16[512,256]{1,0:T(8,128)(2,1)}, bf16[512,256]{1,0:T(8,128)(2,1)}, u32[]{:S(2)}, u32[]{:S(2)}) collective-permute-start(bf16[512,256]{1,0:T(8,128)(2,1)} %collective-permute-done.5.refs_8_), channel_id=1, source_target_pairs={{0,16},{8,24},{16,0},{24,8},{32,48},{40,56},{48,32},{56,40},{64,80... | collective-permute-start | bytes 786440 | tf_op jit(solution)/shard_map/ppermute | solution.py:43
  50.4 2.5 %copy-start.6 = (bf16[1024,256]{1,0:T(8,128)(2,1)}, bf16[1024,256]{1,0:T(8,128)(2,1)S(1)}, u32[]{:S(2)}) copy-start(bf16[1024,256]{1,0:T(8,128)(2,1)S(1)} %collective-permute-done.7.refs_10_) | copy-start | bytes 1572868
  50.5 13.7 %collective-permute-start.18 = (bf16[512,256]{1,0:T(8,128)(2,1)}, bf16[512,256]{1,0:T(8,128)(2,1)}, u32[]{:S(2)}, u32[]{:S(2)}) collective-permute-start(bf16[512,256]{1,0:T(8,128)(2,1)} %collective-permute-done.6.refs_9_), channel_id=1, source_target_pairs={{0,16},{8,24},{16,0},{24,8},{32,48},{40,56},{48,32},{56,40},{64,80... | collective-permute-start | bytes 786440 | tf_op jit(solution)/shard_map/ppermute | solution.py:43
  64.1 4.6 %copy-start.1 = (bf16[1024,256]{1,0:T(8,128)(2,1)}, bf16[1024,256]{1,0:T(8,128)(2,1)S(1)}, u32[]{:S(2)}) copy-start(bf16[1024,256]{1,0:T(8,128)(2,1)S(1)} %collective-permute-done.16.refs_11_) | copy-start | bytes 1572868
  64.1 4.6 %copy-start.2 = (bf16[1024,256]{1,0:T(8,128)(2,1)}, bf16[1024,256]{1,0:T(8,128)(2,1)S(1)}, u32[]{:S(2)}) copy-start(bf16[1024,256]{1,0:T(8,128)(2,1)S(1)} %collective-permute-done.15.refs_10_) | copy-start | bytes 1572868
  64.1 4.5 %collective-permute-start.19 = (bf16[1024,256]{1,0:T(8,128)(2,1)S(1)}, bf16[1024,256]{1,0:T(8,128)(2,1)S(1)}, u32[]{:S(2)}, u32[]{:S(2)}) collective-permute-start(bf16[1024,256]{1,0:T(8,128)(2,1)S(1)} %collective-permute-done.15.refs_10_), channel_id=1, source_target_pairs={{0,8},{8,0},{16,24},{24,16},{32,40},{40,32},{48,56},{56,48},{64,72... | collective-permute-start | bytes 1572872 | tf_op jit(solution)/shard_map/ppermute | solution.py:43
  65.4 3.3 %collective-permute-start.20 = (bf16[1024,256]{1,0:T(8,128)(2,1)S(1)}, bf16[1024,256]{1,0:T(8,128)(2,1)S(1)}, u32[]{:S(2)}, u32[]{:S(2)}) collective-permute-start(bf16[1024,256]{1,0:T(8,128)(2,1)S(1)} %collective-permute-done.16.refs_11_), channel_id=1, source_target_pairs={{0,8},{8,0},{16,24},{24,16},{32,40},{40,32},{48,56},{56,48},{64,72... | collective-permute-start | bytes 1572872 | tf_op jit(solution)/shard_map/ppermute | solution.py:43
  65.5 2.4 %collective-permute-start.21 = (bf16[512,256]{1,0:T(8,128)(2,1)}, bf16[512,256]{1,0:T(8,128)(2,1)S(1)}, u32[]{:S(2)}, u32[]{:S(2)}) collective-permute-start(bf16[512,256]{1,0:T(8,128)(2,1)} %collective-permute-done.17.refs_12_), channel_id=1, source_target_pairs={{0,8},{8,0},{16,24},{24,16},{32,40},{40,32},{48,56},{56,48},{64,72... | collective-permute-start | bytes 786440 | tf_op jit(solution)/shard_map/ppermute | solution.py:43
  65.9 2.7 %collective-permute-start.22 = (bf16[512,256]{1,0:T(8,128)(2,1)}, bf16[512,256]{1,0:T(8,128)(2,1)S(1)}, u32[]{:S(2)}, u32[]{:S(2)}) collective-permute-start(bf16[512,256]{1,0:T(8,128)(2,1)} %collective-permute-done.18.refs_13_), channel_id=1, source_target_pairs={{0,8},{8,0},{16,24},{24,16},{32,40},{40,32},{48,56},{56,48},{64,72... | collective-permute-start | bytes 786440 | tf_op jit(solution)/shard_map/ppermute | solution.py:43
  67.9 0.8 %copy-start.17 = (bf16[512,256]{1,0:T(8,128)(2,1)}, bf16[512,256]{1,0:T(8,128)(2,1)S(1)}, u32[]{:S(2)}) copy-start(bf16[512,256]{1,0:T(8,128)(2,1)S(1)} %collective-permute-done.21.refs_16_) | copy-start | bytes 786436
  68.7 0.7 copy-start.18
  68.7 0.9 %copy-start.3 = (bf16[1024,256]{1,0:T(8,128)(2,1)}, bf16[1024,256]{1,0:T(8,128)(2,1)S(1)}, u32[]{:S(2)}) copy-start(bf16[1024,256]{1,0:T(8,128)(2,1)S(1)} %collective-permute-done.19.refs_14_) | copy-start | bytes 1572868
  68.7 1.1 %copy-start.4 = (bf16[1024,256]{1,0:T(8,128)(2,1)}, bf16[1024,256]{1,0:T(8,128)(2,1)S(1)}, u32[]{:S(2)}) copy-start(bf16[1024,256]{1,0:T(8,128)(2,1)S(1)} %collective-permute-done.20.refs_15_) | copy-start | bytes 1572868

commit v2 on v1

--- a/solution.py
+++ b/solution.py
@@ -21,12 +21,13 @@
 COLS = 2 * HD
 VMEM_BYTES = 60 * 2**20
 CACHE_VMEM = 60 * 2**20
-PLACE_VMEM = 60 * 2**20
-PLACE_COST = pl.CostEstimate(flops=1000, bytes_accessed=1000, transcendentals=0)
+PLACE_VMEM = 48 * 2**20
+PLACE_COST = pl.CostEstimate(flops=20000000000, bytes_accessed=1000, transcendentals=0)
 
 rope_base = 500000.0
 
 ANY = pl.BlockSpec(memory_space=pl.ANY)
+HBM = pl.BlockSpec(memory_space=pltpu.HBM)
 SMEM = pl.BlockSpec(memory_space=pltpu.SMEM)
 VMEM = pl.BlockSpec(memory_space=pltpu.VMEM)
 
@@ -159,60 +160,57 @@
     )(lengths, queries, key_cache, value_cache)
 
 
-def place_pieces(spots, where_ref, hid_ref, piece_refs, out_ref, buf, in_sem, out_sem):
+def place_pieces(spots, where_ref, moved_ref, piece_refs, out_ref, buf, hid, in_sem, out_sem):
     rep = where_ref[0]
-    copies, offset = [], 0
-    for i, (_, _, _, _, count) in enumerate(spots):
-        copy = pltpu.make_async_copy(piece_refs[i], buf.at[pl.ds(offset, count)], in_sem.at[i])
-        copy.start()
-        copies.append((copy, offset))
-        offset += count
-    line = hid_ref.shape[1] // (2 * OWNED // COLS)
-    total = jnp.zeros((line, COLS), jnp.float32)
-    writes = []
+    hidden_in = pltpu.make_async_copy(moved_ref.at[:, pl.ds(ROWS, hid.shape[1])], hid, in_sem.at[len(spots)])
+    hidden_in.start()
+    owners, reads, writes, offset = [], [], [], 0
     for i, (dz, dx, dc, first, count) in enumerate(spots):
-        copy, offset = copies[i]
-        copy.wait()
         owner = ((((rep >> 2) + dz) & 3) << 2) | ((rep & 3) ^ (2 * dx + dc))
         start = pl.multiple_of(owner * OWNED + first, ROWS)
+        read = pltpu.make_async_copy(piece_refs[i], buf.at[pl.ds(offset, count)], in_sem.at[i])
         write = pltpu.make_async_copy(
             buf.at[pl.ds(offset, count)], out_ref.at[pl.ds(start, count)], out_sem.at[i]
         )
+        read.start()
+        owners.append(owner)
+        reads.append(read)
+        writes.append(write)
+        offset += count
+    hidden_in.wait()
+    line = hid.shape[1] // (2 * OWNED // COLS)
+    total, offset = jnp.zeros((line, COLS), jnp.float32), 0
+    for owner, read, write, (_, _, _, first, count) in zip(owners, reads, writes, spots):
+        rows = pl.ds(pl.multiple_of((owner & 1) * (OWNED // COLS * line), 16), OWNED // COLS * line)
+        cut = hid[owner >> 1, rows, :].astype(jnp.float32)
+        cut = [cut[c * line : (c + 1) * line] for c in range(first // COLS, (first + count) // COLS)]
+        cut = jnp.concatenate(cut, axis=1).astype(jnp.bfloat16)
+        read.wait()
         write.start()
-        writes.append(write)
-        rows = pl.ds(pl.multiple_of((owner & 1) * (OWNED // COLS * line), 16), OWNED // COLS * line)
-        blocks = hid_ref[owner >> 1, rows, :].astype(jnp.float32)
-        for c in range(0, count, COLS):
-            part = (first + c) // COLS * line
-            total = total + jnp.dot(
-                blocks[part : part + line].astype(jnp.bfloat16),
-                buf[offset + c : offset + c + COLS, :],
-                preferred_element_type=jnp.float32,
-            )
+        total = total + jnp.dot(
+            cut, buf[offset : offset + count, :], preferred_element_type=jnp.float32
+        )
+        offset += count
     return total, writes
 
 
-def early_kernel(spots, follows, where_ref, hid_ref, *refs):
+def early_kernel(spots, follows, where_ref, moved_ref, *refs):
     if follows:
         before_ref, _, *refs = refs
     count = len(spots)
-    out_ref, sum_ref, buf, in_sem, out_sem = refs[count:]
-    total, writes = place_pieces(
-        spots, where_ref, hid_ref, refs[:count], out_ref, buf, in_sem, out_sem
-    )
+    out_ref, sum_ref, *work = refs[count:]
+    total, writes = place_pieces(spots, where_ref, moved_ref, refs[:count], out_ref, *work)
     sum_ref[...] = total + before_ref[...] if follows else total
     for write in writes:
         write.wait()
 
 
-def late_kernel(spots, steps, rows, groups, where_ref, hid_ref, sum_ref, cos_ref, sin_ref, *refs):
+def late_kernel(spots, steps, rows, groups, where_ref, moved_ref, sum_ref, cos_ref, sin_ref, *refs):
     cached = [refs[4 * i : 4 * i + 4] for i in range(len(groups))]
     refs = refs[4 * len(groups) + 1 :]
     count = len(spots)
-    out_ref, kv_ref, att_ref, buf, turn, in_sem, out_sem = refs[count:]
-    total, writes = place_pieces(
-        spots, where_ref, hid_ref, refs[:count], out_ref, buf, in_sem, out_sem
-    )
+    out_ref, kv_ref, att_ref, turn, *work = refs[count:]
+    total, writes = place_pieces(spots, where_ref, moved_ref, refs[:count], out_ref, *work)
     heads = steps * rows * GROUPS
 
     def join(which):
@@ -263,53 +261,60 @@
         write.wait()
 
 
-def scratch(spots):
-    return (
+def scratch(spots, moved):
+    return [
         pltpu.VMEM((sum(s[4] for s in spots), COLS), jnp.bfloat16),
-        [pltpu.SemaphoreType.DMA((len(spots),)), pltpu.SemaphoreType.DMA((len(spots),))],
-    )
-
-
-def place_early(where, hid, before, pieces):
+        pltpu.VMEM((TP, moved.shape[1] - ROWS, COLS), jnp.bfloat16),
+        pltpu.SemaphoreType.DMA((len(spots) + 1,)),
+        pltpu.SemaphoreType.DMA((len(spots),)),
+    ]
+
+
+def place_early(where, moved, before, pieces):
     spots = [p[1:] for p in pieces]
-    buf, sems = scratch(spots)
+    lines = (moved.shape[1] - ROWS) * COLS // (2 * OWNED)
     return pl.pallas_call(
         lambda *refs: early_kernel(spots, bool(before), *refs),
-        in_specs=[SMEM, VMEM] + [VMEM, ANY][: len(before)] + [ANY] * len(pieces),
-        out_specs=[VMEM, ANY][::-1],
+        in_specs=[SMEM, ANY] + [VMEM, ANY][: len(before)] + [HBM] * len(pieces),
+        out_specs=[ANY, VMEM],
         out_shape=[
             jax.ShapeDtypeStruct((REP * OWNED, COLS), jnp.bfloat16),
-            jax.ShapeDtypeStruct((hid.shape[1] * COLS // (2 * OWNED), COLS), jnp.float32),
-        ],
-        scratch_shapes=[buf, *sems],
+            jax.ShapeDtypeStruct((lines, COLS), jnp.float32),
+        ],
+        scratch_shapes=scratch(spots, moved),
         input_output_aliases={3: 0} if before else {},
         compiler_params=pltpu.CompilerParams(vmem_limit_bytes=PLACE_VMEM),
         cost_estimate=PLACE_COST,
-    )(where, hid, *before, *[p[0] for p in pieces])
-
-
-def place_late(where, hid, partial, cosine, sine, cached, placed, pieces, steps, rows, groups):
+    )(where, moved, *before, *[p[0] for p in pieces])
+
+
+def place_late(where, moved, partial, cosine, sine, cached, placed, pieces, steps, rows, groups):
     spots = [p[1:] for p in pieces]
-    buf, sems = scratch(spots)
-    small = 4 + 4 * len(groups)
+    small = 3 + 4 * len(groups)
     return pl.pallas_call(
         lambda *refs: late_kernel(spots, steps, rows, groups, *refs),
-        in_specs=[SMEM] + [VMEM] * small + [ANY] * (1 + len(pieces)),
+        in_specs=[SMEM, ANY] + [VMEM] * small + [ANY] + [HBM] * len(pieces),
         out_specs=[ANY, VMEM, VMEM],
         out_shape=[
             jax.ShapeDtypeStruct((REP * OWNED, COLS), jnp.bfloat16),
             jax.ShapeDtypeStruct((steps, rows, COLS), jnp.bfloat16),
             jax.ShapeDtypeStruct((steps, rows, GROUPS * HD), jnp.bfloat16),
         ],
-        scratch_shapes=[buf, pltpu.VMEM((steps * rows * GROUPS, HD), jnp.float32), *sems],
-        input_output_aliases={1 + small: 0},
+        scratch_shapes=[
+            pltpu.VMEM((steps * rows * GROUPS, HD), jnp.float32),
+            *scratch(spots, moved),
+        ],
+        input_output_aliases={2 + small: 0},
         compiler_params=pltpu.CompilerParams(vmem_limit_bytes=PLACE_VMEM),
         cost_estimate=PLACE_COST,
-    )(where, hid, partial, cosine, sine, *cached, placed, *[p[0] for p in pieces])
-
-
-def after(value, *others):
-    return lax.optimization_barrier((value, *others))[0]
+    )(where, moved, partial, cosine, sine, *cached, placed, *[p[0] for p in pieces])
+
+
+def exchange(pieces, *behind):
+    held = lax.optimization_barrier(tuple(p[0] for p in pieces) + behind)
+    pieces = [(v, *p[1:]) for v, p in zip(held, pieces)]
+    other = [(send(p[0], CORE_SWAP), p[1], p[2], 1, p[4], p[5]) for p in pieces]
+    return (pieces, other, *held[len(pieces) :])
 
 
 def local(kv_master, hidden, queries, key_cache, value_cache, lengths):
@@ -317,46 +322,47 @@
     where = lax.axis_index("rep").astype(jnp.int32).reshape(1)
 
     moved = lax.all_to_all(pack(kv_master, hidden), "tp", split_axis=0, concat_axis=0, tiled=True)
-    owned, hid = moved[:, :ROWS], moved[:, ROWS:]
-    low, high = owned[: TP // 2].reshape(HALF, COLS), owned[TP // 2 :].reshape(HALF, COLS)
+    owned = moved[:, :ROWS]
     cosine, sine = rotation_tables(lengths, steps)
     cached = attend_cache(queries, key_cache, value_cache, lengths, 0, rows)
+    low, high = owned[: TP // 2].reshape(HALF, COLS), owned[TP // 2 :].reshape(HALF, COLS)
     owned, low, high, *cached = lax.optimization_barrier((owned, low, high, *cached))
     owned = owned.reshape(OWNED, COLS)
 
     up, down = z_shift(1), z_shift(-1)
-    near_x = send(owned, X_SWAP)
     low_b, high_a = send(low, up), send(high, down)
     low_a, high_b = send(low, down), send(high, up)
+    near_x = send(owned, X_SWAP)
     low_b, high_a, cosine, sine = lax.optimization_barrier((low_b, high_a, cosine, sine))
+    below_x, above_x = send(near_x, up), send(near_x, down)
     far_low, far_high = send(low_b, up), send(high_a, down)
-    below_x, above_x = send(near_x, up), send(near_x, down)
     far_low_x, far_high_x = send(far_low, X_SWAP), send(far_high, X_SWAP)
 
-    def both(pieces, *first):
-        values = lax.optimization_barrier(tuple(p[0] for p in pieces) + first)
-        pieces = [(v, *p[1:]) for v, p in zip(values, pieces)]
-        return pieces + [(send(p[0], CORE_SWAP), p[1], p[2], 1, p[4], p[5]) for p in pieces]
-
-    pieces = [
+    near = [
         (owned, 0, 0, 0, 0, OWNED),
         (near_x, 0, 1, 0, 0, OWNED),
         (low_b, 3, 0, 0, 0, HALF),
+        (high_a, 1, 0, 0, HALF, HALF),
         (low_a, 1, 0, 0, 0, HALF),
         (high_b, 3, 0, 0, HALF, HALF),
-        (high_a, 1, 0, 0, HALF, HALF),
     ]
-    pieces += [(far_low, 2, 0, 0, 0, HALF), (far_high, 2, 0, 0, HALF, HALF)]
-    placed, partial = place_early(where, hid, [], both(pieces, far_low, far_high))
-    pieces = [
+    far = [(far_low, 2, 0, 0, 0, HALF), (far_high, 2, 0, 0, HALF, HALF)]
+    near, near_other = exchange(near)
+    far, far_other = exchange(far)
+    pieces = near + far + near_other + far_other
+    placed, partial = place_early(where, moved, [], pieces)
+    last = [
         (below_x, 3, 1, 0, 0, OWNED),
         (above_x, 1, 1, 0, 0, OWNED),
         (far_low_x, 2, 1, 0, 0, HALF),
         (far_high_x, 2, 1, 0, HALF, HALF),
     ]
-    pieces = both(pieces, partial)
+    last, last_other, partial = exchange(last, partial)
+    placed, partial = place_early(where, moved, [partial, placed], last)
     return tuple(
-        place_late(where, hid, partial, cosine, sine, cached, placed, pieces, steps, rows, [rows])
+        place_late(
+            where, moved, partial, cosine, sine, cached, placed, last_other, steps, rows, [rows]
+        )
     )
 
 

time: 74.9 us -> 70.5 us (0.941)
  waiting for transfers between devices: 19.1 us -> 12.5 us
  local copies, waits for them, and re-layouts: 1.98 us -> 6.77 us
  Pallas kernels: 22.9 us -> 19.1 us
  starting transfers between devices: 28.3 us -> 30.1 us
    ppermute x23, waiting for transfers between devices: 18.1 us -> 11.6 us  [send(): return lax.ppermute(value, 'rep', pairs)]
    unnamed x38 -> x24, local copies, waits for them, and re-layouts: 1.09 us -> 6.61 us
    pallas_call x1, Pallas kernels: 4.83 us -> 2.57 us  [place_late(): pl.pallas_call(lambda *refs: late_kernel(spots, steps, rows, groups, *ref...]
    ppermute x23, starting transfers between devices: 22.4 us -> 24.2 us  [send(): return lax.ppermute(value, 'rep', pairs)]
    pallas_call x1 -> x2, Pallas kernels: 6.26 us -> 4.74 us  [place_early(): pl.pallas_call(lambda *refs: early_kernel(spots, bool(before), *refs), in...]
  transfers between devices with their start and end apart: 24 -> 24, of which waited for: 12 -> 8; matrix products, arithmetic and copies ran while one was open for 3% -> 1% of each run, Pallas kernels for 21% -> 21%
where the time goes in v2:
time: 70.5 us; the launch traced here: 70.1 us
  starting transfers between devices  30.1 us (43%)
  Pallas kernels  19.1 us (27%)
  waiting for transfers between devices  12.5 us (18%)
  local copies, waits for them, and re-layouts  6.77 us (10%)
  other arithmetic  0.86 us (1%)
  between operations  0.74 us (1%)
    ppermute x23, starting transfers between devices, send(): return lax.ppermute(value, 'rep', pairs)  24.2 us
    ppermute x23, waiting for transfers between devices, send(): return lax.ppermute(value, 'rep', pairs)  11.6 us
    pallas_call x1, Pallas kernels, attend_cache(): pl.pallas_call(lambda *refs: cache_kernel(first, count, *refs), grid=(cou...  9.65 us
    unnamed x24, local copies, waits for them, and re-layouts  6.61 us
    all_to_all x1, starting transfers between devices, local(): lax.all_to_all(pack(kv_master, hidden), 'tp', split_axis=0, concat_axis=0...  5.95 us
    pallas_call x2, Pallas kernels, place_early(): pl.pallas_call(lambda *refs: early_kernel(spots, bool(before), *refs), in...  4.74 us
    pallas_call x1, Pallas kernels, place_late(): pl.pallas_call(lambda *refs: late_kernel(spots, steps, rows, groups, *ref...  2.57 us
    pallas_call x1, Pallas kernels, pack(): pl.pallas_call(pack_kernel, in_specs=[VMEM, VMEM], out_specs=VMEM, out_sh...  2.17 us
  transfers between devices with their start and end apart: 24, of which 8 were waited for; matrix products, arithmetic and copies ran while one was open for 1% of the time, Pallas kernels for 21%

profile of v2, /device:TPU:1, one launch (start us, length us, event | category | flops | bytes accessed | tf_op | source)
XLA Modules:
  0.0 70.1 jit_solution(9527566896037581990)
XLA Ops:
  0.6 2.2 %shard_map.85 = bf16[8,192,256]{2,1,0:T(8,128)(2,1)} custom-call(f32[128,2048]{1,0:T(8,128)} %kv_ref.1, bf16[2,4,2048]{2,1,0:T(4,128)(2,1)} %hid_ref.1), custom_call_target="tpu_custom_call" | custom-call | tf_op jit(solution)/shard_map/pallas_call | solution.py:79
  2.8 5.9 %all-to-all-start = ((bf16[8,192,256]{2,1,0:T(8,128)(2,1)}), bf16[8,192,256]{2,1,0:T(8,128)(2,1)S(1)}, u32[]{:S(2)}, u32[]{:S(2)}) async-start(bf16[8,192,256]{2,1,0:T(8,128)(2,1)} %shard_map.85), calls=%async_computation | async-start | bytes 1572864 | tf_op jit(solution)/shard_map/all_to_all | solution.py:324
  8.8 0.7 add_convert_fusion
  9.4 0.1 convert_element_type.12
  9.5 9.7 %shard_map.86 = (bf16[8,16,128]{2,1,0:T(8,128)(2,1)}, f32[8,16,128]{2,1,0:T(8,128)}, f32[8,16,128]{2,1,0:T(8,128)}, f32[8,16,128]{2,1,0:T(8,128)}) custom-call(s32[4]{0:T(128)} %refs_0_.1, bf16[2,4,2048]{2,1,0:T(4,128)(2,1)} %refs_1_.1, bf16[4,8192,128]{2,1,0:T(8,128)(2,1)} %refs_2_.1, bf16[4,8192,128]{2,1,0:T(8,128)(2,1)} %refs_3_.1), custom_call_target="tpu_custom_call" | custom-call | flops 536870912 | bytes 16777216 | tf_op jit(solution)/shard_map/pallas_call | solution.py:138
  19.2 1.0 %all-to-all-done.refs_1_ = bf16[8,192,256]{2,1,0:T(8,128)(2,1)S(1)} async-done(((bf16[8,192,256]{2,1,0:T(8,128)(2,1)}), bf16[8,192,256]{2,1,0:T(8,128)(2,1)S(1)}, u32[]{:S(2)}, u32[]{:S(2)}) %all-to-all-start) | async-done | bytes 786464 | tf_op jit(solution)/shard_map/all_to_all | solution.py:324
  20.2 1.7 %collective-permute-start.3 = (bf16[512,256]{1,0:T(8,128)(2,1)S(1)}, bf16[512,256]{1,0:T(8,128)(2,1)S(1)}, u32[]{:S(2)}, u32[]{:S(2)}) collective-permute-start(bf16[512,256]{1,0:T(8,128)(2,1)S(1)} %bitcast.9), channel_id=1, source_target_pairs={{0,32},{8,40},{16,48},{24,56},{32,64},{40,72},{48,80},{56,88},{64,... | collective-permute-start | bytes 786440 | tf_op jit(solution)/shard_map/ppermute | solution.py:44
  21.9 2.2 %collective-permute-start.4 = (bf16[512,256]{1,0:T(8,128)(2,1)S(1)}, bf16[512,256]{1,0:T(8,128)(2,1)S(1)}, u32[]{:S(2)}, u32[]{:S(2)}) collective-permute-start(bf16[512,256]{1,0:T(8,128)(2,1)S(1)} %bitcast.7), channel_id=1, source_target_pairs={{0,96},{8,104},{16,112},{24,120},{32,0},{40,8},{48,16},{56,24},{64... | collective-permute-start | bytes 786440 | tf_op jit(solution)/shard_map/ppermute | solution.py:44
  24.1 2.5 %collective-permute-start = (bf16[1024,256]{1,0:T(8,128)(2,1)S(1)}, bf16[1024,256]{1,0:T(8,128)(2,1)S(1)}, u32[]{:S(2)}, u32[]{:S(2)}) collective-permute-start(bf16[1024,256]{1,0:T(8,128)(2,1)S(1)} %bitcast.4), channel_id=1, source_target_pairs={{0,16},{8,24},{16,0},{24,8},{32,48},{40,56},{48,32},{56,40},{64,80... | collective-permute-start | bytes 1572872 | tf_op jit(solution)/shard_map/ppermute | solution.py:44
  26.6 0.1 fusion
  26.7 1.5 %collective-permute-start.9 = (bf16[512,256]{1,0:T(8,128)(2,1)S(1)}, bf16[512,256]{1,0:T(8,128)(2,1)S(1)}, u32[]{:S(2)}, u32[]{:S(2)}) collective-permute-start(bf16[512,256]{1,0:T(8,128)(2,1)S(1)} %bitcast.10), channel_id=1, source_target_pairs={{0,96},{8,104},{16,112},{24,120},{32,0},{40,8},{48,16},{56,24},{64... | collective-permute-start | bytes 786440 | tf_op jit(solution)/shard_map/ppermute | solution.py:44
  28.1 0.1 collective-permute-start.10
  28.2 0.1 pad_maximum_fusion
  28.3 0.8 %collective-permute-done.3.refs_4_ = bf16[512,256]{1,0:T(8,128)(2,1)S(1)} collective-permute-done((bf16[512,256]{1,0:T(8,128)(2,1)S(1)}, bf16[512,256]{1,0:T(8,128)(2,1)S(1)}, u32[]{:S(2)}, u32[]{:S(2)}) %collective-permute-start.3) | collective-permute-done | bytes 262176 | tf_op jit(solution)/shard_map/ppermute | solution.py:44
  29.1 0.4 collective-permute-start.5
  29.5 2.3 %collective-permute-start.7 = (bf16[512,256]{1,0:T(8,128)(2,1)S(1)}, bf16[512,256]{1,0:T(8,128)(2,1)}, u32[]{:S(2)}, u32[]{:S(2)}) collective-permute-start(bf16[512,256]{1,0:T(8,128)(2,1)S(1)} %collective-permute-done.4.refs_5_), channel_id=1, source_target_pairs={{0,96},{8,104},{16,112},{24,120},{32,0},{40,8},{48,16},{56,24},{64... | collective-permute-start | bytes 786440 | tf_op jit(solution)/shard_map/ppermute | solution.py:44
  31.8 2.6 %collective-permute-done.9.refs_6_ = bf16[512,256]{1,0:T(8,128)(2,1)S(1)} collective-permute-done((bf16[512,256]{1,0:T(8,128)(2,1)S(1)}, bf16[512,256]{1,0:T(8,128)(2,1)S(1)}, u32[]{:S(2)}, u32[]{:S(2)}) %collective-permute-start.9) | collective-permute-done | bytes 262176 | tf_op jit(solution)/shard_map/ppermute | solution.py:44
  34.4 0.5 collective-permute-done.10.refs_7_
  34.9 2.3 %collective-permute-done.refs_3_ = bf16[1024,256]{1,0:T(8,128)(2,1)S(1)} collective-permute-done((bf16[1024,256]{1,0:T(8,128)(2,1)S(1)}, bf16[1024,256]{1,0:T(8,128)(2,1)S(1)}, u32[]{:S(2)}, u32[]{:S(2)}) %collective-permute-start) | collective-permute-done | bytes 524320 | tf_op jit(solution)/shard_map/ppermute | solution.py:44
  37.2 3.8 %collective-permute-start.13 = (bf16[512,256]{1,0:T(8,128)(2,1)S(1)}, bf16[512,256]{1,0:T(8,128)(2,1)S(1)}, u32[]{:S(2)}, u32[]{:S(2)}) collective-permute-start(bf16[512,256]{1,0:T(8,128)(2,1)S(1)} %collective-permute-done.3.refs_4_), channel_id=1, source_target_pairs={{0,8},{8,0},{16,24},{24,16},{32,40},{40,32},{48,56},{56,48},{64,72... | collective-permute-start | bytes 786440 | tf_op jit(solution)/shard_map/ppermute | solution.py:44
  41.0 0.5 collective-permute-start.15
  41.5 0.7 copy-done
  42.2 1.6 %collective-permute-start.11 = (bf16[1024,256]{1,0:T(8,128)(2,1)S(1)}, bf16[1024,256]{1,0:T(8,128)(2,1)S(1)}, u32[]{:S(2)}, u32[]{:S(2)}) collective-permute-start(bf16[1024,256]{1,0:T(8,128)(2,1)S(1)} %bitcast.5), channel_id=1, source_target_pairs={{0,8},{8,0},{16,24},{24,16},{32,40},{40,32},{48,56},{56,48},{64,72... | collective-permute-start | bytes 1572872 | tf_op jit(solution)/shard_map/ppermute | solution.py:44
  43.8 0.7 copy-done.2
  44.5 0.5 collective-permute-start.16
  45.0 0.7 %copy-done.4 = bf16[512,256]{1,0:T(8,128)(2,1)} copy-done((bf16[512,256]{1,0:T(8,128)(2,1)}, bf16[512,256]{1,0:T(8,128)(2,1)S(1)}, u32[]{:S(2)}) %copy-start.4) | copy-done | bytes 262168
  45.7 0.0 collective-permute-start.17
  45.7 0.7 copy-done.6
  46.4 0.5 collective-permute-start.18
  46.9 1.1 %collective-permute-start.2 = (bf16[1024,256]{1,0:T(8,128)(2,1)S(1)}, bf16[1024,256]{1,0:T(8,128)(2,1)S(1)}, u32[]{:S(2)}, u32[]{:S(2)}) collective-permute-start(bf16[1024,256]{1,0:T(8,128)(2,1)S(1)} %collective-permute-done.refs_3_), channel_id=1, source_target_pairs={{0,96},{8,104},{16,112},{24,120},{32,0},{40,8},{48,16},{56,24},{64... | collective-permute-start | bytes 1572872 | tf_op jit(solution)/shard_map/ppermute | solution.py:44
  48.0 0.4 collective-permute-start.1
  48.4 0.0 collective-permute-done.18.refs_17_
  48.4 2.1 %collective-permute-start.6 = (bf16[512,256]{1,0:T(8,128)(2,1)}, bf16[512,256]{1,0:T(8,128)(2,1)S(1)}, u32[]{:S(2)}, u32[]{:S(2)}) collective-permute-start(bf16[512,256]{1,0:T(8,128)(2,1)} %collective-permute-done.5.refs_8_), channel_id=1, source_target_pairs={{0,16},{8,24},{16,0},{24,8},{32,48},{40,56},{48,32},{56,40},{64,80... | collective-permute-start | bytes 786440 | tf_op jit(solution)/shard_map/ppermute | solution.py:44
  50.6 0.8 %collective-permute-start.8 = (bf16[512,256]{1,0:T(8,128)(2,1)}, bf16[512,256]{1,0:T(8,128)(2,1)S(1)}, u32[]{:S(2)}, u32[]{:S(2)}) collective-permute-start(bf16[512,256]{1,0:T(8,128)(2,1)} %collective-permute-done.7.refs_9_), channel_id=1, source_target_pairs={{0,16},{8,24},{16,0},{24,8},{32,48},{40,56},{48,32},{56,40},{64,80... | collective-permute-start | bytes 786440 | tf_op jit(solution)/shard_map/ppermute | solution.py:44
  51.4 0.9 %copy-done.1 = bf16[512,256]{1,0:T(8,128)(2,1)S(1)} copy-done((bf16[512,256]{1,0:T(8,128)(2,1)S(1)}, bf16[512,256]{1,0:T(8,128)(2,1)}, u32[]{:S(2)}) %copy-start.1) | copy-done | bytes 262168
  52.4 0.9 %copy-done.3 = bf16[512,256]{1,0:T(8,128)(2,1)S(1)} copy-done((bf16[512,256]{1,0:T(8,128)(2,1)S(1)}, bf16[512,256]{1,0:T(8,128)(2,1)}, u32[]{:S(2)}) %copy-start.3) | copy-done | bytes 262168
  53.3 0.9 %copy-done.5 = bf16[512,256]{1,0:T(8,128)(2,1)S(1)} copy-done((bf16[512,256]{1,0:T(8,128)(2,1)S(1)}, bf16[512,256]{1,0:T(8,128)(2,1)}, u32[]{:S(2)}) %copy-start.5) | copy-done | bytes 262168
  54.3 0.9 %copy-done.7 = bf16[512,256]{1,0:T(8,128)(2,1)S(1)} copy-done((bf16[512,256]{1,0:T(8,128)(2,1)S(1)}, bf16[512,256]{1,0:T(8,128)(2,1)}, u32[]{:S(2)}) %copy-start.7) | copy-done | bytes 262168
  55.2 3.4 %shard_map.87 = (bf16[16384,256]{1,0:T(8,128)(2,1)}, f32[8,256]{1,0:T(8,128)S(1)}) custom-call(s32[1]{0:T(128)} %bitcast.refs_0_, bf16[8,192,256]{2,1,0:T(8,128)(2,1)S(1)} %all-to-all-done.refs_1_, bf16[1024,256]{1,0:T(8,128)(2,1)S(1)} %bitcast.6, bf16[1024,256]{1,0:T(8,128)(2,1)S(1)} %collective-permute-done.refs_3_, ...), custom_call_target="tpu_custom_call" | custom-call | flops 20000000000 | bytes 1000 | tf_op jit(solution)/shard_map/pallas_call | solution.py:276
  58.6 4.2 %collective-permute-done.8.refs_7_ = bf16[512,256]{1,0:T(8,128)(2,1)S(1)} collective-permute-done((bf16[512,256]{1,0:T(8,128)(2,1)}, bf16[512,256]{1,0:T(8,128)(2,1)S(1)}, u32[]{:S(2)}, u32[]{:S(2)}) %collective-permute-start.8) | collective-permute-done | bytes 262176 | tf_op jit(solution)/shard_map/ppermute | solution.py:44
  62.9 1.7 %collective-permute-start.21 = (bf16[512,256]{1,0:T(8,128)(2,1)S(1)}, bf16[512,256]{1,0:T(8,128)(2,1)S(1)}, u32[]{:S(2)}, u32[]{:S(2)}) collective-permute-start(bf16[512,256]{1,0:T(8,128)(2,1)S(1)} %collective-permute-done.6.refs_6_), channel_id=1, source_target_pairs={{0,8},{8,0},{16,24},{24,16},{32,40},{40,32},{48,56},{56,48},{64,72... | collective-permute-start | bytes 786440 | tf_op jit(solution)/shard_map/ppermute | solution.py:44
  64.5 0.1 collective-permute-start.22
  64.6 0.4 collective-permute-start.19
  65.0 0.1 collective-permute-start.20
  65.1 1.4 %shard_map.88 = (bf16[16384,256]{1,0:T(8,128)(2,1)}, f32[8,256]{1,0:T(8,128)S(1)}) custom-call(s32[1]{0:T(128)} %bitcast.refs_0_, bf16[8,192,256]{2,1,0:T(8,128)(2,1)S(1)} %all-to-all-done.refs_1_, f32[8,256]{1,0:T(8,128)S(1)} %get-tuple-element.53.refs_2_, bf16[16384,256]{1,0:T(8,128)(2,1)} %get-tuple-element.54.refs_3_, ...), custom_call_target="tpu_custom_call", output_to_operand_aliasing={{0}: (3, {})} | custom-call | flops 20000000000 | bytes 1000 | tf_op jit(solution)/shard_map/pallas_call | solution.py:276
  66.5 0.3 collective-permute-done.19.refs_10_
  66.8 0.7 %collective-permute-done.20.refs_11_ = bf16[1024,256]{1,0:T(8,128)(2,1)S(1)} collective-permute-done((bf16[1024,256]{1,0:T(8,128)(2,1)S(1)}, bf16[1024,256]{1,0:T(8,128)(2,1)S(1)}, u32[]{:S(2)}, u32[]{:S(2)}) %collective-permute-start.20) | collective-permute-done | bytes 524320 | tf_op jit(solution)/shard_map/ppermute | solution.py:44
  67.6 2.6 %shard_map.89 = (bf16[16384,256]{1,0:T(8,128)(2,1)}, bf16[2,4,256]{2,1,0:T(4,128)(2,1)}, bf16[2,4,2048]{2,1,0:T(4,128)(2,1)}) custom-call(s32[1]{0:T(128)} %bitcast.refs_0_, bf16[8,192,256]{2,1,0:T(8,128)(2,1)S(1)} %all-to-all-done.refs_1_, f32[8,256]{1,0:T(8,128)S(1)} %get-tuple-element.59.refs_2_, ...), custom_call_target="tpu_custom_call", output_to_operand_aliasing={{0}: (9, {})} | custom-call | flops 20000000000 | bytes 1000 | tf_op jit(solution)/shard_map/pallas_call | solution.py:294
  (36 shorter events, 0.2 us)
Async XLA Ops:
  2.8 17.3 %all-to-all-start = ((bf16[8,192,256]{2,1,0:T(8,128)(2,1)}), bf16[8,192,256]{2,1,0:T(8,128)(2,1)S(1)}, u32[]{:S(2)}, u32[]{:S(2)}) async-start(bf16[8,192,256]{2,1,0:T(8,128)(2,1)} %shard_map.85), calls=%async_computation | async-start | bytes 1572864 | tf_op jit(solution)/shard_map/all_to_all | solution.py:324
  20.2 8.9 %collective-permute-start.3 = (bf16[512,256]{1,0:T(8,128)(2,1)S(1)}, bf16[512,256]{1,0:T(8,128)(2,1)S(1)}, u32[]{:S(2)}, u32[]{:S(2)}) collective-permute-start(bf16[512,256]{1,0:T(8,128)(2,1)S(1)} %bitcast.9), channel_id=1, source_target_pairs={{0,32},{8,40},{16,48},{24,56},{32,64},{40,72},{48,80},{56,88},{64,... | collective-permute-start | bytes 786440 | tf_op jit(solution)/shard_map/ppermute | solution.py:44
  21.9 7.2 %collective-permute-start.4 = (bf16[512,256]{1,0:T(8,128)(2,1)S(1)}, bf16[512,256]{1,0:T(8,128)(2,1)S(1)}, u32[]{:S(2)}, u32[]{:S(2)}) collective-permute-start(bf16[512,256]{1,0:T(8,128)(2,1)S(1)} %bitcast.7), channel_id=1, source_target_pairs={{0,96},{8,104},{16,112},{24,120},{32,0},{40,8},{48,16},{56,24},{64... | collective-permute-start | bytes 786440 | tf_op jit(solution)/shard_map/ppermute | solution.py:44
  24.1 13.1 %collective-permute-start = (bf16[1024,256]{1,0:T(8,128)(2,1)S(1)}, bf16[1024,256]{1,0:T(8,128)(2,1)S(1)}, u32[]{:S(2)}, u32[]{:S(2)}) collective-permute-start(bf16[1024,256]{1,0:T(8,128)(2,1)S(1)} %bitcast.4), channel_id=1, source_target_pairs={{0,16},{8,24},{16,0},{24,8},{32,48},{40,56},{48,32},{56,40},{64,80... | collective-permute-start | bytes 1572872 | tf_op jit(solution)/shard_map/ppermute | solution.py:44
  26.7 7.7 %collective-permute-start.9 = (bf16[512,256]{1,0:T(8,128)(2,1)S(1)}, bf16[512,256]{1,0:T(8,128)(2,1)S(1)}, u32[]{:S(2)}, u32[]{:S(2)}) collective-permute-start(bf16[512,256]{1,0:T(8,128)(2,1)S(1)} %bitcast.10), channel_id=1, source_target_pairs={{0,96},{8,104},{16,112},{24,120},{32,0},{40,8},{48,16},{56,24},{64... | collective-permute-start | bytes 786440 | tf_op jit(solution)/shard_map/ppermute | solution.py:44
  28.1 6.7 %collective-permute-start.10 = (bf16[512,256]{1,0:T(8,128)(2,1)S(1)}, bf16[512,256]{1,0:T(8,128)(2,1)}, u32[]{:S(2)}, u32[]{:S(2)}) collective-permute-start(bf16[512,256]{1,0:T(8,128)(2,1)S(1)} %bitcast.8), channel_id=1, source_target_pairs={{0,32},{8,40},{16,48},{24,56},{32,64},{40,72},{48,80},{56,88},{64,... | collective-permute-start | bytes 786440 | tf_op jit(solution)/shard_map/ppermute | solution.py:44
  29.1 13.1 %collective-permute-start.5 = (bf16[512,256]{1,0:T(8,128)(2,1)S(1)}, bf16[512,256]{1,0:T(8,128)(2,1)}, u32[]{:S(2)}, u32[]{:S(2)}) collective-permute-start(bf16[512,256]{1,0:T(8,128)(2,1)S(1)} %collective-permute-done.3.refs_4_), channel_id=1, source_target_pairs={{0,32},{8,40},{16,48},{24,56},{32,64},{40,72},{48,80},{56,88},{64,... | collective-permute-start | bytes 786440 | tf_op jit(solution)/shard_map/ppermute | solution.py:44
  29.5 14.3 %collective-permute-start.7 = (bf16[512,256]{1,0:T(8,128)(2,1)S(1)}, bf16[512,256]{1,0:T(8,128)(2,1)}, u32[]{:S(2)}, u32[]{:S(2)}) collective-permute-start(bf16[512,256]{1,0:T(8,128)(2,1)S(1)} %collective-permute-done.4.refs_5_), channel_id=1, source_target_pairs={{0,96},{8,104},{16,112},{24,120},{32,0},{40,8},{48,16},{56,24},{64... | collective-permute-start | bytes 786440 | tf_op jit(solution)/shard_map/ppermute | solution.py:44
  37.2 6.6 %collective-permute-start.13 = (bf16[512,256]{1,0:T(8,128)(2,1)S(1)}, bf16[512,256]{1,0:T(8,128)(2,1)S(1)}, u32[]{:S(2)}, u32[]{:S(2)}) collective-permute-start(bf16[512,256]{1,0:T(8,128)(2,1)S(1)} %collective-permute-done.3.refs_4_), channel_id=1, source_target_pairs={{0,8},{8,0},{16,24},{24,16},{32,40},{40,32},{48,56},{56,48},{64,72... | collective-permute-start | bytes 786440 | tf_op jit(solution)/shard_map/ppermute | solution.py:44
  41.0 4.0 %collective-permute-start.14 = (bf16[512,256]{1,0:T(8,128)(2,1)S(1)}, bf16[512,256]{1,0:T(8,128)(2,1)S(1)}, u32[]{:S(2)}, u32[]{:S(2)}) collective-permute-start(bf16[512,256]{1,0:T(8,128)(2,1)S(1)} %collective-permute-done.4.refs_5_), channel_id=1, source_target_pairs={{0,8},{8,0},{16,24},{24,16},{32,40},{40,32},{48,56},{56,48},{64,72... | collective-permute-start | bytes 786440 | tf_op jit(solution)/shard_map/ppermute | solution.py:44
  41.0 4.7 %collective-permute-start.15 = (bf16[512,256]{1,0:T(8,128)(2,1)S(1)}, bf16[512,256]{1,0:T(8,128)(2,1)S(1)}, u32[]{:S(2)}, u32[]{:S(2)}) collective-permute-start(bf16[512,256]{1,0:T(8,128)(2,1)S(1)} %collective-permute-done.9.refs_6_), channel_id=1, source_target_pairs={{0,8},{8,0},{16,24},{24,16},{32,40},{40,32},{48,56},{56,48},{64,72... | collective-permute-start | bytes 786440 | tf_op jit(solution)/shard_map/ppermute | solution.py:44
  41.5 0.7 %copy-start = (bf16[512,256]{1,0:T(8,128)(2,1)}, bf16[512,256]{1,0:T(8,128)(2,1)S(1)}, u32[]{:S(2)}) copy-start(bf16[512,256]{1,0:T(8,128)(2,1)S(1)} %collective-permute-done.9.refs_6_) | copy-start | bytes 786436
  42.2 8.4 %collective-permute-start.11 = (bf16[1024,256]{1,0:T(8,128)(2,1)S(1)}, bf16[1024,256]{1,0:T(8,128)(2,1)S(1)}, u32[]{:S(2)}, u32[]{:S(2)}) collective-permute-start(bf16[1024,256]{1,0:T(8,128)(2,1)S(1)} %bitcast.5), channel_id=1, source_target_pairs={{0,8},{8,0},{16,24},{24,16},{32,40},{40,32},{48,56},{56,48},{64,72... | collective-permute-start | bytes 1572872 | tf_op jit(solution)/shard_map/ppermute | solution.py:44
  43.8 7.6 %collective-permute-start.12 = (bf16[1024,256]{1,0:T(8,128)(2,1)S(1)}, bf16[1024,256]{1,0:T(8,128)(2,1)S(1)}, u32[]{:S(2)}, u32[]{:S(2)}) collective-permute-start(bf16[1024,256]{1,0:T(8,128)(2,1)S(1)} %collective-permute-done.refs_3_), channel_id=1, source_target_pairs={{0,8},{8,0},{16,24},{24,16},{32,40},{40,32},{48,56},{56,48},{64,72... | collective-permute-start | bytes 1572872 | tf_op jit(solution)/shard_map/ppermute | solution.py:44
  43.8 0.7 copy-start.2
  44.5 2.4 %collective-permute-start.16 = (bf16[512,256]{1,0:T(8,128)(2,1)}, bf16[512,256]{1,0:T(8,128)(2,1)}, u32[]{:S(2)}, u32[]{:S(2)}) collective-permute-start(bf16[512,256]{1,0:T(8,128)(2,1)} %collective-permute-done.10.refs_7_), channel_id=1, source_target_pairs={{0,8},{8,0},{16,24},{24,16},{32,40},{40,32},{48,56},{56,48},{64,72... | collective-permute-start | bytes 786440 | tf_op jit(solution)/shard_map/ppermute | solution.py:44
  45.0 0.7 %copy-start.4 = (bf16[512,256]{1,0:T(8,128)(2,1)}, bf16[512,256]{1,0:T(8,128)(2,1)S(1)}, u32[]{:S(2)}) copy-start(bf16[512,256]{1,0:T(8,128)(2,1)S(1)} %collective-permute-done.14.refs_13_) | copy-start | bytes 786436
  45.7 2.3 %collective-permute-start.17 = (bf16[512,256]{1,0:T(8,128)(2,1)}, bf16[512,256]{1,0:T(8,128)(2,1)}, u32[]{:S(2)}, u32[]{:S(2)}) collective-permute-start(bf16[512,256]{1,0:T(8,128)(2,1)} %collective-permute-done.5.refs_8_), channel_id=1, source_target_pairs={{0,8},{8,0},{16,24},{24,16},{32,40},{40,32},{48,56},{56,48},{64,72... | collective-permute-start | bytes 786440 | tf_op jit(solution)/shard_map/ppermute | solution.py:44
  45.7 0.7 copy-start.6
  46.4 2.0 %collective-permute-start.18 = (bf16[512,256]{1,0:T(8,128)(2,1)}, bf16[512,256]{1,0:T(8,128)(2,1)}, u32[]{:S(2)}, u32[]{:S(2)}) collective-permute-start(bf16[512,256]{1,0:T(8,128)(2,1)} %collective-permute-done.7.refs_9_), channel_id=1, source_target_pairs={{0,8},{8,0},{16,24},{24,16},{32,40},{40,32},{48,56},{56,48},{64,72... | collective-permute-start | bytes 786440 | tf_op jit(solution)/shard_map/ppermute | solution.py:44
  46.9 15.9 %collective-permute-start.2 = (bf16[1024,256]{1,0:T(8,128)(2,1)S(1)}, bf16[1024,256]{1,0:T(8,128)(2,1)S(1)}, u32[]{:S(2)}, u32[]{:S(2)}) collective-permute-start(bf16[1024,256]{1,0:T(8,128)(2,1)S(1)} %collective-permute-done.refs_3_), channel_id=1, source_target_pairs={{0,96},{8,104},{16,112},{24,120},{32,0},{40,8},{48,16},{56,24},{64... | collective-permute-start | bytes 1572872 | tf_op jit(solution)/shard_map/ppermute | solution.py:44
  48.0 14.8 %collective-permute-start.1 = (bf16[1024,256]{1,0:T(8,128)(2,1)S(1)}, bf16[1024,256]{1,0:T(8,128)(2,1)S(1)}, u32[]{:S(2)}, u32[]{:S(2)}) collective-permute-start(bf16[1024,256]{1,0:T(8,128)(2,1)S(1)} %collective-permute-done.refs_3_), channel_id=1, source_target_pairs={{0,32},{8,40},{16,48},{24,56},{32,64},{40,72},{48,80},{56,88},{64,... | collective-permute-start | bytes 1572872 | tf_op jit(solution)/shard_map/ppermute | solution.py:44
  48.4 10.2 %collective-permute-start.6 = (bf16[512,256]{1,0:T(8,128)(2,1)}, bf16[512,256]{1,0:T(8,128)(2,1)S(1)}, u32[]{:S(2)}, u32[]{:S(2)}) collective-permute-start(bf16[512,256]{1,0:T(8,128)(2,1)} %collective-permute-done.5.refs_8_), channel_id=1, source_target_pairs={{0,16},{8,24},{16,0},{24,8},{32,48},{40,56},{48,32},{56,40},{64,80... | collective-permute-start | bytes 786440 | tf_op jit(solution)/shard_map/ppermute | solution.py:44
  50.6 12.3 %collective-permute-start.8 = (bf16[512,256]{1,0:T(8,128)(2,1)}, bf16[512,256]{1,0:T(8,128)(2,1)S(1)}, u32[]{:S(2)}, u32[]{:S(2)}) collective-permute-start(bf16[512,256]{1,0:T(8,128)(2,1)} %collective-permute-done.7.refs_9_), channel_id=1, source_target_pairs={{0,16},{8,24},{16,0},{24,8},{32,48},{40,56},{48,32},{56,40},{64,80... | collective-permute-start | bytes 786440 | tf_op jit(solution)/shard_map/ppermute | solution.py:44
  51.4 1.0 %copy-start.1 = (bf16[512,256]{1,0:T(8,128)(2,1)S(1)}, bf16[512,256]{1,0:T(8,128)(2,1)}, u32[]{:S(2)}) copy-start(bf16[512,256]{1,0:T(8,128)(2,1)} %copy-done) | copy-start | bytes 786436
  52.4 0.9 %copy-start.3 = (bf16[512,256]{1,0:T(8,128)(2,1)S(1)}, bf16[512,256]{1,0:T(8,128)(2,1)}, u32[]{:S(2)}) copy-start(bf16[512,256]{1,0:T(8,128)(2,1)} %copy-done.2) | copy-start | bytes 786436
  53.3 0.9 %copy-start.5 = (bf16[512,256]{1,0:T(8,128)(2,1)S(1)}, bf16[512,256]{1,0:T(8,128)(2,1)}, u32[]{:S(2)}) copy-start(bf16[512,256]{1,0:T(8,128)(2,1)} %copy-done.4) | copy-start | bytes 786436
  54.3 0.9 %copy-start.7 = (bf16[512,256]{1,0:T(8,128)(2,1)S(1)}, bf16[512,256]{1,0:T(8,128)(2,1)}, u32[]{:S(2)}) copy-start(bf16[512,256]{1,0:T(8,128)(2,1)} %copy-done.6) | copy-start | bytes 786436
  62.9 3.6 %collective-permute-start.21 = (bf16[512,256]{1,0:T(8,128)(2,1)S(1)}, bf16[512,256]{1,0:T(8,128)(2,1)S(1)}, u32[]{:S(2)}, u32[]{:S(2)}) collective-permute-start(bf16[512,256]{1,0:T(8,128)(2,1)S(1)} %collective-permute-done.6.refs_6_), channel_id=1, source_target_pairs={{0,8},{8,0},{16,24},{24,16},{32,40},{40,32},{48,56},{56,48},{64,72... | collective-permute-start | bytes 786440 | tf_op jit(solution)/shard_map/ppermute | solution.py:44
  64.5 2.0 %collective-permute-start.22 = (bf16[512,256]{1,0:T(8,128)(2,1)S(1)}, bf16[512,256]{1,0:T(8,128)(2,1)S(1)}, u32[]{:S(2)}, u32[]{:S(2)}) collective-permute-start(bf16[512,256]{1,0:T(8,128)(2,1)S(1)} %collective-permute-done.8.refs_7_), channel_id=1, source_target_pairs={{0,8},{8,0},{16,24},{24,16},{32,40},{40,32},{48,56},{56,48},{64,72... | collective-permute-start | bytes 786440 | tf_op jit(solution)/shard_map/ppermute | solution.py:44
  64.6 2.2 %collective-permute-start.19 = (bf16[1024,256]{1,0:T(8,128)(2,1)S(1)}, bf16[1024,256]{1,0:T(8,128)(2,1)S(1)}, u32[]{:S(2)}, u32[]{:S(2)}) collective-permute-start(bf16[1024,256]{1,0:T(8,128)(2,1)S(1)} %collective-permute-done.1.refs_4_), channel_id=1, source_target_pairs={{0,8},{8,0},{16,24},{24,16},{32,40},{40,32},{48,56},{56,48},{64,72... | collective-permute-start | bytes 1572872 | tf_op jit(solution)/shard_map/ppermute | solution.py:44
  65.0 2.5 %collective-permute-start.20 = (bf16[1024,256]{1,0:T(8,128)(2,1)S(1)}, bf16[1024,256]{1,0:T(8,128)(2,1)S(1)}, u32[]{:S(2)}, u32[]{:S(2)}) collective-permute-start(bf16[1024,256]{1,0:T(8,128)(2,1)S(1)} %collective-permute-done.2.refs_5_), channel_id=1, source_target_pairs={{0,8},{8,0},{16,24},{24,16},{32,40},{40,32},{48,56},{56,48},{64,72... | collective-permute-start | bytes 1572872 | tf_op jit(solution)/shard_map/ppermute | solution.py:44
  65.1 2.4 %copy-start.8 = (f32[8,16,128]{2,1,0:T(8,128)S(1)}, f32[8,16,128]{2,1,0:T(8,128)}, u32[]{:S(2)}) copy-start(f32[8,16,128]{2,1,0:T(8,128)} %get-tuple-element.63.refs_6_) | copy-start | bytes 196612
  65.1 2.4 %copy-start.9 = (f32[8,16,128]{2,1,0:T(8,128)S(1)}, f32[8,16,128]{2,1,0:T(8,128)}, u32[]{:S(2)}) copy-start(f32[8,16,128]{2,1,0:T(8,128)} %get-tuple-element.64.refs_7_) | copy-start | bytes 196612
  65.1 2.4 %copy-start.10 = (f32[8,16,128]{2,1,0:T(8,128)S(1)}, f32[8,16,128]{2,1,0:T(8,128)}, u32[]{:S(2)}) copy-start(f32[8,16,128]{2,1,0:T(8,128)} %get-tuple-element.65.refs_8_) | copy-start | bytes 196612
  65.1 2.4 %copy-start.11 = (bf16[8,16,128]{2,1,0:T(8,128)(2,1)S(1)}, bf16[8,16,128]{2,1,0:T(8,128)(2,1)}, u32[]{:S(2)}) copy-start(bf16[8,16,128]{2,1,0:T(8,128)(2,1)} %get-tuple-element.62.refs_5_) | copy-start | bytes 98308

commit v3 on v2

--- a/solution.py
+++ b/solution.py
@@ -160,7 +160,7 @@
     )(lengths, queries, key_cache, value_cache)
 
 
-def place_pieces(spots, where_ref, moved_ref, piece_refs, out_ref, buf, hid, in_sem, out_sem):
+def place_pieces(spots, where_ref, moved_ref, piece_refs, out_ref, buf, hid, in_sem, out_sem, meanwhile=tuple):
     rep = where_ref[0]
     hidden_in = pltpu.make_async_copy(moved_ref.at[:, pl.ds(ROWS, hid.shape[1])], hid, in_sem.at[len(spots)])
     hidden_in.start()
@@ -177,6 +177,7 @@
         reads.append(read)
         writes.append(write)
         offset += count
+    ready = meanwhile()
     hidden_in.wait()
     line = hid.shape[1] // (2 * OWNED // COLS)
     total, offset = jnp.zeros((line, COLS), jnp.float32), 0
@@ -191,7 +192,7 @@
             cut, buf[offset : offset + count, :], preferred_element_type=jnp.float32
         )
         offset += count
-    return total, writes
+    return total, writes, ready
 
 
 def early_kernel(spots, follows, where_ref, moved_ref, *refs):
@@ -199,7 +200,7 @@
         before_ref, _, *refs = refs
     count = len(spots)
     out_ref, sum_ref, *work = refs[count:]
-    total, writes = place_pieces(spots, where_ref, moved_ref, refs[:count], out_ref, *work)
+    total, writes, _ = place_pieces(spots, where_ref, moved_ref, refs[:count], out_ref, *work)
     sum_ref[...] = total + before_ref[...] if follows else total
     for write in writes:
         write.wait()
@@ -210,7 +211,6 @@
     refs = refs[4 * len(groups) + 1 :]
     count = len(spots)
     out_ref, kv_ref, att_ref, turn, *work = refs[count:]
-    total, writes = place_pieces(spots, where_ref, moved_ref, refs[:count], out_ref, *work)
     heads = steps * rows * GROUPS
 
     def join(which):
@@ -223,10 +223,16 @@
             axis=0,
         )
 
-    acc, old_top, old_total = join(1), join(2)[:, :1], join(3)[:, :1]
-    total = total + sum_ref[...]
+    def meanwhile():
+        return join(1), join(2)[:, :1], join(3)[:, :1], sum_ref[...], cos_ref[...], sin_ref[...]
+
+    total, writes, ready = place_pieces(
+        spots, where_ref, moved_ref, refs[:count], out_ref, *work, meanwhile
+    )
+    acc, old_top, old_total, before, cosine, sine = ready
+    total = total + before
     keys = total[:, :HD]
-    keys = keys * cos_ref[...] + pltpu.roll(keys, HD // 2, 1) * sin_ref[...]
+    keys = keys * cosine + pltpu.roll(keys, HD // 2, 1) * sine
     keys = keys.astype(jnp.bfloat16)
     values = total[:, HD:].astype(jnp.bfloat16)
     for s in range(steps):
@@ -330,8 +336,8 @@
     owned = owned.reshape(OWNED, COLS)
 
     up, down = z_shift(1), z_shift(-1)
+    low_a, high_b = send(low, down), send(high, up)
     low_b, high_a = send(low, up), send(high, down)
-    low_a, high_b = send(low, down), send(high, up)
     near_x = send(owned, X_SWAP)
     low_b, high_a, cosine, sine = lax.optimization_barrier((low_b, high_a, cosine, sine))
     below_x, above_x = send(near_x, up), send(near_x, down)

time: 70.5 us -> 70.1 us (level)
  no operation moved by 1% of the time
where the time goes in v3:
time: 70.1 us; the launch traced here: 69.7 us
  starting transfers between devices  30.1 us (43%)
  Pallas kernels  18.7 us (27%)
  waiting for transfers between devices  12.5 us (18%)
  local copies, waits for them, and re-layouts  6.77 us (10%)
  other arithmetic  0.86 us (1%)
  between operations  0.74 us (1%)
    ppermute x23, starting transfers between devices, send(): return lax.ppermute(value, 'rep', pairs)  24.2 us
    ppermute x23, waiting for transfers between devices, send(): return lax.ppermute(value, 'rep', pairs)  11.6 us
    pallas_call x1, Pallas kernels, attend_cache(): pl.pallas_call(lambda *refs: cache_kernel(first, count, *refs), grid=(cou...  9.65 us
    unnamed x24, local copies, waits for them, and re-layouts  6.61 us
    all_to_all x1, starting transfers between devices, local(): lax.all_to_all(pack(kv_master, hidden), 'tp', split_axis=0, concat_axis=0...  5.95 us
    pallas_call x2, Pallas kernels, place_early(): pl.pallas_call(lambda *refs: early_kernel(spots, bool(before), *refs), in...  4.74 us
    pallas_call x1, Pallas kernels, pack(): pl.pallas_call(pack_kernel, in_specs=[VMEM, VMEM], out_specs=VMEM, out_sh...  2.17 us
    pallas_call x1, Pallas kernels, place_late(): pl.pallas_call(lambda *refs: late_kernel(spots, steps, rows, groups, *ref...  2.15 us
  transfers between devices with their start and end apart: 24, of which 8 were waited for; matrix products, arithmetic and copies ran while one was open for 1% of the time, Pallas kernels for 21%

profile of v3, /device:TPU:1, one launch (start us, length us, event | category | flops | bytes accessed | tf_op | source)
XLA Modules:
  0.0 69.7 jit_solution(3635643555933694090)
XLA Ops:
  0.6 2.2 %shard_map.85 = bf16[8,192,256]{2,1,0:T(8,128)(2,1)} custom-call(f32[128,2048]{1,0:T(8,128)} %kv_ref.1, bf16[2,4,2048]{2,1,0:T(4,128)(2,1)} %hid_ref.1), custom_call_target="tpu_custom_call" | custom-call | tf_op jit(solution)/shard_map/pallas_call | solution.py:79
  2.8 5.9 %all-to-all-start = ((bf16[8,192,256]{2,1,0:T(8,128)(2,1)}), bf16[8,192,256]{2,1,0:T(8,128)(2,1)S(1)}, u32[]{:S(2)}, u32[]{:S(2)}) async-start(bf16[8,192,256]{2,1,0:T(8,128)(2,1)} %shard_map.85), calls=%async_computation | async-start | bytes 1572864 | tf_op jit(solution)/shard_map/all_to_all | solution.py:330
  8.8 0.7 add_convert_fusion
  9.4 0.1 convert_element_type.12
  9.5 9.7 %shard_map.86 = (bf16[8,16,128]{2,1,0:T(8,128)(2,1)}, f32[8,16,128]{2,1,0:T(8,128)}, f32[8,16,128]{2,1,0:T(8,128)}, f32[8,16,128]{2,1,0:T(8,128)}) custom-call(s32[4]{0:T(128)} %refs_0_.1, bf16[2,4,2048]{2,1,0:T(4,128)(2,1)} %refs_1_.1, bf16[4,8192,128]{2,1,0:T(8,128)(2,1)} %refs_2_.1, bf16[4,8192,128]{2,1,0:T(8,128)(2,1)} %refs_3_.1), custom_call_target="tpu_custom_call" | custom-call | flops 536870912 | bytes 16777216 | tf_op jit(solution)/shard_map/pallas_call | solution.py:138
  19.2 1.0 %all-to-all-done.refs_1_ = bf16[8,192,256]{2,1,0:T(8,128)(2,1)S(1)} async-done(((bf16[8,192,256]{2,1,0:T(8,128)(2,1)}), bf16[8,192,256]{2,1,0:T(8,128)(2,1)S(1)}, u32[]{:S(2)}, u32[]{:S(2)}) %all-to-all-start) | async-done | bytes 786464 | tf_op jit(solution)/shard_map/all_to_all | solution.py:330
  20.2 1.7 %collective-permute-start.3 = (bf16[512,256]{1,0:T(8,128)(2,1)S(1)}, bf16[512,256]{1,0:T(8,128)(2,1)S(1)}, u32[]{:S(2)}, u32[]{:S(2)}) collective-permute-start(bf16[512,256]{1,0:T(8,128)(2,1)S(1)} %bitcast.9), channel_id=1, source_target_pairs={{0,32},{8,40},{16,48},{24,56},{32,64},{40,72},{48,80},{56,88},{64,... | collective-permute-start | bytes 786440 | tf_op jit(solution)/shard_map/ppermute | solution.py:44
  21.9 2.2 %collective-permute-start.4 = (bf16[512,256]{1,0:T(8,128)(2,1)S(1)}, bf16[512,256]{1,0:T(8,128)(2,1)S(1)}, u32[]{:S(2)}, u32[]{:S(2)}) collective-permute-start(bf16[512,256]{1,0:T(8,128)(2,1)S(1)} %bitcast.7), channel_id=1, source_target_pairs={{0,96},{8,104},{16,112},{24,120},{32,0},{40,8},{48,16},{56,24},{64... | collective-permute-start | bytes 786440 | tf_op jit(solution)/shard_map/ppermute | solution.py:44
  24.1 2.5 %collective-permute-start = (bf16[1024,256]{1,0:T(8,128)(2,1)S(1)}, bf16[1024,256]{1,0:T(8,128)(2,1)S(1)}, u32[]{:S(2)}, u32[]{:S(2)}) collective-permute-start(bf16[1024,256]{1,0:T(8,128)(2,1)S(1)} %bitcast.4), channel_id=1, source_target_pairs={{0,16},{8,24},{16,0},{24,8},{32,48},{40,56},{48,32},{56,40},{64,80... | collective-permute-start | bytes 1572872 | tf_op jit(solution)/shard_map/ppermute | solution.py:44
  26.6 0.1 fusion
  26.7 1.5 %collective-permute-start.9 = (bf16[512,256]{1,0:T(8,128)(2,1)S(1)}, bf16[512,256]{1,0:T(8,128)(2,1)S(1)}, u32[]{:S(2)}, u32[]{:S(2)}) collective-permute-start(bf16[512,256]{1,0:T(8,128)(2,1)S(1)} %bitcast.10), channel_id=1, source_target_pairs={{0,96},{8,104},{16,112},{24,120},{32,0},{40,8},{48,16},{56,24},{64... | collective-permute-start | bytes 786440 | tf_op jit(solution)/shard_map/ppermute | solution.py:44
  28.1 0.1 collective-permute-start.10
  28.2 0.1 pad_maximum_fusion
  28.3 0.8 %collective-permute-done.3.refs_4_ = bf16[512,256]{1,0:T(8,128)(2,1)S(1)} collective-permute-done((bf16[512,256]{1,0:T(8,128)(2,1)S(1)}, bf16[512,256]{1,0:T(8,128)(2,1)S(1)}, u32[]{:S(2)}, u32[]{:S(2)}) %collective-permute-start.3) | collective-permute-done | bytes 262176 | tf_op jit(solution)/shard_map/ppermute | solution.py:44
  29.1 0.4 collective-permute-start.5
  29.5 2.3 %collective-permute-start.7 = (bf16[512,256]{1,0:T(8,128)(2,1)S(1)}, bf16[512,256]{1,0:T(8,128)(2,1)}, u32[]{:S(2)}, u32[]{:S(2)}) collective-permute-start(bf16[512,256]{1,0:T(8,128)(2,1)S(1)} %collective-permute-done.4.refs_5_), channel_id=1, source_target_pairs={{0,96},{8,104},{16,112},{24,120},{32,0},{40,8},{48,16},{56,24},{64... | collective-permute-start | bytes 786440 | tf_op jit(solution)/shard_map/ppermute | solution.py:44
  31.8 2.6 %collective-permute-done.9.refs_6_ = bf16[512,256]{1,0:T(8,128)(2,1)S(1)} collective-permute-done((bf16[512,256]{1,0:T(8,128)(2,1)S(1)}, bf16[512,256]{1,0:T(8,128)(2,1)S(1)}, u32[]{:S(2)}, u32[]{:S(2)}) %collective-permute-start.9) | collective-permute-done | bytes 262176 | tf_op jit(solution)/shard_map/ppermute | solution.py:44
  34.4 0.5 collective-permute-done.10.refs_7_
  34.9 2.3 %collective-permute-done.refs_3_ = bf16[1024,256]{1,0:T(8,128)(2,1)S(1)} collective-permute-done((bf16[1024,256]{1,0:T(8,128)(2,1)S(1)}, bf16[1024,256]{1,0:T(8,128)(2,1)S(1)}, u32[]{:S(2)}, u32[]{:S(2)}) %collective-permute-start) | collective-permute-done | bytes 524320 | tf_op jit(solution)/shard_map/ppermute | solution.py:44
  37.2 3.8 %collective-permute-start.13 = (bf16[512,256]{1,0:T(8,128)(2,1)S(1)}, bf16[512,256]{1,0:T(8,128)(2,1)S(1)}, u32[]{:S(2)}, u32[]{:S(2)}) collective-permute-start(bf16[512,256]{1,0:T(8,128)(2,1)S(1)} %collective-permute-done.3.refs_4_), channel_id=1, source_target_pairs={{0,8},{8,0},{16,24},{24,16},{32,40},{40,32},{48,56},{56,48},{64,72... | collective-permute-start | bytes 786440 | tf_op jit(solution)/shard_map/ppermute | solution.py:44
  41.0 0.5 collective-permute-start.15
  41.5 0.7 %copy-done = bf16[512,256]{1,0:T(8,128)(2,1)} copy-done((bf16[512,256]{1,0:T(8,128)(2,1)}, bf16[512,256]{1,0:T(8,128)(2,1)S(1)}, u32[]{:S(2)}) %copy-start) | copy-done | bytes 262168
  42.2 1.6 %collective-permute-start.11 = (bf16[1024,256]{1,0:T(8,128)(2,1)S(1)}, bf16[1024,256]{1,0:T(8,128)(2,1)S(1)}, u32[]{:S(2)}, u32[]{:S(2)}) collective-permute-start(bf16[1024,256]{1,0:T(8,128)(2,1)S(1)} %bitcast.5), channel_id=1, source_target_pairs={{0,8},{8,0},{16,24},{24,16},{32,40},{40,32},{48,56},{56,48},{64,72... | collective-permute-start | bytes 1572872 | tf_op jit(solution)/shard_map/ppermute | solution.py:44
  43.8 0.7 copy-done.2
  44.5 0.5 collective-permute-start.16
  45.0 0.7 %copy-done.4 = bf16[512,256]{1,0:T(8,128)(2,1)} copy-done((bf16[512,256]{1,0:T(8,128)(2,1)}, bf16[512,256]{1,0:T(8,128)(2,1)S(1)}, u32[]{:S(2)}) %copy-start.4) | copy-done | bytes 262168
  45.7 0.0 collective-permute-start.17
  45.7 0.7 copy-done.6
  46.4 0.5 collective-permute-start.18
  46.9 1.1 %collective-permute-start.2 = (bf16[1024,256]{1,0:T(8,128)(2,1)S(1)}, bf16[1024,256]{1,0:T(8,128)(2,1)S(1)}, u32[]{:S(2)}, u32[]{:S(2)}) collective-permute-start(bf16[1024,256]{1,0:T(8,128)(2,1)S(1)} %collective-permute-done.refs_3_), channel_id=1, source_target_pairs={{0,96},{8,104},{16,112},{24,120},{32,0},{40,8},{48,16},{56,24},{64... | collective-permute-start | bytes 1572872 | tf_op jit(solution)/shard_map/ppermute | solution.py:44
  48.0 0.4 collective-permute-start.1
  48.4 0.0 collective-permute-done.18.refs_17_
  48.4 2.1 %collective-permute-start.6 = (bf16[512,256]{1,0:T(8,128)(2,1)}, bf16[512,256]{1,0:T(8,128)(2,1)S(1)}, u32[]{:S(2)}, u32[]{:S(2)}) collective-permute-start(bf16[512,256]{1,0:T(8,128)(2,1)} %collective-permute-done.5.refs_8_), channel_id=1, source_target_pairs={{0,16},{8,24},{16,0},{24,8},{32,48},{40,56},{48,32},{56,40},{64,80... | collective-permute-start | bytes 786440 | tf_op jit(solution)/shard_map/ppermute | solution.py:44
  50.6 0.8 %collective-permute-start.8 = (bf16[512,256]{1,0:T(8,128)(2,1)}, bf16[512,256]{1,0:T(8,128)(2,1)S(1)}, u32[]{:S(2)}, u32[]{:S(2)}) collective-permute-start(bf16[512,256]{1,0:T(8,128)(2,1)} %collective-permute-done.7.refs_9_), channel_id=1, source_target_pairs={{0,16},{8,24},{16,0},{24,8},{32,48},{40,56},{48,32},{56,40},{64,80... | collective-permute-start | bytes 786440 | tf_op jit(solution)/shard_map/ppermute | solution.py:44
  51.4 0.9 %copy-done.1 = bf16[512,256]{1,0:T(8,128)(2,1)S(1)} copy-done((bf16[512,256]{1,0:T(8,128)(2,1)S(1)}, bf16[512,256]{1,0:T(8,128)(2,1)}, u32[]{:S(2)}) %copy-start.1) | copy-done | bytes 262168
  52.4 0.9 %copy-done.3 = bf16[512,256]{1,0:T(8,128)(2,1)S(1)} copy-done((bf16[512,256]{1,0:T(8,128)(2,1)S(1)}, bf16[512,256]{1,0:T(8,128)(2,1)}, u32[]{:S(2)}) %copy-start.3) | copy-done | bytes 262168
  53.3 0.9 %copy-done.5 = bf16[512,256]{1,0:T(8,128)(2,1)S(1)} copy-done((bf16[512,256]{1,0:T(8,128)(2,1)S(1)}, bf16[512,256]{1,0:T(8,128)(2,1)}, u32[]{:S(2)}) %copy-start.5) | copy-done | bytes 262168
  54.3 0.9 %copy-done.7 = bf16[512,256]{1,0:T(8,128)(2,1)S(1)} copy-done((bf16[512,256]{1,0:T(8,128)(2,1)S(1)}, bf16[512,256]{1,0:T(8,128)(2,1)}, u32[]{:S(2)}) %copy-start.7) | copy-done | bytes 262168
  55.2 3.4 %shard_map.87 = (bf16[16384,256]{1,0:T(8,128)(2,1)}, f32[8,256]{1,0:T(8,128)S(1)}) custom-call(s32[1]{0:T(128)} %bitcast.refs_0_, bf16[8,192,256]{2,1,0:T(8,128)(2,1)S(1)} %all-to-all-done.refs_1_, bf16[1024,256]{1,0:T(8,128)(2,1)S(1)} %bitcast.6, bf16[1024,256]{1,0:T(8,128)(2,1)S(1)} %collective-permute-done.refs_3_, ...), custom_call_target="tpu_custom_call" | custom-call | flops 20000000000 | bytes 1000 | tf_op jit(solution)/shard_map/pallas_call | solution.py:282
  58.6 4.2 %collective-permute-done.8.refs_7_ = bf16[512,256]{1,0:T(8,128)(2,1)S(1)} collective-permute-done((bf16[512,256]{1,0:T(8,128)(2,1)}, bf16[512,256]{1,0:T(8,128)(2,1)S(1)}, u32[]{:S(2)}, u32[]{:S(2)}) %collective-permute-start.8) | collective-permute-done | bytes 262176 | tf_op jit(solution)/shard_map/ppermute | solution.py:44
  62.9 1.7 %collective-permute-start.21 = (bf16[512,256]{1,0:T(8,128)(2,1)S(1)}, bf16[512,256]{1,0:T(8,128)(2,1)S(1)}, u32[]{:S(2)}, u32[]{:S(2)}) collective-permute-start(bf16[512,256]{1,0:T(8,128)(2,1)S(1)} %collective-permute-done.6.refs_6_), channel_id=1, source_target_pairs={{0,8},{8,0},{16,24},{24,16},{32,40},{40,32},{48,56},{56,48},{64,72... | collective-permute-start | bytes 786440 | tf_op jit(solution)/shard_map/ppermute | solution.py:44
  64.5 0.1 collective-permute-start.22
  64.6 0.4 collective-permute-start.19
  65.0 0.1 collective-permute-start.20
  65.1 1.4 %shard_map.88 = (bf16[16384,256]{1,0:T(8,128)(2,1)}, f32[8,256]{1,0:T(8,128)S(1)}) custom-call(s32[1]{0:T(128)} %bitcast.refs_0_, bf16[8,192,256]{2,1,0:T(8,128)(2,1)S(1)} %all-to-all-done.refs_1_, f32[8,256]{1,0:T(8,128)S(1)} %get-tuple-element.53.refs_2_, bf16[16384,256]{1,0:T(8,128)(2,1)} %get-tuple-element.54.refs_3_, ...), custom_call_target="tpu_custom_call", output_to_operand_aliasing={{0}: (3, {})} | custom-call | flops 20000000000 | bytes 1000 | tf_op jit(solution)/shard_map/pallas_call | solution.py:282
  66.5 0.3 collective-permute-done.19.refs_10_
  66.8 0.7 %collective-permute-done.20.refs_11_ = bf16[1024,256]{1,0:T(8,128)(2,1)S(1)} collective-permute-done((bf16[1024,256]{1,0:T(8,128)(2,1)S(1)}, bf16[1024,256]{1,0:T(8,128)(2,1)S(1)}, u32[]{:S(2)}, u32[]{:S(2)}) %collective-permute-start.20) | collective-permute-done | bytes 524320 | tf_op jit(solution)/shard_map/ppermute | solution.py:44
  67.6 2.2 %shard_map.89 = (bf16[16384,256]{1,0:T(8,128)(2,1)}, bf16[2,4,256]{2,1,0:T(4,128)(2,1)}, bf16[2,4,2048]{2,1,0:T(4,128)(2,1)}) custom-call(s32[1]{0:T(128)} %bitcast.refs_0_, bf16[8,192,256]{2,1,0:T(8,128)(2,1)S(1)} %all-to-all-done.refs_1_, f32[8,256]{1,0:T(8,128)S(1)} %get-tuple-element.59.refs_2_, ...), custom_call_target="tpu_custom_call", output_to_operand_aliasing={{0}: (9, {})} | custom-call | flops 20000000000 | bytes 1000 | tf_op jit(solution)/shard_map/pallas_call | solution.py:300
  (36 shorter events, 0.2 us)
Async XLA Ops:
  2.8 17.3 %all-to-all-start = ((bf16[8,192,256]{2,1,0:T(8,128)(2,1)}), bf16[8,192,256]{2,1,0:T(8,128)(2,1)S(1)}, u32[]{:S(2)}, u32[]{:S(2)}) async-start(bf16[8,192,256]{2,1,0:T(8,128)(2,1)} %shard_map.85), calls=%async_computation | async-start | bytes 1572864 | tf_op jit(solution)/shard_map/all_to_all | solution.py:330
  20.2 8.9 %collective-permute-start.3 = (bf16[512,256]{1,0:T(8,128)(2,1)S(1)}, bf16[512,256]{1,0:T(8,128)(2,1)S(1)}, u32[]{:S(2)}, u32[]{:S(2)}) collective-permute-start(bf16[512,256]{1,0:T(8,128)(2,1)S(1)} %bitcast.9), channel_id=1, source_target_pairs={{0,32},{8,40},{16,48},{24,56},{32,64},{40,72},{48,80},{56,88},{64,... | collective-permute-start | bytes 786440 | tf_op jit(solution)/shard_map/ppermute | solution.py:44
  21.9 7.2 %collective-permute-start.4 = (bf16[512,256]{1,0:T(8,128)(2,1)S(1)}, bf16[512,256]{1,0:T(8,128)(2,1)S(1)}, u32[]{:S(2)}, u32[]{:S(2)}) collective-permute-start(bf16[512,256]{1,0:T(8,128)(2,1)S(1)} %bitcast.7), channel_id=1, source_target_pairs={{0,96},{8,104},{16,112},{24,120},{32,0},{40,8},{48,16},{56,24},{64... | collective-permute-start | bytes 786440 | tf_op jit(solution)/shard_map/ppermute | solution.py:44
  24.1 13.1 %collective-permute-start = (bf16[1024,256]{1,0:T(8,128)(2,1)S(1)}, bf16[1024,256]{1,0:T(8,128)(2,1)S(1)}, u32[]{:S(2)}, u32[]{:S(2)}) collective-permute-start(bf16[1024,256]{1,0:T(8,128)(2,1)S(1)} %bitcast.4), channel_id=1, source_target_pairs={{0,16},{8,24},{16,0},{24,8},{32,48},{40,56},{48,32},{56,40},{64,80... | collective-permute-start | bytes 1572872 | tf_op jit(solution)/shard_map/ppermute | solution.py:44
  26.7 7.7 %collective-permute-start.9 = (bf16[512,256]{1,0:T(8,128)(2,1)S(1)}, bf16[512,256]{1,0:T(8,128)(2,1)S(1)}, u32[]{:S(2)}, u32[]{:S(2)}) collective-permute-start(bf16[512,256]{1,0:T(8,128)(2,1)S(1)} %bitcast.10), channel_id=1, source_target_pairs={{0,96},{8,104},{16,112},{24,120},{32,0},{40,8},{48,16},{56,24},{64... | collective-permute-start | bytes 786440 | tf_op jit(solution)/shard_map/ppermute | solution.py:44
  28.1 6.7 %collective-permute-start.10 = (bf16[512,256]{1,0:T(8,128)(2,1)S(1)}, bf16[512,256]{1,0:T(8,128)(2,1)}, u32[]{:S(2)}, u32[]{:S(2)}) collective-permute-start(bf16[512,256]{1,0:T(8,128)(2,1)S(1)} %bitcast.8), channel_id=1, source_target_pairs={{0,32},{8,40},{16,48},{24,56},{32,64},{40,72},{48,80},{56,88},{64,... | collective-permute-start | bytes 786440 | tf_op jit(solution)/shard_map/ppermute | solution.py:44
  29.1 13.1 %collective-permute-start.5 = (bf16[512,256]{1,0:T(8,128)(2,1)S(1)}, bf16[512,256]{1,0:T(8,128)(2,1)}, u32[]{:S(2)}, u32[]{:S(2)}) collective-permute-start(bf16[512,256]{1,0:T(8,128)(2,1)S(1)} %collective-permute-done.3.refs_4_), channel_id=1, source_target_pairs={{0,32},{8,40},{16,48},{24,56},{32,64},{40,72},{48,80},{56,88},{64,... | collective-permute-start | bytes 786440 | tf_op jit(solution)/shard_map/ppermute | solution.py:44
  29.5 14.3 %collective-permute-start.7 = (bf16[512,256]{1,0:T(8,128)(2,1)S(1)}, bf16[512,256]{1,0:T(8,128)(2,1)}, u32[]{:S(2)}, u32[]{:S(2)}) collective-permute-start(bf16[512,256]{1,0:T(8,128)(2,1)S(1)} %collective-permute-done.4.refs_5_), channel_id=1, source_target_pairs={{0,96},{8,104},{16,112},{24,120},{32,0},{40,8},{48,16},{56,24},{64... | collective-permute-start | bytes 786440 | tf_op jit(solution)/shard_map/ppermute | solution.py:44
  37.2 6.6 %collective-permute-start.13 = (bf16[512,256]{1,0:T(8,128)(2,1)S(1)}, bf16[512,256]{1,0:T(8,128)(2,1)S(1)}, u32[]{:S(2)}, u32[]{:S(2)}) collective-permute-start(bf16[512,256]{1,0:T(8,128)(2,1)S(1)} %collective-permute-done.3.refs_4_), channel_id=1, source_target_pairs={{0,8},{8,0},{16,24},{24,16},{32,40},{40,32},{48,56},{56,48},{64,72... | collective-permute-start | bytes 786440 | tf_op jit(solution)/shard_map/ppermute | solution.py:44
  41.0 4.0 %collective-permute-start.14 = (bf16[512,256]{1,0:T(8,128)(2,1)S(1)}, bf16[512,256]{1,0:T(8,128)(2,1)S(1)}, u32[]{:S(2)}, u32[]{:S(2)}) collective-permute-start(bf16[512,256]{1,0:T(8,128)(2,1)S(1)} %collective-permute-done.4.refs_5_), channel_id=1, source_target_pairs={{0,8},{8,0},{16,24},{24,16},{32,40},{40,32},{48,56},{56,48},{64,72... | collective-permute-start | bytes 786440 | tf_op jit(solution)/shard_map/ppermute | solution.py:44
  41.0 4.7 %collective-permute-start.15 = (bf16[512,256]{1,0:T(8,128)(2,1)S(1)}, bf16[512,256]{1,0:T(8,128)(2,1)S(1)}, u32[]{:S(2)}, u32[]{:S(2)}) collective-permute-start(bf16[512,256]{1,0:T(8,128)(2,1)S(1)} %collective-permute-done.9.refs_6_), channel_id=1, source_target_pairs={{0,8},{8,0},{16,24},{24,16},{32,40},{40,32},{48,56},{56,48},{64,72... | collective-permute-start | bytes 786440 | tf_op jit(solution)/shard_map/ppermute | solution.py:44
  41.5 0.7 %copy-start = (bf16[512,256]{1,0:T(8,128)(2,1)}, bf16[512,256]{1,0:T(8,128)(2,1)S(1)}, u32[]{:S(2)}) copy-start(bf16[512,256]{1,0:T(8,128)(2,1)S(1)} %collective-permute-done.9.refs_6_) | copy-start | bytes 786436
  42.2 8.4 %collective-permute-start.11 = (bf16[1024,256]{1,0:T(8,128)(2,1)S(1)}, bf16[1024,256]{1,0:T(8,128)(2,1)S(1)}, u32[]{:S(2)}, u32[]{:S(2)}) collective-permute-start(bf16[1024,256]{1,0:T(8,128)(2,1)S(1)} %bitcast.5), channel_id=1, source_target_pairs={{0,8},{8,0},{16,24},{24,16},{32,40},{40,32},{48,56},{56,48},{64,72... | collective-permute-start | bytes 1572872 | tf_op jit(solution)/shard_map/ppermute | solution.py:44
  43.8 7.6 %collective-permute-start.12 = (bf16[1024,256]{1,0:T(8,128)(2,1)S(1)}, bf16[1024,256]{1,0:T(8,128)(2,1)S(1)}, u32[]{:S(2)}, u32[]{:S(2)}) collective-permute-start(bf16[1024,256]{1,0:T(8,128)(2,1)S(1)} %collective-permute-done.refs_3_), channel_id=1, source_target_pairs={{0,8},{8,0},{16,24},{24,16},{32,40},{40,32},{48,56},{56,48},{64,72... | collective-permute-start | bytes 1572872 | tf_op jit(solution)/shard_map/ppermute | solution.py:44
  43.8 0.7 %copy-start.2 = (bf16[512,256]{1,0:T(8,128)(2,1)}, bf16[512,256]{1,0:T(8,128)(2,1)S(1)}, u32[]{:S(2)}) copy-start(bf16[512,256]{1,0:T(8,128)(2,1)S(1)} %collective-permute-done.13.refs_12_) | copy-start | bytes 786436
  44.5 2.4 %collective-permute-start.16 = (bf16[512,256]{1,0:T(8,128)(2,1)}, bf16[512,256]{1,0:T(8,128)(2,1)}, u32[]{:S(2)}, u32[]{:S(2)}) collective-permute-start(bf16[512,256]{1,0:T(8,128)(2,1)} %collective-permute-done.10.refs_7_), channel_id=1, source_target_pairs={{0,8},{8,0},{16,24},{24,16},{32,40},{40,32},{48,56},{56,48},{64,72... | collective-permute-start | bytes 786440 | tf_op jit(solution)/shard_map/ppermute | solution.py:44
  45.0 0.7 %copy-start.4 = (bf16[512,256]{1,0:T(8,128)(2,1)}, bf16[512,256]{1,0:T(8,128)(2,1)S(1)}, u32[]{:S(2)}) copy-start(bf16[512,256]{1,0:T(8,128)(2,1)S(1)} %collective-permute-done.14.refs_13_) | copy-start | bytes 786436
  45.7 2.3 %collective-permute-start.17 = (bf16[512,256]{1,0:T(8,128)(2,1)}, bf16[512,256]{1,0:T(8,128)(2,1)}, u32[]{:S(2)}, u32[]{:S(2)}) collective-permute-start(bf16[512,256]{1,0:T(8,128)(2,1)} %collective-permute-done.5.refs_8_), channel_id=1, source_target_pairs={{0,8},{8,0},{16,24},{24,16},{32,40},{40,32},{48,56},{56,48},{64,72... | collective-permute-start | bytes 786440 | tf_op jit(solution)/shard_map/ppermute | solution.py:44
  45.7 0.7 %copy-start.6 = (bf16[512,256]{1,0:T(8,128)(2,1)}, bf16[512,256]{1,0:T(8,128)(2,1)S(1)}, u32[]{:S(2)}) copy-start(bf16[512,256]{1,0:T(8,128)(2,1)S(1)} %collective-permute-done.15.refs_14_) | copy-start | bytes 786436
  46.4 2.0 %collective-permute-start.18 = (bf16[512,256]{1,0:T(8,128)(2,1)}, bf16[512,256]{1,0:T(8,128)(2,1)}, u32[]{:S(2)}, u32[]{:S(2)}) collective-permute-start(bf16[512,256]{1,0:T(8,128)(2,1)} %collective-permute-done.7.refs_9_), channel_id=1, source_target_pairs={{0,8},{8,0},{16,24},{24,16},{32,40},{40,32},{48,56},{56,48},{64,72... | collective-permute-start | bytes 786440 | tf_op jit(solution)/shard_map/ppermute | solution.py:44
  46.9 15.9 %collective-permute-start.2 = (bf16[1024,256]{1,0:T(8,128)(2,1)S(1)}, bf16[1024,256]{1,0:T(8,128)(2,1)S(1)}, u32[]{:S(2)}, u32[]{:S(2)}) collective-permute-start(bf16[1024,256]{1,0:T(8,128)(2,1)S(1)} %collective-permute-done.refs_3_), channel_id=1, source_target_pairs={{0,96},{8,104},{16,112},{24,120},{32,0},{40,8},{48,16},{56,24},{64... | collective-permute-start | bytes 1572872 | tf_op jit(solution)/shard_map/ppermute | solution.py:44
  48.0 14.8 %collective-permute-start.1 = (bf16[1024,256]{1,0:T(8,128)(2,1)S(1)}, bf16[1024,256]{1,0:T(8,128)(2,1)S(1)}, u32[]{:S(2)}, u32[]{:S(2)}) collective-permute-start(bf16[1024,256]{1,0:T(8,128)(2,1)S(1)} %collective-permute-done.refs_3_), channel_id=1, source_target_pairs={{0,32},{8,40},{16,48},{24,56},{32,64},{40,72},{48,80},{56,88},{64,... | collective-permute-start | bytes 1572872 | tf_op jit(solution)/shard_map/ppermute | solution.py:44
  48.4 10.2 %collective-permute-start.6 = (bf16[512,256]{1,0:T(8,128)(2,1)}, bf16[512,256]{1,0:T(8,128)(2,1)S(1)}, u32[]{:S(2)}, u32[]{:S(2)}) collective-permute-start(bf16[512,256]{1,0:T(8,128)(2,1)} %collective-permute-done.5.refs_8_), channel_id=1, source_target_pairs={{0,16},{8,24},{16,0},{24,8},{32,48},{40,56},{48,32},{56,40},{64,80... | collective-permute-start | bytes 786440 | tf_op jit(solution)/shard_map/ppermute | solution.py:44
  50.6 12.3 %collective-permute-start.8 = (bf16[512,256]{1,0:T(8,128)(2,1)}, bf16[512,256]{1,0:T(8,128)(2,1)S(1)}, u32[]{:S(2)}, u32[]{:S(2)}) collective-permute-start(bf16[512,256]{1,0:T(8,128)(2,1)} %collective-permute-done.7.refs_9_), channel_id=1, source_target_pairs={{0,16},{8,24},{16,0},{24,8},{32,48},{40,56},{48,32},{56,40},{64,80... | collective-permute-start | bytes 786440 | tf_op jit(solution)/shard_map/ppermute | solution.py:44
  51.4 1.0 %copy-start.1 = (bf16[512,256]{1,0:T(8,128)(2,1)S(1)}, bf16[512,256]{1,0:T(8,128)(2,1)}, u32[]{:S(2)}) copy-start(bf16[512,256]{1,0:T(8,128)(2,1)} %copy-done) | copy-start | bytes 786436
  52.4 0.9 %copy-start.3 = (bf16[512,256]{1,0:T(8,128)(2,1)S(1)}, bf16[512,256]{1,0:T(8,128)(2,1)}, u32[]{:S(2)}) copy-start(bf16[512,256]{1,0:T(8,128)(2,1)} %copy-done.2) | copy-start | bytes 786436
  53.3 0.9 %copy-start.5 = (bf16[512,256]{1,0:T(8,128)(2,1)S(1)}, bf16[512,256]{1,0:T(8,128)(2,1)}, u32[]{:S(2)}) copy-start(bf16[512,256]{1,0:T(8,128)(2,1)} %copy-done.4) | copy-start | bytes 786436
  54.3 0.9 %copy-start.7 = (bf16[512,256]{1,0:T(8,128)(2,1)S(1)}, bf16[512,256]{1,0:T(8,128)(2,1)}, u32[]{:S(2)}) copy-start(bf16[512,256]{1,0:T(8,128)(2,1)} %copy-done.6) | copy-start | bytes 786436
  62.9 3.6 %collective-permute-start.21 = (bf16[512,256]{1,0:T(8,128)(2,1)S(1)}, bf16[512,256]{1,0:T(8,128)(2,1)S(1)}, u32[]{:S(2)}, u32[]{:S(2)}) collective-permute-start(bf16[512,256]{1,0:T(8,128)(2,1)S(1)} %collective-permute-done.6.refs_6_), channel_id=1, source_target_pairs={{0,8},{8,0},{16,24},{24,16},{32,40},{40,32},{48,56},{56,48},{64,72... | collective-permute-start | bytes 786440 | tf_op jit(solution)/shard_map/ppermute | solution.py:44
  64.5 2.0 %collective-permute-start.22 = (bf16[512,256]{1,0:T(8,128)(2,1)S(1)}, bf16[512,256]{1,0:T(8,128)(2,1)S(1)}, u32[]{:S(2)}, u32[]{:S(2)}) collective-permute-start(bf16[512,256]{1,0:T(8,128)(2,1)S(1)} %collective-permute-done.8.refs_7_), channel_id=1, source_target_pairs={{0,8},{8,0},{16,24},{24,16},{32,40},{40,32},{48,56},{56,48},{64,72... | collective-permute-start | bytes 786440 | tf_op jit(solution)/shard_map/ppermute | solution.py:44
  64.6 2.2 %collective-permute-start.19 = (bf16[1024,256]{1,0:T(8,128)(2,1)S(1)}, bf16[1024,256]{1,0:T(8,128)(2,1)S(1)}, u32[]{:S(2)}, u32[]{:S(2)}) collective-permute-start(bf16[1024,256]{1,0:T(8,128)(2,1)S(1)} %collective-permute-done.1.refs_4_), channel_id=1, source_target_pairs={{0,8},{8,0},{16,24},{24,16},{32,40},{40,32},{48,56},{56,48},{64,72... | collective-permute-start | bytes 1572872 | tf_op jit(solution)/shard_map/ppermute | solution.py:44
  65.0 2.5 %collective-permute-start.20 = (bf16[1024,256]{1,0:T(8,128)(2,1)S(1)}, bf16[1024,256]{1,0:T(8,128)(2,1)S(1)}, u32[]{:S(2)}, u32[]{:S(2)}) collective-permute-start(bf16[1024,256]{1,0:T(8,128)(2,1)S(1)} %collective-permute-done.2.refs_5_), channel_id=1, source_target_pairs={{0,8},{8,0},{16,24},{24,16},{32,40},{40,32},{48,56},{56,48},{64,72... | collective-permute-start | bytes 1572872 | tf_op jit(solution)/shard_map/ppermute | solution.py:44
  65.1 2.4 %copy-start.8 = (f32[8,16,128]{2,1,0:T(8,128)S(1)}, f32[8,16,128]{2,1,0:T(8,128)}, u32[]{:S(2)}) copy-start(f32[8,16,128]{2,1,0:T(8,128)} %get-tuple-element.63.refs_6_) | copy-start | bytes 196612
  65.1 2.4 %copy-start.9 = (f32[8,16,128]{2,1,0:T(8,128)S(1)}, f32[8,16,128]{2,1,0:T(8,128)}, u32[]{:S(2)}) copy-start(f32[8,16,128]{2,1,0:T(8,128)} %get-tuple-element.64.refs_7_) | copy-start | bytes 196612
  65.1 2.4 %copy-start.10 = (f32[8,16,128]{2,1,0:T(8,128)S(1)}, f32[8,16,128]{2,1,0:T(8,128)}, u32[]{:S(2)}) copy-start(f32[8,16,128]{2,1,0:T(8,128)} %get-tuple-element.65.refs_8_) | copy-start | bytes 196612
  65.1 2.4 %copy-start.11 = (bf16[8,16,128]{2,1,0:T(8,128)(2,1)S(1)}, bf16[8,16,128]{2,1,0:T(8,128)(2,1)}, u32[]{:S(2)}) copy-start(bf16[8,16,128]{2,1,0:T(8,128)(2,1)} %get-tuple-element.62.refs_5_) | copy-start | bytes 98308

commit v4 on v3

--- a/solution.py
+++ b/solution.py
@@ -20,6 +20,7 @@
 HALF = OWNED // 2
 COLS = 2 * HD
 VMEM_BYTES = 60 * 2**20
+PACK_STEPS = 2
 CACHE_VMEM = 60 * 2**20
 PLACE_VMEM = 48 * 2**20
 PLACE_COST = pl.CostEstimate(flops=20000000000, bytes_accessed=1000, transcendentals=0)
@@ -70,17 +71,22 @@
     flat = jnp.concatenate([hid_ref[s].astype(jnp.float32) for s in range(steps)], axis=0)
     cut = [flat[:, c : c + COLS] for c in range(0, width, COLS)]
     cut = jnp.concatenate(cut, axis=0).astype(jnp.bfloat16)
-    for t in range(TP):
+    for t in range(out_ref.shape[0]):
         out_ref[t, :ROWS] = kv_ref[:, t * COLS : (t + 1) * COLS].astype(jnp.bfloat16)
         out_ref[t, ROWS:] = cut
 
 
 def pack(kv_master, hidden):
+    shape = (TP, ROWS + hidden.size // COLS, COLS)
     return pl.pallas_call(
         pack_kernel,
-        in_specs=[VMEM, VMEM],
-        out_specs=VMEM,
-        out_shape=jax.ShapeDtypeStruct((TP, ROWS + hidden.size // COLS, COLS), jnp.bfloat16),
+        grid=(PACK_STEPS,),
+        in_specs=[
+            pl.BlockSpec((ROWS, TP * COLS // PACK_STEPS), lambda i: (0, i)),
+            pl.BlockSpec(hidden.shape, lambda i: (0, 0, 0)),
+        ],
+        out_specs=pl.BlockSpec((TP // PACK_STEPS, *shape[1:]), lambda i: (i, 0, 0)),
+        out_shape=jax.ShapeDtypeStruct(shape, jnp.bfloat16),
         compiler_params=pltpu.CompilerParams(vmem_limit_bytes=VMEM_BYTES),
     )(kv_master, hidden)
 

time: 70.1 us -> 69.9 us (level)
  no operation moved by 1% of the time
where the time goes in v4:
time: 69.9 us; the launch traced here: 69.6 us
  starting transfers between devices  30.1 us (43%)
  Pallas kernels  18.6 us (27%)
  waiting for transfers between devices  12.5 us (18%)
  local copies, waits for them, and re-layouts  6.77 us (10%)
  other arithmetic  0.86 us (1%)
  between operations  0.74 us (1%)
    ppermute x23, starting transfers between devices, send(): return lax.ppermute(value, 'rep', pairs)  24.2 us
    ppermute x23, waiting for transfers between devices, send(): return lax.ppermute(value, 'rep', pairs)  11.6 us
    pallas_call x1, Pallas kernels, attend_cache(): pl.pallas_call(lambda *refs: cache_kernel(first, count, *refs), grid=(cou...  9.66 us
    unnamed x24, local copies, waits for them, and re-layouts  6.61 us
    all_to_all x1, starting transfers between devices, local(): lax.all_to_all(pack(kv_master, hidden), 'tp', split_axis=0, concat_axis=0...  5.95 us
    pallas_call x2, Pallas kernels, place_early(): pl.pallas_call(lambda *refs: early_kernel(spots, bool(before), *refs), in...  4.74 us
    pallas_call x1, Pallas kernels, place_late(): pl.pallas_call(lambda *refs: late_kernel(spots, steps, rows, groups, *ref...  2.15 us
    pallas_call x1, Pallas kernels, pack(): pl.pallas_call(pack_kernel, grid=(PACK_STEPS,), in_specs=[pl.BlockSpec((R...  2.02 us
  transfers between devices with their start and end apart: 24, of which 8 were waited for; matrix products, arithmetic and copies ran while one was open for 1% of the time, Pallas kernels for 21%

profile of v4, /device:TPU:1, one launch (start us, length us, event | category | flops | bytes accessed | tf_op | source)
XLA Modules:
  0.0 69.6 jit_solution(3943933827255681702)
XLA Ops:
  0.6 2.0 %shard_map.85 = bf16[8,192,256]{2,1,0:T(8,128)(2,1)} custom-call(f32[128,2048]{1,0:T(8,128)} %kv_ref.1, bf16[2,4,2048]{2,1,0:T(4,128)(2,1)} %hid_ref.1), custom_call_target="tpu_custom_call" | custom-call | tf_op jit(solution)/shard_map/pallas_call | solution.py:81
  2.6 5.9 %all-to-all-start = ((bf16[8,192,256]{2,1,0:T(8,128)(2,1)}), bf16[8,192,256]{2,1,0:T(8,128)(2,1)S(1)}, u32[]{:S(2)}, u32[]{:S(2)}) async-start(bf16[8,192,256]{2,1,0:T(8,128)(2,1)} %shard_map.85), calls=%async_computation | async-start | bytes 1572864 | tf_op jit(solution)/shard_map/all_to_all | solution.py:336
  8.6 0.7 add_convert_fusion
  9.3 0.1 convert_element_type.12
  9.3 9.7 %shard_map.86 = (bf16[8,16,128]{2,1,0:T(8,128)(2,1)}, f32[8,16,128]{2,1,0:T(8,128)}, f32[8,16,128]{2,1,0:T(8,128)}, f32[8,16,128]{2,1,0:T(8,128)}) custom-call(s32[4]{0:T(128)} %refs_0_.1, bf16[2,4,2048]{2,1,0:T(4,128)(2,1)} %refs_1_.1, bf16[4,8192,128]{2,1,0:T(8,128)(2,1)} %refs_2_.1, bf16[4,8192,128]{2,1,0:T(8,128)(2,1)} %refs_3_.1), custom_call_target="tpu_custom_call" | custom-call | flops 536870912 | bytes 16777216 | tf_op jit(solution)/shard_map/pallas_call | solution.py:144
  19.0 1.0 %all-to-all-done.refs_1_ = bf16[8,192,256]{2,1,0:T(8,128)(2,1)S(1)} async-done(((bf16[8,192,256]{2,1,0:T(8,128)(2,1)}), bf16[8,192,256]{2,1,0:T(8,128)(2,1)S(1)}, u32[]{:S(2)}, u32[]{:S(2)}) %all-to-all-start) | async-done | bytes 786464 | tf_op jit(solution)/shard_map/all_to_all | solution.py:336
  20.1 1.7 %collective-permute-start.3 = (bf16[512,256]{1,0:T(8,128)(2,1)S(1)}, bf16[512,256]{1,0:T(8,128)(2,1)S(1)}, u32[]{:S(2)}, u32[]{:S(2)}) collective-permute-start(bf16[512,256]{1,0:T(8,128)(2,1)S(1)} %bitcast.9), channel_id=1, source_target_pairs={{0,32},{8,40},{16,48},{24,56},{32,64},{40,72},{48,80},{56,88},{64,... | collective-permute-start | bytes 786440 | tf_op jit(solution)/shard_map/ppermute | solution.py:45
  21.8 2.2 %collective-permute-start.4 = (bf16[512,256]{1,0:T(8,128)(2,1)S(1)}, bf16[512,256]{1,0:T(8,128)(2,1)S(1)}, u32[]{:S(2)}, u32[]{:S(2)}) collective-permute-start(bf16[512,256]{1,0:T(8,128)(2,1)S(1)} %bitcast.7), channel_id=1, source_target_pairs={{0,96},{8,104},{16,112},{24,120},{32,0},{40,8},{48,16},{56,24},{64... | collective-permute-start | bytes 786440 | tf_op jit(solution)/shard_map/ppermute | solution.py:45
  24.0 2.5 %collective-permute-start = (bf16[1024,256]{1,0:T(8,128)(2,1)S(1)}, bf16[1024,256]{1,0:T(8,128)(2,1)S(1)}, u32[]{:S(2)}, u32[]{:S(2)}) collective-permute-start(bf16[1024,256]{1,0:T(8,128)(2,1)S(1)} %bitcast.4), channel_id=1, source_target_pairs={{0,16},{8,24},{16,0},{24,8},{32,48},{40,56},{48,32},{56,40},{64,80... | collective-permute-start | bytes 1572872 | tf_op jit(solution)/shard_map/ppermute | solution.py:45
  26.4 0.1 fusion
  26.5 1.5 %collective-permute-start.9 = (bf16[512,256]{1,0:T(8,128)(2,1)S(1)}, bf16[512,256]{1,0:T(8,128)(2,1)S(1)}, u32[]{:S(2)}, u32[]{:S(2)}) collective-permute-start(bf16[512,256]{1,0:T(8,128)(2,1)S(1)} %bitcast.10), channel_id=1, source_target_pairs={{0,96},{8,104},{16,112},{24,120},{32,0},{40,8},{48,16},{56,24},{64... | collective-permute-start | bytes 786440 | tf_op jit(solution)/shard_map/ppermute | solution.py:45
  28.0 0.1 collective-permute-start.10
  28.1 0.1 pad_maximum_fusion
  28.1 0.8 %collective-permute-done.3.refs_4_ = bf16[512,256]{1,0:T(8,128)(2,1)S(1)} collective-permute-done((bf16[512,256]{1,0:T(8,128)(2,1)S(1)}, bf16[512,256]{1,0:T(8,128)(2,1)S(1)}, u32[]{:S(2)}, u32[]{:S(2)}) %collective-permute-start.3) | collective-permute-done | bytes 262176 | tf_op jit(solution)/shard_map/ppermute | solution.py:45
  28.9 0.4 collective-permute-start.5
  29.4 2.3 %collective-permute-start.7 = (bf16[512,256]{1,0:T(8,128)(2,1)S(1)}, bf16[512,256]{1,0:T(8,128)(2,1)}, u32[]{:S(2)}, u32[]{:S(2)}) collective-permute-start(bf16[512,256]{1,0:T(8,128)(2,1)S(1)} %collective-permute-done.4.refs_5_), channel_id=1, source_target_pairs={{0,96},{8,104},{16,112},{24,120},{32,0},{40,8},{48,16},{56,24},{64... | collective-permute-start | bytes 786440 | tf_op jit(solution)/shard_map/ppermute | solution.py:45
  31.6 2.6 %collective-permute-done.9.refs_6_ = bf16[512,256]{1,0:T(8,128)(2,1)S(1)} collective-permute-done((bf16[512,256]{1,0:T(8,128)(2,1)S(1)}, bf16[512,256]{1,0:T(8,128)(2,1)S(1)}, u32[]{:S(2)}, u32[]{:S(2)}) %collective-permute-start.9) | collective-permute-done | bytes 262176 | tf_op jit(solution)/shard_map/ppermute | solution.py:45
  34.2 0.5 collective-permute-done.10.refs_7_
  34.7 2.3 %collective-permute-done.refs_3_ = bf16[1024,256]{1,0:T(8,128)(2,1)S(1)} collective-permute-done((bf16[1024,256]{1,0:T(8,128)(2,1)S(1)}, bf16[1024,256]{1,0:T(8,128)(2,1)S(1)}, u32[]{:S(2)}, u32[]{:S(2)}) %collective-permute-start) | collective-permute-done | bytes 524320 | tf_op jit(solution)/shard_map/ppermute | solution.py:45
  37.0 3.8 %collective-permute-start.13 = (bf16[512,256]{1,0:T(8,128)(2,1)S(1)}, bf16[512,256]{1,0:T(8,128)(2,1)S(1)}, u32[]{:S(2)}, u32[]{:S(2)}) collective-permute-start(bf16[512,256]{1,0:T(8,128)(2,1)S(1)} %collective-permute-done.3.refs_4_), channel_id=1, source_target_pairs={{0,8},{8,0},{16,24},{24,16},{32,40},{40,32},{48,56},{56,48},{64,72... | collective-permute-start | bytes 786440 | tf_op jit(solution)/shard_map/ppermute | solution.py:45
  40.8 0.5 collective-permute-start.15
  41.3 0.7 %copy-done = bf16[512,256]{1,0:T(8,128)(2,1)} copy-done((bf16[512,256]{1,0:T(8,128)(2,1)}, bf16[512,256]{1,0:T(8,128)(2,1)S(1)}, u32[]{:S(2)}) %copy-start) | copy-done | bytes 262168
  42.0 1.6 %collective-permute-start.11 = (bf16[1024,256]{1,0:T(8,128)(2,1)S(1)}, bf16[1024,256]{1,0:T(8,128)(2,1)S(1)}, u32[]{:S(2)}, u32[]{:S(2)}) collective-permute-start(bf16[1024,256]{1,0:T(8,128)(2,1)S(1)} %bitcast.5), channel_id=1, source_target_pairs={{0,8},{8,0},{16,24},{24,16},{32,40},{40,32},{48,56},{56,48},{64,72... | collective-permute-start | bytes 1572872 | tf_op jit(solution)/shard_map/ppermute | solution.py:45
  43.7 0.7 copy-done.2
  44.3 0.5 collective-permute-start.16
  44.9 0.7 %copy-done.4 = bf16[512,256]{1,0:T(8,128)(2,1)} copy-done((bf16[512,256]{1,0:T(8,128)(2,1)}, bf16[512,256]{1,0:T(8,128)(2,1)S(1)}, u32[]{:S(2)}) %copy-start.4) | copy-done | bytes 262168
  45.6 0.0 collective-permute-start.17
  45.6 0.7 %copy-done.6 = bf16[512,256]{1,0:T(8,128)(2,1)} copy-done((bf16[512,256]{1,0:T(8,128)(2,1)}, bf16[512,256]{1,0:T(8,128)(2,1)S(1)}, u32[]{:S(2)}) %copy-start.6) | copy-done | bytes 262168
  46.3 0.5 collective-permute-start.18
  46.8 1.1 %collective-permute-start.2 = (bf16[1024,256]{1,0:T(8,128)(2,1)S(1)}, bf16[1024,256]{1,0:T(8,128)(2,1)S(1)}, u32[]{:S(2)}, u32[]{:S(2)}) collective-permute-start(bf16[1024,256]{1,0:T(8,128)(2,1)S(1)} %collective-permute-done.refs_3_), channel_id=1, source_target_pairs={{0,96},{8,104},{16,112},{24,120},{32,0},{40,8},{48,16},{56,24},{64... | collective-permute-start | bytes 1572872 | tf_op jit(solution)/shard_map/ppermute | solution.py:45
  47.9 0.4 collective-permute-start.1
  48.3 0.0 collective-permute-done.18.refs_17_
  48.3 2.1 %collective-permute-start.6 = (bf16[512,256]{1,0:T(8,128)(2,1)}, bf16[512,256]{1,0:T(8,128)(2,1)S(1)}, u32[]{:S(2)}, u32[]{:S(2)}) collective-permute-start(bf16[512,256]{1,0:T(8,128)(2,1)} %collective-permute-done.5.refs_8_), channel_id=1, source_target_pairs={{0,16},{8,24},{16,0},{24,8},{32,48},{40,56},{48,32},{56,40},{64,80... | collective-permute-start | bytes 786440 | tf_op jit(solution)/shard_map/ppermute | solution.py:45
  50.4 0.8 %collective-permute-start.8 = (bf16[512,256]{1,0:T(8,128)(2,1)}, bf16[512,256]{1,0:T(8,128)(2,1)S(1)}, u32[]{:S(2)}, u32[]{:S(2)}) collective-permute-start(bf16[512,256]{1,0:T(8,128)(2,1)} %collective-permute-done.7.refs_9_), channel_id=1, source_target_pairs={{0,16},{8,24},{16,0},{24,8},{32,48},{40,56},{48,32},{56,40},{64,80... | collective-permute-start | bytes 786440 | tf_op jit(solution)/shard_map/ppermute | solution.py:45
  51.3 0.9 %copy-done.1 = bf16[512,256]{1,0:T(8,128)(2,1)S(1)} copy-done((bf16[512,256]{1,0:T(8,128)(2,1)S(1)}, bf16[512,256]{1,0:T(8,128)(2,1)}, u32[]{:S(2)}) %copy-start.1) | copy-done | bytes 262168
  52.2 0.9 %copy-done.3 = bf16[512,256]{1,0:T(8,128)(2,1)S(1)} copy-done((bf16[512,256]{1,0:T(8,128)(2,1)S(1)}, bf16[512,256]{1,0:T(8,128)(2,1)}, u32[]{:S(2)}) %copy-start.3) | copy-done | bytes 262168
  53.2 0.9 %copy-done.5 = bf16[512,256]{1,0:T(8,128)(2,1)S(1)} copy-done((bf16[512,256]{1,0:T(8,128)(2,1)S(1)}, bf16[512,256]{1,0:T(8,128)(2,1)}, u32[]{:S(2)}) %copy-start.5) | copy-done | bytes 262168
  54.1 0.9 %copy-done.7 = bf16[512,256]{1,0:T(8,128)(2,1)S(1)} copy-done((bf16[512,256]{1,0:T(8,128)(2,1)S(1)}, bf16[512,256]{1,0:T(8,128)(2,1)}, u32[]{:S(2)}) %copy-start.7) | copy-done | bytes 262168
  55.1 3.4 %shard_map.87 = (bf16[16384,256]{1,0:T(8,128)(2,1)}, f32[8,256]{1,0:T(8,128)S(1)}) custom-call(s32[1]{0:T(128)} %bitcast.refs_0_, bf16[8,192,256]{2,1,0:T(8,128)(2,1)S(1)} %all-to-all-done.refs_1_, bf16[1024,256]{1,0:T(8,128)(2,1)S(1)} %bitcast.6, bf16[1024,256]{1,0:T(8,128)(2,1)S(1)} %collective-permute-done.refs_3_, ...), custom_call_target="tpu_custom_call" | custom-call | flops 20000000000 | bytes 1000 | tf_op jit(solution)/shard_map/pallas_call | solution.py:288
  58.4 4.2 %collective-permute-done.8.refs_7_ = bf16[512,256]{1,0:T(8,128)(2,1)S(1)} collective-permute-done((bf16[512,256]{1,0:T(8,128)(2,1)}, bf16[512,256]{1,0:T(8,128)(2,1)S(1)}, u32[]{:S(2)}, u32[]{:S(2)}) %collective-permute-start.8) | collective-permute-done | bytes 262176 | tf_op jit(solution)/shard_map/ppermute | solution.py:45
  62.7 1.7 %collective-permute-start.21 = (bf16[512,256]{1,0:T(8,128)(2,1)S(1)}, bf16[512,256]{1,0:T(8,128)(2,1)S(1)}, u32[]{:S(2)}, u32[]{:S(2)}) collective-permute-start(bf16[512,256]{1,0:T(8,128)(2,1)S(1)} %collective-permute-done.6.refs_6_), channel_id=1, source_target_pairs={{0,8},{8,0},{16,24},{24,16},{32,40},{40,32},{48,56},{56,48},{64,72... | collective-permute-start | bytes 786440 | tf_op jit(solution)/shard_map/ppermute | solution.py:45
  64.3 0.1 collective-permute-start.22
  64.4 0.4 collective-permute-start.19
  64.9 0.1 collective-permute-start.20
  65.0 1.4 %shard_map.88 = (bf16[16384,256]{1,0:T(8,128)(2,1)}, f32[8,256]{1,0:T(8,128)S(1)}) custom-call(s32[1]{0:T(128)} %bitcast.refs_0_, bf16[8,192,256]{2,1,0:T(8,128)(2,1)S(1)} %all-to-all-done.refs_1_, f32[8,256]{1,0:T(8,128)S(1)} %get-tuple-element.53.refs_2_, bf16[16384,256]{1,0:T(8,128)(2,1)} %get-tuple-element.54.refs_3_, ...), custom_call_target="tpu_custom_call", output_to_operand_aliasing={{0}: (3, {})} | custom-call | flops 20000000000 | bytes 1000 | tf_op jit(solution)/shard_map/pallas_call | solution.py:288
  66.4 0.3 collective-permute-done.19.refs_10_
  66.6 0.7 %collective-permute-done.20.refs_11_ = bf16[1024,256]{1,0:T(8,128)(2,1)S(1)} collective-permute-done((bf16[1024,256]{1,0:T(8,128)(2,1)S(1)}, bf16[1024,256]{1,0:T(8,128)(2,1)S(1)}, u32[]{:S(2)}, u32[]{:S(2)}) %collective-permute-start.20) | collective-permute-done | bytes 524320 | tf_op jit(solution)/shard_map/ppermute | solution.py:45
  67.4 2.2 %shard_map.89 = (bf16[16384,256]{1,0:T(8,128)(2,1)}, bf16[2,4,256]{2,1,0:T(4,128)(2,1)}, bf16[2,4,2048]{2,1,0:T(4,128)(2,1)}) custom-call(s32[1]{0:T(128)} %bitcast.refs_0_, bf16[8,192,256]{2,1,0:T(8,128)(2,1)S(1)} %all-to-all-done.refs_1_, f32[8,256]{1,0:T(8,128)S(1)} %get-tuple-element.59.refs_2_, ...), custom_call_target="tpu_custom_call", output_to_operand_aliasing={{0}: (9, {})} | custom-call | flops 20000000000 | bytes 1000 | tf_op jit(solution)/shard_map/pallas_call | solution.py:306
  (36 shorter events, 0.2 us)
Async XLA Ops:
  2.6 17.3 %all-to-all-start = ((bf16[8,192,256]{2,1,0:T(8,128)(2,1)}), bf16[8,192,256]{2,1,0:T(8,128)(2,1)S(1)}, u32[]{:S(2)}, u32[]{:S(2)}) async-start(bf16[8,192,256]{2,1,0:T(8,128)(2,1)} %shard_map.85), calls=%async_computation | async-start | bytes 1572864 | tf_op jit(solution)/shard_map/all_to_all | solution.py:336
  20.1 8.9 %collective-permute-start.3 = (bf16[512,256]{1,0:T(8,128)(2,1)S(1)}, bf16[512,256]{1,0:T(8,128)(2,1)S(1)}, u32[]{:S(2)}, u32[]{:S(2)}) collective-permute-start(bf16[512,256]{1,0:T(8,128)(2,1)S(1)} %bitcast.9), channel_id=1, source_target_pairs={{0,32},{8,40},{16,48},{24,56},{32,64},{40,72},{48,80},{56,88},{64,... | collective-permute-start | bytes 786440 | tf_op jit(solution)/shard_map/ppermute | solution.py:45
  21.8 7.2 %collective-permute-start.4 = (bf16[512,256]{1,0:T(8,128)(2,1)S(1)}, bf16[512,256]{1,0:T(8,128)(2,1)S(1)}, u32[]{:S(2)}, u32[]{:S(2)}) collective-permute-start(bf16[512,256]{1,0:T(8,128)(2,1)S(1)} %bitcast.7), channel_id=1, source_target_pairs={{0,96},{8,104},{16,112},{24,120},{32,0},{40,8},{48,16},{56,24},{64... | collective-permute-start | bytes 786440 | tf_op jit(solution)/shard_map/ppermute | solution.py:45
  24.0 13.1 %collective-permute-start = (bf16[1024,256]{1,0:T(8,128)(2,1)S(1)}, bf16[1024,256]{1,0:T(8,128)(2,1)S(1)}, u32[]{:S(2)}, u32[]{:S(2)}) collective-permute-start(bf16[1024,256]{1,0:T(8,128)(2,1)S(1)} %bitcast.4), channel_id=1, source_target_pairs={{0,16},{8,24},{16,0},{24,8},{32,48},{40,56},{48,32},{56,40},{64,80... | collective-permute-start | bytes 1572872 | tf_op jit(solution)/shard_map/ppermute | solution.py:45
  26.5 7.7 %collective-permute-start.9 = (bf16[512,256]{1,0:T(8,128)(2,1)S(1)}, bf16[512,256]{1,0:T(8,128)(2,1)S(1)}, u32[]{:S(2)}, u32[]{:S(2)}) collective-permute-start(bf16[512,256]{1,0:T(8,128)(2,1)S(1)} %bitcast.10), channel_id=1, source_target_pairs={{0,96},{8,104},{16,112},{24,120},{32,0},{40,8},{48,16},{56,24},{64... | collective-permute-start | bytes 786440 | tf_op jit(solution)/shard_map/ppermute | solution.py:45
  28.0 6.7 %collective-permute-start.10 = (bf16[512,256]{1,0:T(8,128)(2,1)S(1)}, bf16[512,256]{1,0:T(8,128)(2,1)}, u32[]{:S(2)}, u32[]{:S(2)}) collective-permute-start(bf16[512,256]{1,0:T(8,128)(2,1)S(1)} %bitcast.8), channel_id=1, source_target_pairs={{0,32},{8,40},{16,48},{24,56},{32,64},{40,72},{48,80},{56,88},{64,... | collective-permute-start | bytes 786440 | tf_op jit(solution)/shard_map/ppermute | solution.py:45
  28.9 13.1 %collective-permute-start.5 = (bf16[512,256]{1,0:T(8,128)(2,1)S(1)}, bf16[512,256]{1,0:T(8,128)(2,1)}, u32[]{:S(2)}, u32[]{:S(2)}) collective-permute-start(bf16[512,256]{1,0:T(8,128)(2,1)S(1)} %collective-permute-done.3.refs_4_), channel_id=1, source_target_pairs={{0,32},{8,40},{16,48},{24,56},{32,64},{40,72},{48,80},{56,88},{64,... | collective-permute-start | bytes 786440 | tf_op jit(solution)/shard_map/ppermute | solution.py:45
  29.4 14.3 %collective-permute-start.7 = (bf16[512,256]{1,0:T(8,128)(2,1)S(1)}, bf16[512,256]{1,0:T(8,128)(2,1)}, u32[]{:S(2)}, u32[]{:S(2)}) collective-permute-start(bf16[512,256]{1,0:T(8,128)(2,1)S(1)} %collective-permute-done.4.refs_5_), channel_id=1, source_target_pairs={{0,96},{8,104},{16,112},{24,120},{32,0},{40,8},{48,16},{56,24},{64... | collective-permute-start | bytes 786440 | tf_op jit(solution)/shard_map/ppermute | solution.py:45
  37.0 6.6 %collective-permute-start.13 = (bf16[512,256]{1,0:T(8,128)(2,1)S(1)}, bf16[512,256]{1,0:T(8,128)(2,1)S(1)}, u32[]{:S(2)}, u32[]{:S(2)}) collective-permute-start(bf16[512,256]{1,0:T(8,128)(2,1)S(1)} %collective-permute-done.3.refs_4_), channel_id=1, source_target_pairs={{0,8},{8,0},{16,24},{24,16},{32,40},{40,32},{48,56},{56,48},{64,72... | collective-permute-start | bytes 786440 | tf_op jit(solution)/shard_map/ppermute | solution.py:45
  40.8 4.0 %collective-permute-start.14 = (bf16[512,256]{1,0:T(8,128)(2,1)S(1)}, bf16[512,256]{1,0:T(8,128)(2,1)S(1)}, u32[]{:S(2)}, u32[]{:S(2)}) collective-permute-start(bf16[512,256]{1,0:T(8,128)(2,1)S(1)} %collective-permute-done.4.refs_5_), channel_id=1, source_target_pairs={{0,8},{8,0},{16,24},{24,16},{32,40},{40,32},{48,56},{56,48},{64,72... | collective-permute-start | bytes 786440 | tf_op jit(solution)/shard_map/ppermute | solution.py:45
  40.8 4.7 %collective-permute-start.15 = (bf16[512,256]{1,0:T(8,128)(2,1)S(1)}, bf16[512,256]{1,0:T(8,128)(2,1)S(1)}, u32[]{:S(2)}, u32[]{:S(2)}) collective-permute-start(bf16[512,256]{1,0:T(8,128)(2,1)S(1)} %collective-permute-done.9.refs_6_), channel_id=1, source_target_pairs={{0,8},{8,0},{16,24},{24,16},{32,40},{40,32},{48,56},{56,48},{64,72... | collective-permute-start | bytes 786440 | tf_op jit(solution)/shard_map/ppermute | solution.py:45
  41.3 0.7 %copy-start = (bf16[512,256]{1,0:T(8,128)(2,1)}, bf16[512,256]{1,0:T(8,128)(2,1)S(1)}, u32[]{:S(2)}) copy-start(bf16[512,256]{1,0:T(8,128)(2,1)S(1)} %collective-permute-done.9.refs_6_) | copy-start | bytes 786436
  42.0 8.4 %collective-permute-start.11 = (bf16[1024,256]{1,0:T(8,128)(2,1)S(1)}, bf16[1024,256]{1,0:T(8,128)(2,1)S(1)}, u32[]{:S(2)}, u32[]{:S(2)}) collective-permute-start(bf16[1024,256]{1,0:T(8,128)(2,1)S(1)} %bitcast.5), channel_id=1, source_target_pairs={{0,8},{8,0},{16,24},{24,16},{32,40},{40,32},{48,56},{56,48},{64,72... | collective-permute-start | bytes 1572872 | tf_op jit(solution)/shard_map/ppermute | solution.py:45
  43.6 7.6 %collective-permute-start.12 = (bf16[1024,256]{1,0:T(8,128)(2,1)S(1)}, bf16[1024,256]{1,0:T(8,128)(2,1)S(1)}, u32[]{:S(2)}, u32[]{:S(2)}) collective-permute-start(bf16[1024,256]{1,0:T(8,128)(2,1)S(1)} %collective-permute-done.refs_3_), channel_id=1, source_target_pairs={{0,8},{8,0},{16,24},{24,16},{32,40},{40,32},{48,56},{56,48},{64,72... | collective-permute-start | bytes 1572872 | tf_op jit(solution)/shard_map/ppermute | solution.py:45
  43.6 0.7 %copy-start.2 = (bf16[512,256]{1,0:T(8,128)(2,1)}, bf16[512,256]{1,0:T(8,128)(2,1)S(1)}, u32[]{:S(2)}) copy-start(bf16[512,256]{1,0:T(8,128)(2,1)S(1)} %collective-permute-done.13.refs_12_) | copy-start | bytes 786436
  44.3 2.4 %collective-permute-start.16 = (bf16[512,256]{1,0:T(8,128)(2,1)}, bf16[512,256]{1,0:T(8,128)(2,1)}, u32[]{:S(2)}, u32[]{:S(2)}) collective-permute-start(bf16[512,256]{1,0:T(8,128)(2,1)} %collective-permute-done.10.refs_7_), channel_id=1, source_target_pairs={{0,8},{8,0},{16,24},{24,16},{32,40},{40,32},{48,56},{56,48},{64,72... | collective-permute-start | bytes 786440 | tf_op jit(solution)/shard_map/ppermute | solution.py:45
  44.9 0.7 %copy-start.4 = (bf16[512,256]{1,0:T(8,128)(2,1)}, bf16[512,256]{1,0:T(8,128)(2,1)S(1)}, u32[]{:S(2)}) copy-start(bf16[512,256]{1,0:T(8,128)(2,1)S(1)} %collective-permute-done.14.refs_13_) | copy-start | bytes 786436
  45.6 2.3 %collective-permute-start.17 = (bf16[512,256]{1,0:T(8,128)(2,1)}, bf16[512,256]{1,0:T(8,128)(2,1)}, u32[]{:S(2)}, u32[]{:S(2)}) collective-permute-start(bf16[512,256]{1,0:T(8,128)(2,1)} %collective-permute-done.5.refs_8_), channel_id=1, source_target_pairs={{0,8},{8,0},{16,24},{24,16},{32,40},{40,32},{48,56},{56,48},{64,72... | collective-permute-start | bytes 786440 | tf_op jit(solution)/shard_map/ppermute | solution.py:45
  45.6 0.7 %copy-start.6 = (bf16[512,256]{1,0:T(8,128)(2,1)}, bf16[512,256]{1,0:T(8,128)(2,1)S(1)}, u32[]{:S(2)}) copy-start(bf16[512,256]{1,0:T(8,128)(2,1)S(1)} %collective-permute-done.15.refs_14_) | copy-start | bytes 786436
  46.3 2.0 %collective-permute-start.18 = (bf16[512,256]{1,0:T(8,128)(2,1)}, bf16[512,256]{1,0:T(8,128)(2,1)}, u32[]{:S(2)}, u32[]{:S(2)}) collective-permute-start(bf16[512,256]{1,0:T(8,128)(2,1)} %collective-permute-done.7.refs_9_), channel_id=1, source_target_pairs={{0,8},{8,0},{16,24},{24,16},{32,40},{40,32},{48,56},{56,48},{64,72... | collective-permute-start | bytes 786440 | tf_op jit(solution)/shard_map/ppermute | solution.py:45
  46.8 15.9 %collective-permute-start.2 = (bf16[1024,256]{1,0:T(8,128)(2,1)S(1)}, bf16[1024,256]{1,0:T(8,128)(2,1)S(1)}, u32[]{:S(2)}, u32[]{:S(2)}) collective-permute-start(bf16[1024,256]{1,0:T(8,128)(2,1)S(1)} %collective-permute-done.refs_3_), channel_id=1, source_target_pairs={{0,96},{8,104},{16,112},{24,120},{32,0},{40,8},{48,16},{56,24},{64... | collective-permute-start | bytes 1572872 | tf_op jit(solution)/shard_map/ppermute | solution.py:45
  47.9 14.8 %collective-permute-start.1 = (bf16[1024,256]{1,0:T(8,128)(2,1)S(1)}, bf16[1024,256]{1,0:T(8,128)(2,1)S(1)}, u32[]{:S(2)}, u32[]{:S(2)}) collective-permute-start(bf16[1024,256]{1,0:T(8,128)(2,1)S(1)} %collective-permute-done.refs_3_), channel_id=1, source_target_pairs={{0,32},{8,40},{16,48},{24,56},{32,64},{40,72},{48,80},{56,88},{64,... | collective-permute-start | bytes 1572872 | tf_op jit(solution)/shard_map/ppermute | solution.py:45
  48.3 10.2 %collective-permute-start.6 = (bf16[512,256]{1,0:T(8,128)(2,1)}, bf16[512,256]{1,0:T(8,128)(2,1)S(1)}, u32[]{:S(2)}, u32[]{:S(2)}) collective-permute-start(bf16[512,256]{1,0:T(8,128)(2,1)} %collective-permute-done.5.refs_8_), channel_id=1, source_target_pairs={{0,16},{8,24},{16,0},{24,8},{32,48},{40,56},{48,32},{56,40},{64,80... | collective-permute-start | bytes 786440 | tf_op jit(solution)/shard_map/ppermute | solution.py:45
  50.4 12.3 %collective-permute-start.8 = (bf16[512,256]{1,0:T(8,128)(2,1)}, bf16[512,256]{1,0:T(8,128)(2,1)S(1)}, u32[]{:S(2)}, u32[]{:S(2)}) collective-permute-start(bf16[512,256]{1,0:T(8,128)(2,1)} %collective-permute-done.7.refs_9_), channel_id=1, source_target_pairs={{0,16},{8,24},{16,0},{24,8},{32,48},{40,56},{48,32},{56,40},{64,80... | collective-permute-start | bytes 786440 | tf_op jit(solution)/shard_map/ppermute | solution.py:45
  51.3 1.0 %copy-start.1 = (bf16[512,256]{1,0:T(8,128)(2,1)S(1)}, bf16[512,256]{1,0:T(8,128)(2,1)}, u32[]{:S(2)}) copy-start(bf16[512,256]{1,0:T(8,128)(2,1)} %copy-done) | copy-start | bytes 786436
  52.2 0.9 %copy-start.3 = (bf16[512,256]{1,0:T(8,128)(2,1)S(1)}, bf16[512,256]{1,0:T(8,128)(2,1)}, u32[]{:S(2)}) copy-start(bf16[512,256]{1,0:T(8,128)(2,1)} %copy-done.2) | copy-start | bytes 786436
  53.2 0.9 %copy-start.5 = (bf16[512,256]{1,0:T(8,128)(2,1)S(1)}, bf16[512,256]{1,0:T(8,128)(2,1)}, u32[]{:S(2)}) copy-start(bf16[512,256]{1,0:T(8,128)(2,1)} %copy-done.4) | copy-start | bytes 786436
  54.1 0.9 %copy-start.7 = (bf16[512,256]{1,0:T(8,128)(2,1)S(1)}, bf16[512,256]{1,0:T(8,128)(2,1)}, u32[]{:S(2)}) copy-start(bf16[512,256]{1,0:T(8,128)(2,1)} %copy-done.6) | copy-start | bytes 786436
  62.7 3.6 %collective-permute-start.21 = (bf16[512,256]{1,0:T(8,128)(2,1)S(1)}, bf16[512,256]{1,0:T(8,128)(2,1)S(1)}, u32[]{:S(2)}, u32[]{:S(2)}) collective-permute-start(bf16[512,256]{1,0:T(8,128)(2,1)S(1)} %collective-permute-done.6.refs_6_), channel_id=1, source_target_pairs={{0,8},{8,0},{16,24},{24,16},{32,40},{40,32},{48,56},{56,48},{64,72... | collective-permute-start | bytes 786440 | tf_op jit(solution)/shard_map/ppermute | solution.py:45
  64.3 2.0 %collective-permute-start.22 = (bf16[512,256]{1,0:T(8,128)(2,1)S(1)}, bf16[512,256]{1,0:T(8,128)(2,1)S(1)}, u32[]{:S(2)}, u32[]{:S(2)}) collective-permute-start(bf16[512,256]{1,0:T(8,128)(2,1)S(1)} %collective-permute-done.8.refs_7_), channel_id=1, source_target_pairs={{0,8},{8,0},{16,24},{24,16},{32,40},{40,32},{48,56},{56,48},{64,72... | collective-permute-start | bytes 786440 | tf_op jit(solution)/shard_map/ppermute | solution.py:45
  64.4 2.2 %collective-permute-start.19 = (bf16[1024,256]{1,0:T(8,128)(2,1)S(1)}, bf16[1024,256]{1,0:T(8,128)(2,1)S(1)}, u32[]{:S(2)}, u32[]{:S(2)}) collective-permute-start(bf16[1024,256]{1,0:T(8,128)(2,1)S(1)} %collective-permute-done.1.refs_4_), channel_id=1, source_target_pairs={{0,8},{8,0},{16,24},{24,16},{32,40},{40,32},{48,56},{56,48},{64,72... | collective-permute-start | bytes 1572872 | tf_op jit(solution)/shard_map/ppermute | solution.py:45
  64.9 2.5 %collective-permute-start.20 = (bf16[1024,256]{1,0:T(8,128)(2,1)S(1)}, bf16[1024,256]{1,0:T(8,128)(2,1)S(1)}, u32[]{:S(2)}, u32[]{:S(2)}) collective-permute-start(bf16[1024,256]{1,0:T(8,128)(2,1)S(1)} %collective-permute-done.2.refs_5_), channel_id=1, source_target_pairs={{0,8},{8,0},{16,24},{24,16},{32,40},{40,32},{48,56},{56,48},{64,72... | collective-permute-start | bytes 1572872 | tf_op jit(solution)/shard_map/ppermute | solution.py:45
  64.9 2.4 %copy-start.8 = (f32[8,16,128]{2,1,0:T(8,128)S(1)}, f32[8,16,128]{2,1,0:T(8,128)}, u32[]{:S(2)}) copy-start(f32[8,16,128]{2,1,0:T(8,128)} %get-tuple-element.63.refs_6_) | copy-start | bytes 196612
  64.9 2.4 %copy-start.9 = (f32[8,16,128]{2,1,0:T(8,128)S(1)}, f32[8,16,128]{2,1,0:T(8,128)}, u32[]{:S(2)}) copy-start(f32[8,16,128]{2,1,0:T(8,128)} %get-tuple-element.64.refs_7_) | copy-start | bytes 196612
  64.9 2.4 %copy-start.10 = (f32[8,16,128]{2,1,0:T(8,128)S(1)}, f32[8,16,128]{2,1,0:T(8,128)}, u32[]{:S(2)}) copy-start(f32[8,16,128]{2,1,0:T(8,128)} %get-tuple-element.65.refs_8_) | copy-start | bytes 196612
  65.0 2.4 %copy-start.11 = (bf16[8,16,128]{2,1,0:T(8,128)(2,1)S(1)}, bf16[8,16,128]{2,1,0:T(8,128)(2,1)}, u32[]{:S(2)}) copy-start(bf16[8,16,128]{2,1,0:T(8,128)(2,1)} %get-tuple-element.62.refs_5_) | copy-start | bytes 98308

commit v5 on v4

--- a/solution.py
+++ b/solution.py
@@ -20,7 +20,7 @@
 HALF = OWNED // 2
 COLS = 2 * HD
 VMEM_BYTES = 60 * 2**20
-PACK_STEPS = 2
+PACK_STEPS = 4
 CACHE_VMEM = 60 * 2**20
 PLACE_VMEM = 48 * 2**20
 PLACE_COST = pl.CostEstimate(flops=20000000000, bytes_accessed=1000, transcendentals=0)

time: 69.9 us -> 71.3 us (1.020)
  Pallas kernels: 18.6 us -> 19.9 us
    pallas_call x1, Pallas kernels: 2.02 us -> 3.33 us  [pack(): pl.pallas_call(pack_kernel, grid=(PACK_STEPS,), in_specs=[pl.BlockSpec((R...]
  transfers between devices with their start and end apart: 24 -> 24, of which waited for: 8 -> 8; matrix products, arithmetic and copies ran while one was open for 1% -> 1% of each run, Pallas kernels for 21% -> 20%
where the time goes in v5:
time: 71.3 us; the launch traced here: 70.9 us
  starting transfers between devices  30.1 us (42%)
  Pallas kernels  19.9 us (28%)
  waiting for transfers between devices  12.5 us (18%)
  local copies, waits for them, and re-layouts  6.77 us (9%)
  other arithmetic  0.86 us (1%)
  between operations  0.74 us (1%)
    ppermute x23, starting transfers between devices, send(): return lax.ppermute(value, 'rep', pairs)  24.2 us
    ppermute x23, waiting for transfers between devices, send(): return lax.ppermute(value, 'rep', pairs)  11.6 us
    pallas_call x1, Pallas kernels, attend_cache(): pl.pallas_call(lambda *refs: cache_kernel(first, count, *refs), grid=(cou...  9.66 us
    unnamed x24, local copies, waits for them, and re-layouts  6.61 us
    all_to_all x1, starting transfers between devices, local(): lax.all_to_all(pack(kv_master, hidden), 'tp', split_axis=0, concat_axis=0...  5.95 us
    pallas_call x2, Pallas kernels, place_early(): pl.pallas_call(lambda *refs: early_kernel(spots, bool(before), *refs), in...  4.74 us
    pallas_call x1, Pallas kernels, pack(): pl.pallas_call(pack_kernel, grid=(PACK_STEPS,), in_specs=[pl.BlockSpec((R...  3.33 us
    pallas_call x1, Pallas kernels, place_late(): pl.pallas_call(lambda *refs: late_kernel(spots, steps, rows, groups, *ref...  2.15 us
  transfers between devices with their start and end apart: 24, of which 8 were waited for; matrix products, arithmetic and copies ran while one was open for 1% of the time, Pallas kernels for 20%

profile of v5, /device:TPU:1, one launch (start us, length us, event | category | flops | bytes accessed | tf_op | source)
XLA Modules:
  0.0 70.9 jit_solution(1103187435469675558)
XLA Ops:
  0.6 3.3 %shard_map.85 = bf16[8,192,256]{2,1,0:T(8,128)(2,1)} custom-call(f32[128,2048]{1,0:T(8,128)} %kv_ref.1, bf16[2,4,2048]{2,1,0:T(4,128)(2,1)} %hid_ref.1), custom_call_target="tpu_custom_call" | custom-call | tf_op jit(solution)/shard_map/pallas_call | solution.py:81
  4.0 5.9 %all-to-all-start = ((bf16[8,192,256]{2,1,0:T(8,128)(2,1)}), bf16[8,192,256]{2,1,0:T(8,128)(2,1)S(1)}, u32[]{:S(2)}, u32[]{:S(2)}) async-start(bf16[8,192,256]{2,1,0:T(8,128)(2,1)} %shard_map.85), calls=%async_computation | async-start | bytes 1572864 | tf_op jit(solution)/shard_map/all_to_all | solution.py:336
  9.9 0.7 add_convert_fusion
  10.6 0.1 convert_element_type.12
  10.6 9.7 %shard_map.86 = (bf16[8,16,128]{2,1,0:T(8,128)(2,1)}, f32[8,16,128]{2,1,0:T(8,128)}, f32[8,16,128]{2,1,0:T(8,128)}, f32[8,16,128]{2,1,0:T(8,128)}) custom-call(s32[4]{0:T(128)} %refs_0_.1, bf16[2,4,2048]{2,1,0:T(4,128)(2,1)} %refs_1_.1, bf16[4,8192,128]{2,1,0:T(8,128)(2,1)} %refs_2_.1, bf16[4,8192,128]{2,1,0:T(8,128)(2,1)} %refs_3_.1), custom_call_target="tpu_custom_call" | custom-call | flops 536870912 | bytes 16777216 | tf_op jit(solution)/shard_map/pallas_call | solution.py:144
  20.3 1.0 %all-to-all-done.refs_1_ = bf16[8,192,256]{2,1,0:T(8,128)(2,1)S(1)} async-done(((bf16[8,192,256]{2,1,0:T(8,128)(2,1)}), bf16[8,192,256]{2,1,0:T(8,128)(2,1)S(1)}, u32[]{:S(2)}, u32[]{:S(2)}) %all-to-all-start) | async-done | bytes 786464 | tf_op jit(solution)/shard_map/all_to_all | solution.py:336
  21.4 1.7 %collective-permute-start.3 = (bf16[512,256]{1,0:T(8,128)(2,1)S(1)}, bf16[512,256]{1,0:T(8,128)(2,1)S(1)}, u32[]{:S(2)}, u32[]{:S(2)}) collective-permute-start(bf16[512,256]{1,0:T(8,128)(2,1)S(1)} %bitcast.9), channel_id=1, source_target_pairs={{0,32},{8,40},{16,48},{24,56},{32,64},{40,72},{48,80},{56,88},{64,... | collective-permute-start | bytes 786440 | tf_op jit(solution)/shard_map/ppermute | solution.py:45
  23.1 2.2 %collective-permute-start.4 = (bf16[512,256]{1,0:T(8,128)(2,1)S(1)}, bf16[512,256]{1,0:T(8,128)(2,1)S(1)}, u32[]{:S(2)}, u32[]{:S(2)}) collective-permute-start(bf16[512,256]{1,0:T(8,128)(2,1)S(1)} %bitcast.7), channel_id=1, source_target_pairs={{0,96},{8,104},{16,112},{24,120},{32,0},{40,8},{48,16},{56,24},{64... | collective-permute-start | bytes 786440 | tf_op jit(solution)/shard_map/ppermute | solution.py:45
  25.3 2.5 %collective-permute-start = (bf16[1024,256]{1,0:T(8,128)(2,1)S(1)}, bf16[1024,256]{1,0:T(8,128)(2,1)S(1)}, u32[]{:S(2)}, u32[]{:S(2)}) collective-permute-start(bf16[1024,256]{1,0:T(8,128)(2,1)S(1)} %bitcast.4), channel_id=1, source_target_pairs={{0,16},{8,24},{16,0},{24,8},{32,48},{40,56},{48,32},{56,40},{64,80... | collective-permute-start | bytes 1572872 | tf_op jit(solution)/shard_map/ppermute | solution.py:45
  27.7 0.1 fusion
  27.8 1.5 %collective-permute-start.9 = (bf16[512,256]{1,0:T(8,128)(2,1)S(1)}, bf16[512,256]{1,0:T(8,128)(2,1)S(1)}, u32[]{:S(2)}, u32[]{:S(2)}) collective-permute-start(bf16[512,256]{1,0:T(8,128)(2,1)S(1)} %bitcast.10), channel_id=1, source_target_pairs={{0,96},{8,104},{16,112},{24,120},{32,0},{40,8},{48,16},{56,24},{64... | collective-permute-start | bytes 786440 | tf_op jit(solution)/shard_map/ppermute | solution.py:45
  29.3 0.1 collective-permute-start.10
  29.4 0.1 pad_maximum_fusion
  29.4 0.8 %collective-permute-done.3.refs_4_ = bf16[512,256]{1,0:T(8,128)(2,1)S(1)} collective-permute-done((bf16[512,256]{1,0:T(8,128)(2,1)S(1)}, bf16[512,256]{1,0:T(8,128)(2,1)S(1)}, u32[]{:S(2)}, u32[]{:S(2)}) %collective-permute-start.3) | collective-permute-done | bytes 262176 | tf_op jit(solution)/shard_map/ppermute | solution.py:45
  30.3 0.4 collective-permute-start.5
  30.7 2.3 %collective-permute-start.7 = (bf16[512,256]{1,0:T(8,128)(2,1)S(1)}, bf16[512,256]{1,0:T(8,128)(2,1)}, u32[]{:S(2)}, u32[]{:S(2)}) collective-permute-start(bf16[512,256]{1,0:T(8,128)(2,1)S(1)} %collective-permute-done.4.refs_5_), channel_id=1, source_target_pairs={{0,96},{8,104},{16,112},{24,120},{32,0},{40,8},{48,16},{56,24},{64... | collective-permute-start | bytes 786440 | tf_op jit(solution)/shard_map/ppermute | solution.py:45
  32.9 2.6 %collective-permute-done.9.refs_6_ = bf16[512,256]{1,0:T(8,128)(2,1)S(1)} collective-permute-done((bf16[512,256]{1,0:T(8,128)(2,1)S(1)}, bf16[512,256]{1,0:T(8,128)(2,1)S(1)}, u32[]{:S(2)}, u32[]{:S(2)}) %collective-permute-start.9) | collective-permute-done | bytes 262176 | tf_op jit(solution)/shard_map/ppermute | solution.py:45
  35.5 0.5 collective-permute-done.10.refs_7_
  36.0 2.3 %collective-permute-done.refs_3_ = bf16[1024,256]{1,0:T(8,128)(2,1)S(1)} collective-permute-done((bf16[1024,256]{1,0:T(8,128)(2,1)S(1)}, bf16[1024,256]{1,0:T(8,128)(2,1)S(1)}, u32[]{:S(2)}, u32[]{:S(2)}) %collective-permute-start) | collective-permute-done | bytes 524320 | tf_op jit(solution)/shard_map/ppermute | solution.py:45
  38.4 3.8 %collective-permute-start.13 = (bf16[512,256]{1,0:T(8,128)(2,1)S(1)}, bf16[512,256]{1,0:T(8,128)(2,1)S(1)}, u32[]{:S(2)}, u32[]{:S(2)}) collective-permute-start(bf16[512,256]{1,0:T(8,128)(2,1)S(1)} %collective-permute-done.3.refs_4_), channel_id=1, source_target_pairs={{0,8},{8,0},{16,24},{24,16},{32,40},{40,32},{48,56},{56,48},{64,72... | collective-permute-start | bytes 786440 | tf_op jit(solution)/shard_map/ppermute | solution.py:45
  42.1 0.5 collective-permute-start.15
  42.7 0.7 copy-done
  43.4 1.6 %collective-permute-start.11 = (bf16[1024,256]{1,0:T(8,128)(2,1)S(1)}, bf16[1024,256]{1,0:T(8,128)(2,1)S(1)}, u32[]{:S(2)}, u32[]{:S(2)}) collective-permute-start(bf16[1024,256]{1,0:T(8,128)(2,1)S(1)} %bitcast.5), channel_id=1, source_target_pairs={{0,8},{8,0},{16,24},{24,16},{32,40},{40,32},{48,56},{56,48},{64,72... | collective-permute-start | bytes 1572872 | tf_op jit(solution)/shard_map/ppermute | solution.py:45
  45.0 0.7 copy-done.2
  45.7 0.5 collective-permute-start.16
  46.2 0.7 copy-done.4
  46.9 0.0 collective-permute-start.17
  46.9 0.7 copy-done.6
  47.6 0.5 collective-permute-start.18
  48.1 1.1 %collective-permute-start.2 = (bf16[1024,256]{1,0:T(8,128)(2,1)S(1)}, bf16[1024,256]{1,0:T(8,128)(2,1)S(1)}, u32[]{:S(2)}, u32[]{:S(2)}) collective-permute-start(bf16[1024,256]{1,0:T(8,128)(2,1)S(1)} %collective-permute-done.refs_3_), channel_id=1, source_target_pairs={{0,96},{8,104},{16,112},{24,120},{32,0},{40,8},{48,16},{56,24},{64... | collective-permute-start | bytes 1572872 | tf_op jit(solution)/shard_map/ppermute | solution.py:45
  49.2 0.4 collective-permute-start.1
  49.6 0.0 collective-permute-done.18.refs_17_
  49.6 2.1 %collective-permute-start.6 = (bf16[512,256]{1,0:T(8,128)(2,1)}, bf16[512,256]{1,0:T(8,128)(2,1)S(1)}, u32[]{:S(2)}, u32[]{:S(2)}) collective-permute-start(bf16[512,256]{1,0:T(8,128)(2,1)} %collective-permute-done.5.refs_8_), channel_id=1, source_target_pairs={{0,16},{8,24},{16,0},{24,8},{32,48},{40,56},{48,32},{56,40},{64,80... | collective-permute-start | bytes 786440 | tf_op jit(solution)/shard_map/ppermute | solution.py:45
  51.7 0.8 %collective-permute-start.8 = (bf16[512,256]{1,0:T(8,128)(2,1)}, bf16[512,256]{1,0:T(8,128)(2,1)S(1)}, u32[]{:S(2)}, u32[]{:S(2)}) collective-permute-start(bf16[512,256]{1,0:T(8,128)(2,1)} %collective-permute-done.7.refs_9_), channel_id=1, source_target_pairs={{0,16},{8,24},{16,0},{24,8},{32,48},{40,56},{48,32},{56,40},{64,80... | collective-permute-start | bytes 786440 | tf_op jit(solution)/shard_map/ppermute | solution.py:45
  52.6 0.9 %copy-done.1 = bf16[512,256]{1,0:T(8,128)(2,1)S(1)} copy-done((bf16[512,256]{1,0:T(8,128)(2,1)S(1)}, bf16[512,256]{1,0:T(8,128)(2,1)}, u32[]{:S(2)}) %copy-start.1) | copy-done | bytes 262168
  53.5 0.9 %copy-done.3 = bf16[512,256]{1,0:T(8,128)(2,1)S(1)} copy-done((bf16[512,256]{1,0:T(8,128)(2,1)S(1)}, bf16[512,256]{1,0:T(8,128)(2,1)}, u32[]{:S(2)}) %copy-start.3) | copy-done | bytes 262168
  54.5 0.9 %copy-done.5 = bf16[512,256]{1,0:T(8,128)(2,1)S(1)} copy-done((bf16[512,256]{1,0:T(8,128)(2,1)S(1)}, bf16[512,256]{1,0:T(8,128)(2,1)}, u32[]{:S(2)}) %copy-start.5) | copy-done | bytes 262168
  55.4 0.9 %copy-done.7 = bf16[512,256]{1,0:T(8,128)(2,1)S(1)} copy-done((bf16[512,256]{1,0:T(8,128)(2,1)S(1)}, bf16[512,256]{1,0:T(8,128)(2,1)}, u32[]{:S(2)}) %copy-start.7) | copy-done | bytes 262168
  56.4 3.4 %shard_map.87 = (bf16[16384,256]{1,0:T(8,128)(2,1)}, f32[8,256]{1,0:T(8,128)S(1)}) custom-call(s32[1]{0:T(128)} %bitcast.refs_0_, bf16[8,192,256]{2,1,0:T(8,128)(2,1)S(1)} %all-to-all-done.refs_1_, bf16[1024,256]{1,0:T(8,128)(2,1)S(1)} %bitcast.6, bf16[1024,256]{1,0:T(8,128)(2,1)S(1)} %collective-permute-done.refs_3_, ...), custom_call_target="tpu_custom_call" | custom-call | flops 20000000000 | bytes 1000 | tf_op jit(solution)/shard_map/pallas_call | solution.py:288
  59.8 4.2 %collective-permute-done.8.refs_7_ = bf16[512,256]{1,0:T(8,128)(2,1)S(1)} collective-permute-done((bf16[512,256]{1,0:T(8,128)(2,1)}, bf16[512,256]{1,0:T(8,128)(2,1)S(1)}, u32[]{:S(2)}, u32[]{:S(2)}) %collective-permute-start.8) | collective-permute-done | bytes 262176 | tf_op jit(solution)/shard_map/ppermute | solution.py:45
  64.0 1.7 %collective-permute-start.21 = (bf16[512,256]{1,0:T(8,128)(2,1)S(1)}, bf16[512,256]{1,0:T(8,128)(2,1)S(1)}, u32[]{:S(2)}, u32[]{:S(2)}) collective-permute-start(bf16[512,256]{1,0:T(8,128)(2,1)S(1)} %collective-permute-done.6.refs_6_), channel_id=1, source_target_pairs={{0,8},{8,0},{16,24},{24,16},{32,40},{40,32},{48,56},{56,48},{64,72... | collective-permute-start | bytes 786440 | tf_op jit(solution)/shard_map/ppermute | solution.py:45
  65.7 0.1 collective-permute-start.22
  65.7 0.4 collective-permute-start.19
  66.2 0.1 collective-permute-start.20
  66.3 1.4 %shard_map.88 = (bf16[16384,256]{1,0:T(8,128)(2,1)}, f32[8,256]{1,0:T(8,128)S(1)}) custom-call(s32[1]{0:T(128)} %bitcast.refs_0_, bf16[8,192,256]{2,1,0:T(8,128)(2,1)S(1)} %all-to-all-done.refs_1_, f32[8,256]{1,0:T(8,128)S(1)} %get-tuple-element.53.refs_2_, bf16[16384,256]{1,0:T(8,128)(2,1)} %get-tuple-element.54.refs_3_, ...), custom_call_target="tpu_custom_call", output_to_operand_aliasing={{0}: (3, {})} | custom-call | flops 20000000000 | bytes 1000 | tf_op jit(solution)/shard_map/pallas_call | solution.py:288
  67.7 0.3 collective-permute-done.19.refs_10_
  67.9 0.7 %collective-permute-done.20.refs_11_ = bf16[1024,256]{1,0:T(8,128)(2,1)S(1)} collective-permute-done((bf16[1024,256]{1,0:T(8,128)(2,1)S(1)}, bf16[1024,256]{1,0:T(8,128)(2,1)S(1)}, u32[]{:S(2)}, u32[]{:S(2)}) %collective-permute-start.20) | collective-permute-done | bytes 524320 | tf_op jit(solution)/shard_map/ppermute | solution.py:45
  68.7 2.2 %shard_map.89 = (bf16[16384,256]{1,0:T(8,128)(2,1)}, bf16[2,4,256]{2,1,0:T(4,128)(2,1)}, bf16[2,4,2048]{2,1,0:T(4,128)(2,1)}) custom-call(s32[1]{0:T(128)} %bitcast.refs_0_, bf16[8,192,256]{2,1,0:T(8,128)(2,1)S(1)} %all-to-all-done.refs_1_, f32[8,256]{1,0:T(8,128)S(1)} %get-tuple-element.59.refs_2_, ...), custom_call_target="tpu_custom_call", output_to_operand_aliasing={{0}: (9, {})} | custom-call | flops 20000000000 | bytes 1000 | tf_op jit(solution)/shard_map/pallas_call | solution.py:306
  (36 shorter events, 0.2 us)
Async XLA Ops:
  4.0 17.3 %all-to-all-start = ((bf16[8,192,256]{2,1,0:T(8,128)(2,1)}), bf16[8,192,256]{2,1,0:T(8,128)(2,1)S(1)}, u32[]{:S(2)}, u32[]{:S(2)}) async-start(bf16[8,192,256]{2,1,0:T(8,128)(2,1)} %shard_map.85), calls=%async_computation | async-start | bytes 1572864 | tf_op jit(solution)/shard_map/all_to_all | solution.py:336
  21.4 8.9 %collective-permute-start.3 = (bf16[512,256]{1,0:T(8,128)(2,1)S(1)}, bf16[512,256]{1,0:T(8,128)(2,1)S(1)}, u32[]{:S(2)}, u32[]{:S(2)}) collective-permute-start(bf16[512,256]{1,0:T(8,128)(2,1)S(1)} %bitcast.9), channel_id=1, source_target_pairs={{0,32},{8,40},{16,48},{24,56},{32,64},{40,72},{48,80},{56,88},{64,... | collective-permute-start | bytes 786440 | tf_op jit(solution)/shard_map/ppermute | solution.py:45
  23.1 7.2 %collective-permute-start.4 = (bf16[512,256]{1,0:T(8,128)(2,1)S(1)}, bf16[512,256]{1,0:T(8,128)(2,1)S(1)}, u32[]{:S(2)}, u32[]{:S(2)}) collective-permute-start(bf16[512,256]{1,0:T(8,128)(2,1)S(1)} %bitcast.7), channel_id=1, source_target_pairs={{0,96},{8,104},{16,112},{24,120},{32,0},{40,8},{48,16},{56,24},{64... | collective-permute-start | bytes 786440 | tf_op jit(solution)/shard_map/ppermute | solution.py:45
  25.3 13.1 %collective-permute-start = (bf16[1024,256]{1,0:T(8,128)(2,1)S(1)}, bf16[1024,256]{1,0:T(8,128)(2,1)S(1)}, u32[]{:S(2)}, u32[]{:S(2)}) collective-permute-start(bf16[1024,256]{1,0:T(8,128)(2,1)S(1)} %bitcast.4), channel_id=1, source_target_pairs={{0,16},{8,24},{16,0},{24,8},{32,48},{40,56},{48,32},{56,40},{64,80... | collective-permute-start | bytes 1572872 | tf_op jit(solution)/shard_map/ppermute | solution.py:45
  27.8 7.7 %collective-permute-start.9 = (bf16[512,256]{1,0:T(8,128)(2,1)S(1)}, bf16[512,256]{1,0:T(8,128)(2,1)S(1)}, u32[]{:S(2)}, u32[]{:S(2)}) collective-permute-start(bf16[512,256]{1,0:T(8,128)(2,1)S(1)} %bitcast.10), channel_id=1, source_target_pairs={{0,96},{8,104},{16,112},{24,120},{32,0},{40,8},{48,16},{56,24},{64... | collective-permute-start | bytes 786440 | tf_op jit(solution)/shard_map/ppermute | solution.py:45
  29.3 6.7 %collective-permute-start.10 = (bf16[512,256]{1,0:T(8,128)(2,1)S(1)}, bf16[512,256]{1,0:T(8,128)(2,1)}, u32[]{:S(2)}, u32[]{:S(2)}) collective-permute-start(bf16[512,256]{1,0:T(8,128)(2,1)S(1)} %bitcast.8), channel_id=1, source_target_pairs={{0,32},{8,40},{16,48},{24,56},{32,64},{40,72},{48,80},{56,88},{64,... | collective-permute-start | bytes 786440 | tf_op jit(solution)/shard_map/ppermute | solution.py:45
  30.3 13.1 %collective-permute-start.5 = (bf16[512,256]{1,0:T(8,128)(2,1)S(1)}, bf16[512,256]{1,0:T(8,128)(2,1)}, u32[]{:S(2)}, u32[]{:S(2)}) collective-permute-start(bf16[512,256]{1,0:T(8,128)(2,1)S(1)} %collective-permute-done.3.refs_4_), channel_id=1, source_target_pairs={{0,32},{8,40},{16,48},{24,56},{32,64},{40,72},{48,80},{56,88},{64,... | collective-permute-start | bytes 786440 | tf_op jit(solution)/shard_map/ppermute | solution.py:45
  30.7 14.3 %collective-permute-start.7 = (bf16[512,256]{1,0:T(8,128)(2,1)S(1)}, bf16[512,256]{1,0:T(8,128)(2,1)}, u32[]{:S(2)}, u32[]{:S(2)}) collective-permute-start(bf16[512,256]{1,0:T(8,128)(2,1)S(1)} %collective-permute-done.4.refs_5_), channel_id=1, source_target_pairs={{0,96},{8,104},{16,112},{24,120},{32,0},{40,8},{48,16},{56,24},{64... | collective-permute-start | bytes 786440 | tf_op jit(solution)/shard_map/ppermute | solution.py:45
  38.4 6.6 %collective-permute-start.13 = (bf16[512,256]{1,0:T(8,128)(2,1)S(1)}, bf16[512,256]{1,0:T(8,128)(2,1)S(1)}, u32[]{:S(2)}, u32[]{:S(2)}) collective-permute-start(bf16[512,256]{1,0:T(8,128)(2,1)S(1)} %collective-permute-done.3.refs_4_), channel_id=1, source_target_pairs={{0,8},{8,0},{16,24},{24,16},{32,40},{40,32},{48,56},{56,48},{64,72... | collective-permute-start | bytes 786440 | tf_op jit(solution)/shard_map/ppermute | solution.py:45
  42.1 4.0 %collective-permute-start.14 = (bf16[512,256]{1,0:T(8,128)(2,1)S(1)}, bf16[512,256]{1,0:T(8,128)(2,1)S(1)}, u32[]{:S(2)}, u32[]{:S(2)}) collective-permute-start(bf16[512,256]{1,0:T(8,128)(2,1)S(1)} %collective-permute-done.4.refs_5_), channel_id=1, source_target_pairs={{0,8},{8,0},{16,24},{24,16},{32,40},{40,32},{48,56},{56,48},{64,72... | collective-permute-start | bytes 786440 | tf_op jit(solution)/shard_map/ppermute | solution.py:45
  42.1 4.7 %collective-permute-start.15 = (bf16[512,256]{1,0:T(8,128)(2,1)S(1)}, bf16[512,256]{1,0:T(8,128)(2,1)S(1)}, u32[]{:S(2)}, u32[]{:S(2)}) collective-permute-start(bf16[512,256]{1,0:T(8,128)(2,1)S(1)} %collective-permute-done.9.refs_6_), channel_id=1, source_target_pairs={{0,8},{8,0},{16,24},{24,16},{32,40},{40,32},{48,56},{56,48},{64,72... | collective-permute-start | bytes 786440 | tf_op jit(solution)/shard_map/ppermute | solution.py:45
  42.7 0.7 copy-start
  43.4 8.4 %collective-permute-start.11 = (bf16[1024,256]{1,0:T(8,128)(2,1)S(1)}, bf16[1024,256]{1,0:T(8,128)(2,1)S(1)}, u32[]{:S(2)}, u32[]{:S(2)}) collective-permute-start(bf16[1024,256]{1,0:T(8,128)(2,1)S(1)} %bitcast.5), channel_id=1, source_target_pairs={{0,8},{8,0},{16,24},{24,16},{32,40},{40,32},{48,56},{56,48},{64,72... | collective-permute-start | bytes 1572872 | tf_op jit(solution)/shard_map/ppermute | solution.py:45
  45.0 7.6 %collective-permute-start.12 = (bf16[1024,256]{1,0:T(8,128)(2,1)S(1)}, bf16[1024,256]{1,0:T(8,128)(2,1)S(1)}, u32[]{:S(2)}, u32[]{:S(2)}) collective-permute-start(bf16[1024,256]{1,0:T(8,128)(2,1)S(1)} %collective-permute-done.refs_3_), channel_id=1, source_target_pairs={{0,8},{8,0},{16,24},{24,16},{32,40},{40,32},{48,56},{56,48},{64,72... | collective-permute-start | bytes 1572872 | tf_op jit(solution)/shard_map/ppermute | solution.py:45
  45.0 0.7 copy-start.2
  45.7 2.4 %collective-permute-start.16 = (bf16[512,256]{1,0:T(8,128)(2,1)}, bf16[512,256]{1,0:T(8,128)(2,1)}, u32[]{:S(2)}, u32[]{:S(2)}) collective-permute-start(bf16[512,256]{1,0:T(8,128)(2,1)} %collective-permute-done.10.refs_7_), channel_id=1, source_target_pairs={{0,8},{8,0},{16,24},{24,16},{32,40},{40,32},{48,56},{56,48},{64,72... | collective-permute-start | bytes 786440 | tf_op jit(solution)/shard_map/ppermute | solution.py:45
  46.2 0.7 copy-start.4
  46.9 2.3 %collective-permute-start.17 = (bf16[512,256]{1,0:T(8,128)(2,1)}, bf16[512,256]{1,0:T(8,128)(2,1)}, u32[]{:S(2)}, u32[]{:S(2)}) collective-permute-start(bf16[512,256]{1,0:T(8,128)(2,1)} %collective-permute-done.5.refs_8_), channel_id=1, source_target_pairs={{0,8},{8,0},{16,24},{24,16},{32,40},{40,32},{48,56},{56,48},{64,72... | collective-permute-start | bytes 786440 | tf_op jit(solution)/shard_map/ppermute | solution.py:45
  46.9 0.7 copy-start.6
  47.6 2.0 %collective-permute-start.18 = (bf16[512,256]{1,0:T(8,128)(2,1)}, bf16[512,256]{1,0:T(8,128)(2,1)}, u32[]{:S(2)}, u32[]{:S(2)}) collective-permute-start(bf16[512,256]{1,0:T(8,128)(2,1)} %collective-permute-done.7.refs_9_), channel_id=1, source_target_pairs={{0,8},{8,0},{16,24},{24,16},{32,40},{40,32},{48,56},{56,48},{64,72... | collective-permute-start | bytes 786440 | tf_op jit(solution)/shard_map/ppermute | solution.py:45
  48.1 15.9 %collective-permute-start.2 = (bf16[1024,256]{1,0:T(8,128)(2,1)S(1)}, bf16[1024,256]{1,0:T(8,128)(2,1)S(1)}, u32[]{:S(2)}, u32[]{:S(2)}) collective-permute-start(bf16[1024,256]{1,0:T(8,128)(2,1)S(1)} %collective-permute-done.refs_3_), channel_id=1, source_target_pairs={{0,96},{8,104},{16,112},{24,120},{32,0},{40,8},{48,16},{56,24},{64... | collective-permute-start | bytes 1572872 | tf_op jit(solution)/shard_map/ppermute | solution.py:45
  49.2 14.8 %collective-permute-start.1 = (bf16[1024,256]{1,0:T(8,128)(2,1)S(1)}, bf16[1024,256]{1,0:T(8,128)(2,1)S(1)}, u32[]{:S(2)}, u32[]{:S(2)}) collective-permute-start(bf16[1024,256]{1,0:T(8,128)(2,1)S(1)} %collective-permute-done.refs_3_), channel_id=1, source_target_pairs={{0,32},{8,40},{16,48},{24,56},{32,64},{40,72},{48,80},{56,88},{64,... | collective-permute-start | bytes 1572872 | tf_op jit(solution)/shard_map/ppermute | solution.py:45
  49.6 10.2 %collective-permute-start.6 = (bf16[512,256]{1,0:T(8,128)(2,1)}, bf16[512,256]{1,0:T(8,128)(2,1)S(1)}, u32[]{:S(2)}, u32[]{:S(2)}) collective-permute-start(bf16[512,256]{1,0:T(8,128)(2,1)} %collective-permute-done.5.refs_8_), channel_id=1, source_target_pairs={{0,16},{8,24},{16,0},{24,8},{32,48},{40,56},{48,32},{56,40},{64,80... | collective-permute-start | bytes 786440 | tf_op jit(solution)/shard_map/ppermute | solution.py:45
  51.7 12.3 %collective-permute-start.8 = (bf16[512,256]{1,0:T(8,128)(2,1)}, bf16[512,256]{1,0:T(8,128)(2,1)S(1)}, u32[]{:S(2)}, u32[]{:S(2)}) collective-permute-start(bf16[512,256]{1,0:T(8,128)(2,1)} %collective-permute-done.7.refs_9_), channel_id=1, source_target_pairs={{0,16},{8,24},{16,0},{24,8},{32,48},{40,56},{48,32},{56,40},{64,80... | collective-permute-start | bytes 786440 | tf_op jit(solution)/shard_map/ppermute | solution.py:45
  52.6 1.0 %copy-start.1 = (bf16[512,256]{1,0:T(8,128)(2,1)S(1)}, bf16[512,256]{1,0:T(8,128)(2,1)}, u32[]{:S(2)}) copy-start(bf16[512,256]{1,0:T(8,128)(2,1)} %copy-done) | copy-start | bytes 786436
  53.5 0.9 %copy-start.3 = (bf16[512,256]{1,0:T(8,128)(2,1)S(1)}, bf16[512,256]{1,0:T(8,128)(2,1)}, u32[]{:S(2)}) copy-start(bf16[512,256]{1,0:T(8,128)(2,1)} %copy-done.2) | copy-start | bytes 786436
  54.5 0.9 %copy-start.5 = (bf16[512,256]{1,0:T(8,128)(2,1)S(1)}, bf16[512,256]{1,0:T(8,128)(2,1)}, u32[]{:S(2)}) copy-start(bf16[512,256]{1,0:T(8,128)(2,1)} %copy-done.4) | copy-start | bytes 786436
  55.4 0.9 %copy-start.7 = (bf16[512,256]{1,0:T(8,128)(2,1)S(1)}, bf16[512,256]{1,0:T(8,128)(2,1)}, u32[]{:S(2)}) copy-start(bf16[512,256]{1,0:T(8,128)(2,1)} %copy-done.6) | copy-start | bytes 786436
  64.0 3.6 %collective-permute-start.21 = (bf16[512,256]{1,0:T(8,128)(2,1)S(1)}, bf16[512,256]{1,0:T(8,128)(2,1)S(1)}, u32[]{:S(2)}, u32[]{:S(2)}) collective-permute-start(bf16[512,256]{1,0:T(8,128)(2,1)S(1)} %collective-permute-done.6.refs_6_), channel_id=1, source_target_pairs={{0,8},{8,0},{16,24},{24,16},{32,40},{40,32},{48,56},{56,48},{64,72... | collective-permute-start | bytes 786440 | tf_op jit(solution)/shard_map/ppermute | solution.py:45
  65.7 2.0 %collective-permute-start.22 = (bf16[512,256]{1,0:T(8,128)(2,1)S(1)}, bf16[512,256]{1,0:T(8,128)(2,1)S(1)}, u32[]{:S(2)}, u32[]{:S(2)}) collective-permute-start(bf16[512,256]{1,0:T(8,128)(2,1)S(1)} %collective-permute-done.8.refs_7_), channel_id=1, source_target_pairs={{0,8},{8,0},{16,24},{24,16},{32,40},{40,32},{48,56},{56,48},{64,72... | collective-permute-start | bytes 786440 | tf_op jit(solution)/shard_map/ppermute | solution.py:45
  65.7 2.2 %collective-permute-start.19 = (bf16[1024,256]{1,0:T(8,128)(2,1)S(1)}, bf16[1024,256]{1,0:T(8,128)(2,1)S(1)}, u32[]{:S(2)}, u32[]{:S(2)}) collective-permute-start(bf16[1024,256]{1,0:T(8,128)(2,1)S(1)} %collective-permute-done.1.refs_4_), channel_id=1, source_target_pairs={{0,8},{8,0},{16,24},{24,16},{32,40},{40,32},{48,56},{56,48},{64,72... | collective-permute-start | bytes 1572872 | tf_op jit(solution)/shard_map/ppermute | solution.py:45
  66.2 2.5 %collective-permute-start.20 = (bf16[1024,256]{1,0:T(8,128)(2,1)S(1)}, bf16[1024,256]{1,0:T(8,128)(2,1)S(1)}, u32[]{:S(2)}, u32[]{:S(2)}) collective-permute-start(bf16[1024,256]{1,0:T(8,128)(2,1)S(1)} %collective-permute-done.2.refs_5_), channel_id=1, source_target_pairs={{0,8},{8,0},{16,24},{24,16},{32,40},{40,32},{48,56},{56,48},{64,72... | collective-permute-start | bytes 1572872 | tf_op jit(solution)/shard_map/ppermute | solution.py:45
  66.3 2.4 %copy-start.8 = (f32[8,16,128]{2,1,0:T(8,128)S(1)}, f32[8,16,128]{2,1,0:T(8,128)}, u32[]{:S(2)}) copy-start(f32[8,16,128]{2,1,0:T(8,128)} %get-tuple-element.63.refs_6_) | copy-start | bytes 196612
  66.3 2.4 %copy-start.9 = (f32[8,16,128]{2,1,0:T(8,128)S(1)}, f32[8,16,128]{2,1,0:T(8,128)}, u32[]{:S(2)}) copy-start(f32[8,16,128]{2,1,0:T(8,128)} %get-tuple-element.64.refs_7_) | copy-start | bytes 196612
  66.3 2.4 %copy-start.10 = (f32[8,16,128]{2,1,0:T(8,128)S(1)}, f32[8,16,128]{2,1,0:T(8,128)}, u32[]{:S(2)}) copy-start(f32[8,16,128]{2,1,0:T(8,128)} %get-tuple-element.65.refs_8_) | copy-start | bytes 196612
  66.3 2.4 %copy-start.11 = (bf16[8,16,128]{2,1,0:T(8,128)(2,1)S(1)}, bf16[8,16,128]{2,1,0:T(8,128)(2,1)}, u32[]{:S(2)}) copy-start(bf16[8,16,128]{2,1,0:T(8,128)(2,1)} %get-tuple-element.62.refs_5_) | copy-start | bytes 98308
